TPU v7x, 512 devices: a whole 4x4x16 slice. The times are simulated.
512 devices in a mesh: rows: 64 (over z_lo, x, y), aggs: 4 (over z_hi), vecs: 2 (over core).
Axes of the slice: x: 4, y: 4, z: 16 (z_hi: 4, z_lo: 4; z = z_hi * 4 + z_lo), core: 2. Of those that a mesh axis runs over, the one named last changes fastest.
Arguments:
- couplings: bfloat16 [1024, 8, 192, 192], P('rows', 'aggs'), may hold values from -0.19921875 to 0.19921875
- diag_blocks: bfloat16 [1024, 192, 192], P('rows'), may hold values from -0.201 to 3, as said below
- coupling_cols: int32 [1024, 8], P('rows', 'aggs'), may hold values from 0 to 1023, as said below
- aggregate: int32 [1024], P('rows'), may hold values from 0 to 511, as said below
- pattern: int32 [1024, 3], P('rows'), may hold values from 0 to 511, as said below
- tests: float32 [1024, 32, 192], P('rows', 'vecs'), may hold values from -6 to 6
Outputs:
- prolongator: bfloat16 [1024, 4, 32, 192], P('rows', 'aggs', 'vecs')
- coarse: float32 [512, 24, 32, 32], P('rows', 'aggs', 'vecs')
Inputs may be any that keep to these rules, and one draw needn't show every extreme that they name: `diag_blocks`: Off-diagonal entries of each block lie within about 0.2 of zero; the diagonal entries lie between 1 and 3. `coupling_cols`: the columns of a block row are distinct, none equals the row, and each lies in the row's own slab of 16 block rows or in the slab just before or after it. A block row of slab s belongs to one of the aggregates s * 8 to s * 8 + 7, and every aggregate has one block row or more. `pattern`: the entries of a row are distinct aggregates of the row's own slab, none equal to the row's aggregate.
All inputs are finite; a program needn't handle non-finite values.
Results may differ from a plain program's by a relative error of at most 0.009.
Values may be sent and summed in bfloat16 or wider, within the bound.
No kernel may reach another device: no remote copies, remote signals or barrier semaphores. Data moves between devices by JAX's collectives and lax.ppermute only.
A program may use at most 64 MiB of HBM per device.

v0:
```python
import jax
import jax.numpy as jnp
from jax import lax
from jax.sharding import PartitionSpec as P

VECTORS = 32
SWEEPS = 3
SLAB_AGGS = 8


DAMPING = 2.0 / 3.0
HIGHEST_PRECISION = lax.Precision.HIGHEST


def with_halo(x, sides, width):
    for axis, dim in sides:
        size, length = (lax.axis_size(axis), x.shape[dim])
        up = [(i, (i + 1) % size) for i in range(size - 1)]
        down = [(j, i) for i, j in up]
        last = lax.slice_in_dim(x, length - width, length, axis=dim)
        initial = lax.slice_in_dim(x, 0, width, axis=dim)
        before = lax.ppermute(last, axis, up)
        after = lax.ppermute(initial, axis, down)
        x = jnp.concatenate([before, x, after], axis=dim)
    return x


def on_device(couplings, diag_blocks, coupling_cols, aggregate, pattern, tests):
    slab_rows = tests.shape[0]
    vector_part = tests.shape[1]
    block_width = tests.shape[2]
    slab_index = lax.axis_index("rows")
    slot_index = lax.axis_index("aggs")
    slot_count = lax.axis_size("aggs")
    share_width = block_width // slot_count
    share_start = slot_index * share_width
    first_row = slab_index * slab_rows
    pivots = jnp.diagonal(diag_blocks, axis1=1, axis2=2).astype(jnp.float32)
    diag_rows = lax.dynamic_slice_in_dim(diag_blocks, share_start, share_width, 1)
    local_cols = coupling_cols - first_row + slab_rows
    current = tests
    rounded = tests.astype(jnp.bfloat16)
    for sweep_index in range(SWEEPS):
        rounded = current.astype(jnp.bfloat16)
        extended = with_halo(rounded, (("rows", 0),), slab_rows)
        partial_sum = jnp.einsum(
            "ikab,ikvb->iva", couplings, extended[local_cols], preferred_element_type=jnp.float32
        )
        center_part = jnp.einsum(
            "isb,ivb->ivs", diag_rows, rounded, preferred_element_type=jnp.float32
        )
        corner = lax.dynamic_slice_in_dim(partial_sum, share_start, share_width, 2)
        partial_sum = lax.dynamic_update_slice_in_dim(
            partial_sum, corner + center_part, share_start, 2
        )
        whole_sum = lax.psum(partial_sum, "aggs")
        current = current - DAMPING * whole_sum / pivots[:, None, :]
    every_vector = lax.all_gather(current, "vecs", axis=1, tiled=True)
    grams_rows = jnp.einsum("ivb,iwb->ivw", every_vector, every_vector, precision=HIGHEST_PRECISION)
    local_aggs = aggregate - slab_index * SLAB_AGGS
    members = (local_aggs[:, None] == jnp.arange(SLAB_AGGS, dtype=jnp.int32)[None, :]).astype(
        jnp.float32
    )
    totals = (
        jnp.einsum("ig,ivw->gvw", members, grams_rows, precision=HIGHEST_PRECISION) / block_width
    )
    factor_low = jnp.linalg.cholesky(totals)
    identity = jnp.broadcast_to(jnp.eye(VECTORS, dtype=jnp.float32), totals.shape)
    inverse = lax.linalg.triangular_solve(factor_low, identity, left_side=True, lower=True)
    row_inverse = jnp.einsum("ig,gcv->icv", members, inverse, precision=HIGHEST_PRECISION)
    row_inverse = lax.dynamic_slice_in_dim(
        row_inverse, lax.axis_index("vecs") * vector_part, vector_part, 1
    )
    tentative = jnp.einsum("icv,ivb->icb", row_inverse, every_vector, precision=HIGHEST_PRECISION)
    tentative_b = tentative.astype(jnp.bfloat16)
    own_index = coupling_cols - first_row
    inside_hits = (
        own_index[:, :, None] == jnp.arange(slab_rows, dtype=jnp.int32)[None, None, :]
    ).astype(jnp.int32)
    column_aggs = jnp.sum(inside_hits * (aggregate + 1)[None, None, :], axis=2) - 1
    safe_index = jnp.clip(own_index, 0, slab_rows - 1)
    slot_aggs = jnp.concatenate([aggregate[:, None], pattern], axis=1)
    matches = (column_aggs[:, :, None] == slot_aggs[:, None, :]).astype(jnp.float32)
    moved_rows = jnp.einsum(
        "ikab,ikcb->ikca", couplings, tentative_b[safe_index], preferred_element_type=jnp.float32
    )
    partials = jnp.einsum("ikp,ikca->ipca", matches, moved_rows, precision=HIGHEST_PRECISION)
    center_fit = jnp.einsum(
        "isb,icb->ics", diag_rows, tentative_b, preferred_element_type=jnp.float32
    )
    corner_fit = lax.dynamic_slice(
        partials, (0, 0, 0, share_start), (slab_rows, 1, vector_part, share_width)
    )
    partials = lax.dynamic_update_slice(
        partials, corner_fit + center_fit[:, None], (0, 0, 0, share_start)
    )
    owned_slots = lax.psum_scatter(partials, "aggs", scatter_dimension=1, tiled=True)
    slot_here = owned_slots.shape[1]
    slot_ids = slot_index * slot_here + jnp.arange(slot_here, dtype=jnp.int32)
    leading = (slot_ids == 0).astype(jnp.float32)[None, :, None, None]
    prolong_part = (
        leading * tentative[:, None] - DAMPING * owned_slots / pivots[:, None, None, :]
    ).astype(jnp.bfloat16)
    own_slots = lax.all_gather(prolong_part, "aggs", axis=1, tiled=True)
    own_every = lax.all_gather(own_slots, "vecs", axis=2, tiled=True)
    extended_full = with_halo(own_every, (("rows", 0),), slab_rows)
    pattern_ext = with_halo(slot_aggs, (("rows", 0),), slab_rows)
    center_every = extended_full[slab_rows : 2 * slab_rows]
    reached = jnp.einsum(
        "ikxy,ikqey->ikqex",
        couplings,
        extended_full[local_cols],
        preferred_element_type=jnp.float32,
    ).astype(jnp.bfloat16)
    center_reach = jnp.einsum(
        "isy,iqey->iqes", diag_rows, center_every, preferred_element_type=jnp.float32
    ).astype(jnp.bfloat16)
    crossed = jnp.einsum(
        "ipdx,ikqex->ikpqde", own_slots, reached, preferred_element_type=jnp.float32
    )
    own_share = lax.dynamic_slice_in_dim(own_slots, share_start, share_width, 3)
    center_cross = jnp.einsum(
        "ipdx,iqex->ipqde", own_share, center_reach, preferred_element_type=jnp.float32
    )
    span_width = 3 * SLAB_AGGS
    column_base = (slab_index - 1) * SLAB_AGGS
    row_hot = (
        (slot_aggs - slab_index * SLAB_AGGS)[:, :, None] == jnp.arange(SLAB_AGGS, dtype=jnp.int32)
    ).astype(jnp.float32)
    col_hot = (
        (pattern_ext[local_cols] - column_base)[..., None]
        == jnp.arange(span_width, dtype=jnp.int32)
    ).astype(jnp.float32)
    center_hot = (
        (slot_aggs - column_base)[..., None] == jnp.arange(span_width, dtype=jnp.int32)
    ).astype(jnp.float32)
    coarse_part = jnp.einsum(
        "ipg,ikqn,ikpqde->gnde", row_hot, col_hot, crossed, precision=HIGHEST_PRECISION
    )
    coarse_part = coarse_part + jnp.einsum(
        "ipg,iqn,ipqde->gnde", row_hot, center_hot, center_cross, precision=HIGHEST_PRECISION
    )
    coarse_part = coarse_part / block_width
    coarse_owned = lax.psum_scatter(coarse_part, "aggs", scatter_dimension=1, tiled=True)
    return (prolong_part, coarse_owned)


def solution(mesh):
    return jax.shard_map(
        on_device,
        mesh=mesh,
        in_specs=(
            P("rows", "aggs", None, None),
            P("rows", None, None),
            P("rows", "aggs"),
            P("rows"),
            P("rows", None),
            P("rows", "vecs", None),
        ),
        out_specs=(P("rows", "aggs", "vecs", None), P("rows", "aggs", "vecs", None)),
        check_vma=False,
    )
```

profile of v0, /device:TPU:1, one launch (start us, length us, event | category | flops | bytes accessed | tf_op | source)
XLA Modules:
  0.0 684.2 jit_solution(1546142800844624656)
XLA Ops:
  7.2 1.1 convert_element_type.46
  8.3 1.3 collective-permute-start.1
  9.6 5.3 collective-permute-start
  15.0 8.3 %copy.72 = bf16[16,192,192]{0,2,1:T(8,128)(2,1)} copy(bf16[16,192,192]{2,1,0:T(8,128)(2,1)} %param.7) | data formatting | bytes 2359296 | tf_op args[1]
  23.3 5.3 gather_fusion.1
  30.1 1.8 pad_maximum_fusion.1
  31.9 2.3 gather_fusion
  34.2 1.8 convolution_bitcast_fusion.5
  36.8 1.9 fusion.22
  38.7 1.8 dynamic_update_slice.12
  41.0 1.6 copy.73
  42.8 77.7 %all-reduce.6.cloned.1.call-done = f32[16,16,192]{2,1,0:T(8,128)} async-done(((f32[16,16,192]{2,1,0:T(8,128)}), f32[16,16,192]{2,1,0:T(8,128)}) %all-reduce.6.cloned.1.call-update) | async-done | bytes 196624 | tf_op jit(solution)/shard_map/psum | solution.py:56
  120.5 1.0 fusion.75
  121.5 1.3 collective-permute-start.3
  122.8 4.7 collective-permute-start.2
  129.5 1.8 pad_maximum_fusion.2
  131.3 2.3 gather_fusion.2
  133.5 1.8 convolution_bitcast_fusion.4
  136.1 1.9 convolution_add_fusion.1
  138.0 1.8 dynamic_update_slice.13
  141.2 1.3 copy.80
  143.2 71.2 %all-reduce.8.cloned.1.call-done = f32[16,16,192]{2,1,0:T(8,128)} async-done(((f32[16,16,192]{2,1,0:T(8,128)}), f32[16,16,192]{2,1,0:T(8,128)}) %all-reduce.8.cloned.1.call-update) | async-done | bytes 196624 | tf_op jit(solution)/shard_map/psum | solution.py:56
  214.4 1.8 fusion.76
  216.2 1.3 collective-permute-start.5
  217.5 4.0 collective-permute-start.4
  222.1 1.3 collective-permute-done.4
  224.2 2.3 gather_fusion.3
  226.5 1.8 convolution_bitcast_fusion.3
  228.4 1.9 convolution_add_fusion
  230.3 1.1 dynamic_update_slice.14
  233.5 73.8 %all-reduce.10.cloned.1.call-done = f32[16,16,192]{2,1,0:T(8,128)} async-done(((f32[16,16,192]{2,1,0:T(8,128)}), f32[16,16,192]{2,1,0:T(8,128)}) %all-reduce.10.cloned.1.call-update) | async-done | bytes 196624 | tf_op jit(solution)/shard_map/psum | solution.py:56
  307.3 1.1 divide_subtract_fusion
  308.4 3.5 all_gather.9
  313.3 1.0 fusion.31
  314.5 23.4 %custom-call.7 = f32[8,32,32]{2,1,0:T(8,128)S(1)} custom-call(f32[8,32,32]{2,1,0:T(8,128)S(1)} %fusion.42), custom_call_target="Cholesky" | custom-call | tf_op jit(solution)/shard_map/jit(cholesky)/cholesky | solution.py:67
  339.6 19.7 %custom-call.8 = f32[8,1,32,32]{2,3,1,0:T(8,128)S(1)} custom-call(f32[8,1,32,32]{3,2,1,0:T(8,128)S(1)} %select_bitcast_fusion), custom_call_target="InvertDiagBlocksLowerTriangular" | custom-call | tf_op jit(solution)/shard_map/triangular_solve | solution.py:69
  359.3 1.1 fusion.40
  361.4 1.5 fusion.77
  362.8 1.3 gather_fusion.4
  364.1 1.9 fusion.79
  366.0 1.6 fusion.25
  367.8 1.0 copy-done.4
  368.8 1.9 fusion.23
  370.7 1.8 dynamic_update_slice.15
  372.5 1.3 collective-permute-start.9
  373.8 4.1 collective-permute-start.8
  381.5 49.3 %reduce-scatter.3.cloned.1.call-done = f32[16,1,16,192]{3,2,0,1:T(8,128)} async-done(((f32[16,4,16,192]{3,2,0,1:T(8,128)}), f32[16,1,16,192]{3,2,0,1:T(8,128)}) %reduce-scatter.3.cloned.1.call-update) | async-done | bytes 196624 | tf_op jit(solution)/shard_map/reduce_scatter | solution.py:97
  430.7 1.0 fusion.30
  431.8 23.9 %all_gather.10 = bf16[16,4,16,192]{3,2,0,1:T(8,128)(2,1)S(1)} all-gather(bf16[16,1,16,192]{3,2,0,1:T(8,128)(2,1)S(1)} %fusion.30), channel_id=1, replica_groups=mesh['rows'=64,'aggs'=4,'vecs'=2] {'aggs'}, dimensions={1}, use_global_device_ids=true | all-gather | bytes 491520 | tf_op jit(solution)/shard_map/all_gather | solution.py:104
  456.6 3.2 all_gather.11
  459.8 1.3 collective-permute-start.7
  461.1 6.3 collective-permute-start.6
  467.3 4.1 convolution_bitcast_fusion.2
  471.4 4.3 fusion.8
  475.7 5.0 fusion.16
  480.8 6.7 collective-permute-done.7
  488.3 3.5 pad_maximum_fusion
  491.8 3.9 gather_fusion.5
  495.7 6.5 convolution_bitcast_fusion.1
  502.3 12.0 %convolution_bitcast_fusion = f32[16,4,16,32,24]{3,4,2,1,0:T(8,128)S(1)} fusion(f32[16,2,4,4,16,32]{5,4,2,3,1,0:T(8,128)} %convolution_bitcast_fusion.1, s32[16,2,4]{2,1,0:T(2,128)S(1)} %bitcast.150), kind=kOutput, calls=%fused_computation.9 | convolution fusion | flops 75500544 | bytes 4194816 | tf_op jit(solution)/shard_map/ipg,ikqn,ikpqde->gnde/dot_general | solution.py:137
  514.3 12.9 %fusion.15 = f32[8,24,16,32]{3,0,1,2:T(8,128)} fusion(f32[16,32,8,24]{1,3,2,0:T(8,128)S(1)} %copy-done.3, f32[16,4,16,32,24]{3,4,2,1,0:T(8,128)S(1)} %convolution_bitcast_fusion, pred[16,4,8,1,1]{2,1,0,4,3:T(4,128)(4,1)S(1)} %copy-done.11), kind=kOutput, calls=%fused_computation.23 | convolution fusion | flops 75694080 | bytes 3932672 | tf_op jit(solution)/shard_map/ipg,ikqn,ikpqde->gnde/dot_general | solution.py:137
  527.2 1.3 dynamic-slice
  529.1 146.5 %all-reduce.12.cloned.1.call-done = f32[8,24,16,32]{3,0,1,2:T(8,128)} async-done(((f32[8,24,16,32]{3,0,1,2:T(8,128)}), f32[8,24,16,32]{3,0,1,2:T(8,128)}) %all-reduce.12.cloned.1.call-update) | async-done | bytes 393232
  675.6 1.0 constant_dynamic-slice_fusion.1
  (92 shorter events, 21.8 us)
Async XLA Ops:
  7.2 27.0 %copy-start = (bf16[16,2,192,192]{3,2,1,0:T(8,128)(2,1)S(1)}, bf16[16,2,192,192]{3,2,1,0:T(8,128)(2,1)}, u32[]{:S(2)}) copy-start(bf16[16,2,192,192]{3,2,1,0:T(8,128)(2,1)} %param.6) | copy-start | bytes 7077892
  7.2 113.3 %all-reduce.6.cloned.1.call-start = ((), (), s32[]{:S(2)}) async-start(), calls=%async_computation.1 | async-start | bytes 524288 | tf_op jit(solution)/shard_map/psum | solution.py:56
  8.3 21.7 %collective-permute-start.1 = (bf16[16,16,192]{2,1,0:T(8,128)(2,1)S(1)}, bf16[16,16,192]{2,1,0:T(8,128)(2,1)}, u32[]{:S(2)}, u32[]{:S(2)}) collective-permute-start(bf16[16,16,192]{2,1,0:T(8,128)(2,1)S(1)} %convert_element_type.46), channel_id=1, source_target_pairs={{8,0},{16,8},{24,16},{32,24},{40,32},{48,40},{56,48},{64,56},{72,6... | collective-permute-start | bytes 294920 | tf_op jit(solution)/shard_map/ppermute | solution.py:23
  9.6 20.4 %collective-permute-start = (bf16[16,16,192]{2,1,0:T(8,128)(2,1)S(1)}, bf16[16,16,192]{2,1,0:T(8,128)(2,1)}, u32[]{:S(2)}, u32[]{:S(2)}) collective-permute-start(bf16[16,16,192]{2,1,0:T(8,128)(2,1)S(1)} %convert_element_type.46), channel_id=1, source_target_pairs={{0,8},{8,16},{16,24},{24,32},{32,40},{40,48},{48,56},{56,64},{64,7... | collective-permute-start | bytes 294920 | tf_op jit(solution)/shard_map/ppermute | solution.py:22
  15.0 14.3 %copy-start.17 = (s32[16,2]{0,1:T(2,128)S(1)}, s32[16,2]{0,1:T(2,128)}, u32[]{:S(2)}) copy-start(s32[16,2]{0,1:T(2,128)} %param.8) | copy-start | bytes 388
  30.0 10.5 %copy-start.16 = (s32[16]{0:T(128)S(1)}, s32[16]{0:T(128)}, u32[]{:S(2)}) copy-start(s32[16]{0:T(128)} %param.9) | copy-start | bytes 196
  30.1 90.4 %copy-start.5 = (f32[16,16,192]{2,1,0:T(8,128)S(1)}, f32[16,16,192]{2,1,0:T(8,128)}, u32[]{:S(2)}) copy-start(f32[16,16,192]{2,1,0:T(8,128)} %param.11) | copy-start | bytes 589828
  36.0 0.7 copy-start.6
  40.5 173.9 %all-reduce.8.cloned.1.call-start = ((), (), s32[]{:S(2)}) async-start(), calls=%async_computation.2 | async-start | bytes 524288 | tf_op jit(solution)/shard_map/psum | solution.py:56
  121.5 8.0 %collective-permute-start.3 = (bf16[16,16,192]{2,1,0:T(8,128)(2,1)S(1)}, bf16[16,16,192]{2,1,0:T(8,128)(2,1)}, u32[]{:S(2)}, u32[]{:S(2)}) collective-permute-start(bf16[16,16,192]{2,1,0:T(8,128)(2,1)S(1)} %fusion.75), channel_id=1, source_target_pairs={{8,0},{16,8},{24,16},{32,24},{40,32},{48,40},{56,48},{64,56},{72,6... | collective-permute-start | bytes 294920 | tf_op jit(solution)/shard_map/ppermute | solution.py:23
  122.8 6.7 collective-permute-start.2
  129.5 10.4 %copy-start.14 = (s32[16,3]{0,1:T(4,128)S(1)}, s32[16,3]{0,1:T(4,128)}, u32[]{:S(2)}) copy-start(s32[16,3]{0,1:T(4,128)} %param.10) | copy-start | bytes 580
  135.4 0.7 copy-start.7
  139.8 167.5 %all-reduce.10.cloned.1.call-start = ((), (), s32[]{:S(2)}) async-start(), calls=%async_computation.3 | async-start | bytes 524288 | tf_op jit(solution)/shard_map/psum | solution.py:56
  216.2 5.9 collective-permute-start.5
  217.5 5.9 collective-permute-start.4
  231.4 0.7 copy-start.8
  232.1 198.6 %reduce-scatter.3.cloned.1.call-start = ((), (), s32[]{:S(2)}) async-start(), calls=%async_computation.4 | async-start | bytes 1310720 | tf_op jit(solution)/shard_map/reduce_scatter | solution.py:97
  311.9 0.8 copy-start.1
  364.1 1.9 copy-start.12
  367.6 11.9 %copy-start.15 = (s32[16,3]{0,1:T(4,128)S(1)}, s32[16,3]{0,1:T(4,128)}, u32[]{:S(2)}) copy-start(s32[16,3]{0,1:T(4,128)} %param.10) | copy-start | bytes 580
  367.8 1.0 copy-start.4
  372.5 303.1 %all-reduce.12.cloned.1.call-start = ((), (), s32[]{:S(2)}) async-start(), calls=%async_computation.5 | async-start | bytes 3145728
  372.5 6.9 %collective-permute-start.9 = (s32[16,4]{0,1:T(4,128)}, s32[16,4]{0,1:T(4,128)S(1)}, u32[]{:S(2)}, u32[]{:S(2)}) collective-permute-start(s32[16,4]{0,1:T(4,128)} %get-tuple-element.11), channel_id=1, source_target_pairs={{8,0},{16,8},{24,16},{32,24},{40,32},{48,40},{56,48},{64,56},{72,6... | collective-permute-start | bytes 776 | tf_op jit(solution)/shard_map/ppermute | solution.py:23
  373.8 5.6 collective-permute-start.8
  431.7 39.7 %copy-start.9 = (bf16[16,1,16,192]{3,2,0,1:T(8,128)(2,1)}, bf16[16,1,16,192]{3,2,0,1:T(8,128)(2,1)S(1)}, u32[]{:S(2)}) copy-start(bf16[16,1,16,192]{3,2,0,1:T(8,128)(2,1)S(1)} %fusion.30) | copy-start | bytes 294916
  455.7 0.8 copy-start.2
  459.8 27.7 %collective-permute-start.7 = (bf16[16,4,32,192]{3,2,1,0:T(8,128)(2,1)}, bf16[16,4,32,192]{3,2,1,0:T(8,128)(2,1)}, u32[]{:S(2)}, u32[]{:S(2)}) collective-permute-start(bf16[16,4,32,192]{3,2,1,0:T(8,128)(2,1)} %all_gather.11), channel_id=1, source_target_pairs={{8,0},{16,8},{24,16},{32,24},{40,32},{48,40},{56,48},{64,56},{72,6... | collective-permute-start | bytes 2359304 | tf_op jit(solution)/shard_map/ppermute | solution.py:23
  461.1 27.2 %collective-permute-start.6 = (bf16[16,4,32,192]{3,2,1,0:T(8,128)(2,1)}, bf16[16,4,32,192]{3,2,1,0:T(8,128)(2,1)}, u32[]{:S(2)}, u32[]{:S(2)}) collective-permute-start(bf16[16,4,32,192]{3,2,1,0:T(8,128)(2,1)} %all_gather.11), channel_id=1, source_target_pairs={{0,8},{8,16},{16,24},{24,32},{32,40},{40,48},{48,56},{56,64},{64,7... | collective-permute-start | bytes 2359304 | tf_op jit(solution)/shard_map/ppermute | solution.py:22
  471.4 4.3 copy-start.13
  495.7 6.5 copy-start.10
  502.2 12.0 %copy-start.3 = (f32[16,32,8,24]{1,3,2,0:T(8,128)S(1)}, f32[16,32,8,24]{1,3,2,0:T(8,128)}, u32[]{:S(2)}) copy-start(f32[16,32,8,24]{1,3,2,0:T(8,128)} %fusion.16) | copy-start | bytes 1179652
  502.2 12.0 %copy-start.11 = (pred[16,4,8,1,1]{2,1,0,4,3:T(4,128)(4,1)S(1)}, pred[16,4,8,1,1]{2,1,0,4,3:T(4,128)(4,1)}, u32[]{:S(2)}) copy-start(pred[16,4,8,1,1]{2,1,0,4,3:T(4,128)(4,1)} %fusion.51) | copy-start | bytes 1540
Sparse Core Ops, SparseCore 0:
  40.6 79.8 all-reduce.5
  139.9 74.4 all-reduce.7
  232.3 74.9 all-reduce.9
  372.6 58.0 reduce-scatter.2
  527.3 148.2 all-reduce.11
where the time goes:
time: 691 us; the launch traced here: 684 us
  waiting for transfers between devices  427 us (62%)
  other arithmetic  67.1 us (10%)
  matrix products  66.4 us (10%)
  local copies, waits for them, and re-layouts  46.5 us (7%)
  starting transfers between devices  31 us (4%)
  blocking collectives  30.7 us (4%)
  between operations  15 us (2%)
    psum x3, waiting for transfers between devices, on_device(): whole_sum = lax.psum(partial_sum, 'aggs')  223 us
    unnamed x6, waiting for transfers between devices  147 us
    reduce_scatter x1, waiting for transfers between devices, on_device(): lax.psum_scatter(partials, 'aggs', scatter_dimension=1, tiled=True)  49.3 us
    dot_general x2, matrix products, on_device(): jnp.einsum('ipg,ikqn,ikpqde->gnde', row_hot, col_hot, crossed, precision=...  24.9 us
    another operation x4, other arithmetic, on_device(): factor_low = jnp.linalg.cholesky(totals)  24.9 us
    ppermute x5, starting transfers between devices, with_halo(): before = lax.ppermute(last, axis, up)  24.4 us
    all_gather x1, blocking collectives, on_device(): own_slots = lax.all_gather(prolong_part, 'aggs', axis=1, tiled=True)  23.9 us
    another operation x3, other arithmetic, on_device(): lax.linalg.triangular_solve(factor_low, identity, left_side=True, lower=T...  21.1 us
  transfers between devices with their start and end apart: 15, of which 8 were waited for; matrix products, arithmetic and copies ran while one was open for 6% of the time, Pallas kernels for 0%

commit v1 on v0

v1 whole, which is shorter than its diff:
```python
import functools

import jax
import jax.numpy as jnp
from jax import lax
from jax.experimental import pallas as pl
from jax.experimental.pallas import tpu as pltpu
from jax.sharding import PartitionSpec as P

VECTORS = 32
SWEEPS = 3
SLAB_AGGS = 8
SLOTS = 4
DAMPING = 2.0 / 3.0
HIGHEST_PRECISION = lax.Precision.HIGHEST
BF16 = jnp.bfloat16
F32 = jnp.float32
VMEM_LIMIT = 32 * 1024 * 1024

SMEM_SPEC = pl.BlockSpec(memory_space=pltpu.SMEM)
VMEM_SPEC = pl.BlockSpec(memory_space=pltpu.VMEM)


def dot_nt(left, right):
    return lax.dot_general(left, right, (((1,), (1,)), ((), ())), preferred_element_type=F32)


def params():
    return pltpu.CompilerParams(vmem_limit_bytes=VMEM_LIMIT)


def center_kernel(diag_ref, x_ref, scale_ref, y_ref):
    for i in range(x_ref.shape[0]):
        x = x_ref[i]
        y_ref[i] = x - scale_ref[i : i + 1, :] * dot_nt(x.astype(BF16), diag_ref[i])


def first_center_kernel(diag_ref, x_ref, y_ref, scale_ref):
    width = x_ref.shape[2]
    on_diagonal = lax.broadcasted_iota(jnp.int32, (width, width), 0) == lax.broadcasted_iota(
        jnp.int32, (width, width), 1
    )
    for i in range(x_ref.shape[0]):
        x = x_ref[i]
        block = diag_ref[i]
        pivot = jnp.sum(jnp.where(on_diagonal, block.astype(F32), 0.0), axis=0, keepdims=True)
        scale = DAMPING / pivot
        scale_ref[i : i + 1, :] = scale
        y_ref[i] = x - scale * dot_nt(x.astype(BF16), block)


def couple_kernel(col_ref, a_ref, before_ref, own_ref, after_ref, out_ref, ext):
    rows, stored = a_ref.shape[:2]
    ext[0:rows] = before_ref[...]
    ext[rows : 2 * rows] = own_ref[...]
    ext[2 * rows : 3 * rows] = after_ref[...]
    for i in range(rows):
        total = dot_nt(ext[col_ref[i, 0]], a_ref[i, 0])
        for k in range(1, stored):
            total = total + dot_nt(ext[col_ref[i, k]], a_ref[i, k])
        out_ref[i] = total.astype(BF16)


def fit_kernel(col_ref, a_ref, own_ref, out_ref):
    rows, stored = a_ref.shape[:2]
    for i in range(rows):
        for k in range(stored):
            row = jnp.clip(col_ref[i, k] - rows, 0, rows - 1)
            out_ref[i, k] = dot_nt(own_ref[row], a_ref[i, k]).astype(BF16)


def slot_kernel(slot_ref, far_slot_ref, near_ref, far_ref, out_ref):
    rows, stored = near_ref.shape[:2]
    for i in range(rows):
        for p in range(SLOTS):
            total = jnp.zeros(near_ref.shape[2:], F32)
            for k in range(stored):
                total = total + jnp.where(slot_ref[i, k] == p, near_ref[i, k].astype(F32), 0.0)
                total = total + jnp.where(far_slot_ref[i, k] == p, far_ref[i, k].astype(F32), 0.0)
            out_ref[i, p] = total.astype(BF16)


def inverse_factor_kernel(m_ref, out_ref):
    size = m_ref.shape[0]
    rows = [m_ref[v] for v in range(size)]
    place = lax.broadcasted_iota(jnp.int32, rows[0].shape, 0)
    for k in range(size):
        root = lax.rsqrt(rows[k][k : k + 1, :])
        here = place == k
        pivot_row = jnp.where(here, root, rows[k] * root)
        rows[k] = jnp.where(place <= k, pivot_row, 0.0)
        out_ref[k] = rows[k]
        for v in range(k + 1, size):
            rows[v] = jnp.where(here, 0.0, rows[v]) - pivot_row[v : v + 1, :] * pivot_row


def coarse_kernel(
    where_ref, col_ref, place_ref, a_ref, diag_ref, before_ref, own_ref, after_ref, other_ref,
    keep_ref, send_ref, ext, reach, left, total,
):
    rows, stored = a_ref.shape[:2]
    vectors = own_ref.shape[2]
    width = own_ref.shape[3]
    share = rows // 4
    core, slot = where_ref[0], where_ref[1]
    ext[0:rows] = before_ref[...]
    ext[rows : 2 * rows] = own_ref[...]
    ext[2 * rows : 3 * rows] = after_ref[...]
    reach[...] = jnp.zeros_like(reach)
    left[...] = jnp.zeros_like(left)
    span = reach.shape[1]

    def add(i, row, block):
        image = dot_nt(ext[row].reshape(SLOTS * vectors, width), block)
        for q in range(SLOTS):
            at = place_ref[row, q]
            reach[i, at] = reach[i, at] + image[q * vectors : (q + 1) * vectors]

    for i in range(rows):
        for p in range(SLOTS):
            group = place_ref[rows + i, p] - SLAB_AGGS
            left[i, group, core] = own_ref[i, p]
            left[i, group, 1 - core] = other_ref[i, p]
        for k in range(stored):
            add(i, col_ref[i, k], a_ref[i, k])

    for r in range(share):
        i = slot * share + r
        add(i, rows + i, diag_ref[i])

    for i in range(rows):
        product = dot_nt(
            reach[i].astype(BF16).reshape(span * vectors, width),
            left[i].reshape(SLAB_AGGS * 2 * vectors, width),
        )
        if i == 0:
            total[...] = product
        else:
            total[...] = total[...] + product
    quarter = span * vectors // 4
    for n in range(2):
        start = pl.multiple_of(where_ref[2 + n] * quarter, 32)
        keep_ref[n] = total[pl.ds(start, quarter), :] * (1.0 / width)
        start = pl.multiple_of(where_ref[4 + n] * quarter, 32)
        send_ref[n] = (total[pl.ds(start, quarter), :] * (1.0 / width)).astype(BF16)


def shift(x, by):
    size = lax.axis_size("rows")
    return lax.ppermute(x, "rows", [(i, i + by) for i in range(size) if 0 <= i + by < size])


def partner(slot, core, phase):
    return slot ^ 1 if (core + phase) % 2 == 0 else 3 - slot


def exchange(x, phase):
    pairs = [(2 * s + c, 2 * partner(s, c, phase) + c) for s in range(4) for c in range(2)]
    return lax.ppermute(x, ("aggs", "vecs"), pairs)


def on_device(couplings, diag_blocks, coupling_cols, aggregate, pattern, tests):
    rows, vectors, width = tests.shape
    stored = couplings.shape[1]
    slab = lax.axis_index("rows")
    slot = lax.axis_index("aggs")
    core = lax.axis_index("vecs")
    shape = (rows, vectors, width)
    cols = coupling_cols - slab * rows + rows

    local_aggs = aggregate - slab * SLAB_AGGS
    slot_aggs = jnp.concatenate([aggregate[:, None], pattern], axis=1) - slab * SLAB_AGGS
    before_slots = shift(slot_aggs, 1)
    after_slots = shift(slot_aggs, -1)
    places = jnp.concatenate(
        [before_slots, slot_aggs + SLAB_AGGS, after_slots + 2 * SLAB_AGGS], axis=0
    )

    def slots_of(columns):
        inside = columns[:, :, None] == jnp.arange(rows, 2 * rows, dtype=jnp.int32)
        aggs = jnp.sum(jnp.where(inside, local_aggs + 1, 0), axis=2) - 1
        hits = aggs[:, :, None] == slot_aggs[:, None, :]
        return jnp.sum(jnp.where(hits, jnp.arange(1, SLOTS + 1, dtype=jnp.int32), 0), axis=2) - 1

    near_slot = slots_of(cols)
    far_slot = exchange(near_slot, 0)

    center = pl.pallas_call(
        center_kernel,
        out_shape=jax.ShapeDtypeStruct(shape, F32),
        in_specs=[VMEM_SPEC] * 3,
        out_specs=VMEM_SPEC,
        compiler_params=params(),
        name="center",
    )
    first_center = pl.pallas_call(
        first_center_kernel,
        out_shape=[jax.ShapeDtypeStruct(shape, F32), jax.ShapeDtypeStruct((rows, width), F32)],
        in_specs=[VMEM_SPEC] * 2,
        out_specs=[VMEM_SPEC] * 2,
        compiler_params=params(),
        name="first_center",
    )
    couple = pl.pallas_call(
        couple_kernel,
        out_shape=jax.ShapeDtypeStruct(shape, BF16),
        in_specs=[SMEM_SPEC] + [VMEM_SPEC] * 4,
        out_specs=VMEM_SPEC,
        scratch_shapes=[pltpu.VMEM((3 * rows, vectors, width), BF16)],
        compiler_params=params(),
        name="couple",
    )

    current = tests
    scale = None
    for sweep in range(SWEEPS):
        rounded = current.astype(BF16)
        before = shift(rounded, 1)
        after = shift(rounded, -1)
        if sweep == 0:
            rest, scale = first_center(diag_blocks, current)
        else:
            rest = center(diag_blocks, current, scale)
        part = couple(cols, couplings, before, rounded, after)
        pair = (part.astype(F32) + exchange(part, 0).astype(F32)).astype(BF16)
        whole = pair.astype(F32) + exchange(pair, 1).astype(F32)
        current = rest - scale[:, None, :] * whole

    every = lax.all_gather(current, "vecs", axis=1, tiled=True)
    grams = jnp.einsum("ivb,iwb->ivw", every, every, precision=HIGHEST_PRECISION)
    members = (local_aggs[:, None] == jnp.arange(SLAB_AGGS, dtype=jnp.int32)[None, :]).astype(F32)
    totals = jnp.einsum("ig,ivw->vwg", members, grams, precision=HIGHEST_PRECISION) / width
    inverse = pl.pallas_call(
        inverse_factor_kernel,
        out_shape=jax.ShapeDtypeStruct((VECTORS, VECTORS, SLAB_AGGS), F32),
        in_specs=[VMEM_SPEC],
        out_specs=VMEM_SPEC,
        compiler_params=params(),
        name="inverse_factor",
    )(totals)
    own_inverse = lax.dynamic_slice_in_dim(inverse, core * vectors, vectors, 0)
    row_inverse = jnp.einsum("ig,cvg->icv", members, own_inverse, precision=HIGHEST_PRECISION)
    tentative = jnp.einsum("icv,ivb->icb", row_inverse, every, precision=HIGHEST_PRECISION)

    moved = pl.pallas_call(
        fit_kernel,
        out_shape=jax.ShapeDtypeStruct((rows, stored, vectors, width), BF16),
        in_specs=[SMEM_SPEC] + [VMEM_SPEC] * 2,
        out_specs=VMEM_SPEC,
        compiler_params=params(),
        name="fit",
    )(cols, couplings, tentative.astype(BF16))
    rest = center(diag_blocks, tentative, scale)
    far_moved = exchange(moved, 0)
    pair = pl.pallas_call(
        slot_kernel,
        out_shape=jax.ShapeDtypeStruct((rows, SLOTS, vectors, width), BF16),
        in_specs=[SMEM_SPEC] * 2 + [VMEM_SPEC] * 2,
        out_specs=VMEM_SPEC,
        compiler_params=params(),
        name="slots",
    )(near_slot, far_slot, moved, far_moved)
    fitted = pair.astype(F32) + exchange(pair, 1).astype(F32)
    leading = (jnp.arange(SLOTS, dtype=jnp.int32) == 0)[None, :, None, None]
    prolong = (
        jnp.where(leading, rest[:, None], 0.0) - scale[:, None, None, :] * fitted
    ).astype(BF16)
    prolong_here = lax.dynamic_slice_in_dim(prolong, slot, 1, 1)

    before = shift(prolong, 1)
    after = shift(prolong, -1)
    other = lax.ppermute(prolong, "vecs", [(0, 1), (1, 0)])
    first = jnp.where(core == 0, slot ^ 1, 3 - slot)
    second = jnp.where(core == 0, 3 - slot, slot ^ 1)
    where = jnp.stack([core, slot, slot, second, first, slot ^ 2]).astype(jnp.int32)
    span = 3 * SLAB_AGGS
    quarter = span * vectors // 4
    wide = SLAB_AGGS * 2 * vectors
    keep, send = pl.pallas_call(
        coarse_kernel,
        out_shape=[
            jax.ShapeDtypeStruct((2, quarter, wide), F32),
            jax.ShapeDtypeStruct((2, quarter, wide), BF16),
        ],
        in_specs=[SMEM_SPEC] * 3 + [VMEM_SPEC] * 6,
        out_specs=[VMEM_SPEC] * 2,
        scratch_shapes=[
            pltpu.VMEM((3 * rows, SLOTS, vectors, width), BF16),
            pltpu.VMEM((rows, span, vectors, width), F32),
            pltpu.VMEM((rows, SLAB_AGGS, 2, vectors, width), BF16),
            pltpu.VMEM((span * vectors, wide), F32),
        ],
        compiler_params=params(),
        name="coarse",
    )(where, cols, places, couplings, diag_blocks, before, prolong, after, other)
    half = keep + exchange(send, 0).astype(F32)
    owned = half[0] + exchange(half[1].astype(BF16), 1).astype(F32)
    owned = owned.reshape(span // 4, vectors, SLAB_AGGS, 2, vectors)
    mine = lax.dynamic_index_in_dim(owned, core, 3, keepdims=False)
    theirs = lax.dynamic_index_in_dim(owned, 1 - core, 3, keepdims=False)
    theirs = lax.ppermute(theirs, "vecs", [(0, 1), (1, 0)])
    low = jnp.where(core == 0, mine, theirs)
    high = jnp.where(core == 0, theirs, mine)
    coarse = jnp.concatenate([low, high], axis=1).transpose(2, 0, 3, 1)
    return (prolong_here, coarse)


def solution(mesh):
    return jax.shard_map(
        on_device,
        mesh=mesh,
        in_specs=(
            P("rows", "aggs", None, None),
            P("rows", None, None),
            P("rows", "aggs"),
            P("rows"),
            P("rows", None),
            P("rows", "vecs", None),
        ),
        out_specs=(P("rows", "aggs", "vecs", None), P("rows", "aggs", "vecs", None)),
        check_vma=False,
    )
```

time: 691 us -> 258 us (0.37)
  the two profiles are of different devices: /device:TPU:1 before, /device:TPU:65 now
where the time goes in v1:
time: 258 us; the launch traced here: 257 us
  starting transfers between devices  147 us (57%)
  waiting for transfers between devices  50.4 us (20%)
  local copies, waits for them, and re-layouts  15.3 us (6%)
  blocking collectives  15.2 us (6%)
  Pallas kernels  15.1 us (6%)
  other arithmetic  10.2 us (4%)
    ppermute x11, starting transfers between devices, exchange(): return lax.ppermute(x, ('aggs', 'vecs'), pairs)  72.6 us
    ppermute x10, starting transfers between devices, shift(): lax.ppermute(x, 'rows', [(i, i + by) for i in range(size) if 0 <= i + by...  54.2 us
    ppermute x11, waiting for transfers between devices, exchange(): return lax.ppermute(x, ('aggs', 'vecs'), pairs)  40.9 us
    ppermute x1, starting transfers between devices, on_device(): other = lax.ppermute(prolong, 'vecs', [(0, 1), (1, 0)])  16 us
    all_gather x1, blocking collectives, on_device(): every = lax.all_gather(current, 'vecs', axis=1, tiled=True)  15.2 us
    unnamed x28, local copies, waits for them, and re-layouts  10.7 us
    ppermute x10, waiting for transfers between devices, shift(): lax.ppermute(x, 'rows', [(i, i + by) for i in range(size) if 0 <= i + by...  9.57 us
    pallas_call x3, Pallas kernels, on_device(): part = couple(cols, couplings, before, rounded, after)  5.41 us
  transfers between devices with their start and end apart: 23, of which 17 were waited for; matrix products, arithmetic and copies ran while one was open for 1% of the time, Pallas kernels for 1%

profile of v1, /device:TPU:65, one launch (start us, length us, event | category | flops | bytes accessed | tf_op | source)
XLA Modules:
  0.0 257.3 jit_solution(8545646473620271787)
XLA Ops:
  0.6 1.0 convert_element_type.77.own_ref
  1.7 3.2 %collective-permute-start = (bf16[16,16,192]{2,1,0:T(8,128)(2,1)S(1)}, bf16[16,16,192]{2,1,0:T(8,128)(2,1)S(1)}, u32[]{:S(2)}, u32[]{:S(2)}) collective-permute-start(bf16[16,16,192]{2,1,0:T(8,128)(2,1)S(1)} %convert_element_type.77.own_ref), channel_id=1, source_target_pairs={{0,8},{8,16},{16,24},{24,32},{32,40},{40,48},{48,56},{56,64},{64,7... | collective-permute-start | bytes 294920 | tf_op jit(solution)/shard_map/ppermute | solution.py:150
  4.9 6.3 %collective-permute-start.1 = (bf16[16,16,192]{2,1,0:T(8,128)(2,1)S(1)}, bf16[16,16,192]{2,1,0:T(8,128)(2,1)S(1)}, u32[]{:S(2)}, u32[]{:S(2)}) collective-permute-start(bf16[16,16,192]{2,1,0:T(8,128)(2,1)S(1)} %convert_element_type.77.own_ref), channel_id=1, source_target_pairs={{8,0},{16,8},{24,16},{32,24},{40,32},{48,40},{56,48},{64,56},{72,6... | collective-permute-start | bytes 294920 | tf_op jit(solution)/shard_map/ppermute | solution.py:150
  11.2 0.7 broadcast_subtract_fusion
  13.8 1.9 copy-done
  15.7 0.9 copy-done.9
  16.6 0.9 copy-done.11
  17.5 2.3 couple.3
  19.7 10.6 %collective-permute-start.2 = (bf16[16,16,192]{2,1,0:T(8,128)(2,1)}, bf16[16,16,192]{2,1,0:T(8,128)(2,1)S(1)}, u32[]{:S(2)}, u32[]{:S(2)}) collective-permute-start(bf16[16,16,192]{2,1,0:T(8,128)(2,1)} %couple.3), channel_id=1, source_target_pairs={{0,2},{1,7},{2,0},{3,5},{4,6},{5,3},{6,4},{7,1},{8,10},{9,15},{10,... | collective-permute-start | bytes 294920 | tf_op jit(solution)/shard_map/ppermute | solution.py:159
  30.4 4.3 %collective-permute-done.2 = bf16[16,16,192]{2,1,0:T(8,128)(2,1)S(1)} collective-permute-done((bf16[16,16,192]{2,1,0:T(8,128)(2,1)}, bf16[16,16,192]{2,1,0:T(8,128)(2,1)S(1)}, u32[]{:S(2)}, u32[]{:S(2)}) %collective-permute-start.2) | collective-permute-done | bytes 98336 | tf_op jit(solution)/shard_map/ppermute | solution.py:159
  34.6 1.6 add_convert_fusion.2
  36.2 4.5 %collective-permute-start.3 = (bf16[16,16,192]{2,1,0:T(8,128)(2,1)}, bf16[16,16,192]{2,1,0:T(8,128)(2,1)}, u32[]{:S(2)}, u32[]{:S(2)}) collective-permute-start(bf16[16,16,192]{2,1,0:T(8,128)(2,1)} %add_convert_fusion.2), channel_id=1, source_target_pairs={{0,6},{1,3},{2,4},{3,1},{4,2},{5,7},{6,0},{7,5},{8,14},{9,11},{10,... | collective-permute-start | bytes 294920 | tf_op jit(solution)/shard_map/ppermute | solution.py:159
  40.9 1.4 copy-done.2
  42.8 6.5 %collective-permute-done.3 = bf16[16,16,192]{2,1,0:T(8,128)(2,1)} collective-permute-done((bf16[16,16,192]{2,1,0:T(8,128)(2,1)}, bf16[16,16,192]{2,1,0:T(8,128)(2,1)}, u32[]{:S(2)}, u32[]{:S(2)}) %collective-permute-start.3) | collective-permute-done | bytes 98336 | tf_op jit(solution)/shard_map/ppermute | solution.py:159
  49.3 1.0 fusion.15
  50.3 1.9 collective-permute-start.4
  52.3 7.6 %collective-permute-start.5 = (bf16[16,16,192]{2,1,0:T(8,128)(2,1)S(1)}, bf16[16,16,192]{2,1,0:T(8,128)(2,1)S(1)}, u32[]{:S(2)}, u32[]{:S(2)}) collective-permute-start(bf16[16,16,192]{2,1,0:T(8,128)(2,1)S(1)} %get-tuple-element.14.own_ref), channel_id=1, source_target_pairs={{8,0},{16,8},{24,16},{32,24},{40,32},{48,40},{56,48},{64,56},{72,6... | collective-permute-start | bytes 294920 | tf_op jit(solution)/shard_map/ppermute | solution.py:150
  60.3 1.5 collective-permute-done.5.after_ref
  61.8 1.6 couple.4
  63.4 6.1 %collective-permute-start.6 = (bf16[16,16,192]{2,1,0:T(8,128)(2,1)S(1)}, bf16[16,16,192]{2,1,0:T(8,128)(2,1)S(1)}, u32[]{:S(2)}, u32[]{:S(2)}) collective-permute-start(bf16[16,16,192]{2,1,0:T(8,128)(2,1)S(1)} %couple.4), channel_id=1, source_target_pairs={{0,2},{1,7},{2,0},{3,5},{4,6},{5,3},{6,4},{7,1},{8,10},{9,15},{10,... | collective-permute-start | bytes 294920 | tf_op jit(solution)/shard_map/ppermute | solution.py:159
  69.7 3.4 %collective-permute-done.6 = bf16[16,16,192]{2,1,0:T(8,128)(2,1)S(1)} collective-permute-done((bf16[16,16,192]{2,1,0:T(8,128)(2,1)S(1)}, bf16[16,16,192]{2,1,0:T(8,128)(2,1)S(1)}, u32[]{:S(2)}, u32[]{:S(2)}) %collective-permute-start.6) | collective-permute-done | bytes 98336 | tf_op jit(solution)/shard_map/ppermute | solution.py:159
  73.1 0.7 add_convert_fusion.1
  73.8 7.2 %collective-permute-start.7 = (bf16[16,16,192]{2,1,0:T(8,128)(2,1)}, bf16[16,16,192]{2,1,0:T(8,128)(2,1)}, u32[]{:S(2)}, u32[]{:S(2)}) collective-permute-start(bf16[16,16,192]{2,1,0:T(8,128)(2,1)} %add_convert_fusion.1), channel_id=1, source_target_pairs={{0,6},{1,3},{2,4},{3,1},{4,2},{5,7},{6,0},{7,5},{8,14},{9,11},{10,... | collective-permute-start | bytes 294920 | tf_op jit(solution)/shard_map/ppermute | solution.py:159
  81.0 1.4 copy-done.3
  83.0 0.7 collective-permute-done.7
  83.7 1.0 fusion.14
  84.7 1.9 collective-permute-start.8
  86.6 9.5 %collective-permute-start.9 = (bf16[16,16,192]{2,1,0:T(8,128)(2,1)S(1)}, bf16[16,16,192]{2,1,0:T(8,128)(2,1)S(1)}, u32[]{:S(2)}, u32[]{:S(2)}) collective-permute-start(bf16[16,16,192]{2,1,0:T(8,128)(2,1)S(1)} %get-tuple-element.12.own_ref), channel_id=1, source_target_pairs={{8,0},{16,8},{24,16},{32,24},{40,32},{48,40},{56,48},{64,56},{72,6... | collective-permute-start | bytes 294920 | tf_op jit(solution)/shard_map/ppermute | solution.py:150
  96.2 1.6 collective-permute-done.8.before_ref
  98.1 1.6 couple.5
  99.7 7.2 %collective-permute-start.10 = (bf16[16,16,192]{2,1,0:T(8,128)(2,1)S(1)}, bf16[16,16,192]{2,1,0:T(8,128)(2,1)S(1)}, u32[]{:S(2)}, u32[]{:S(2)}) collective-permute-start(bf16[16,16,192]{2,1,0:T(8,128)(2,1)S(1)} %couple.5), channel_id=1, source_target_pairs={{0,2},{1,7},{2,0},{3,5},{4,6},{5,3},{6,4},{7,1},{8,10},{9,15},{10,... | collective-permute-start | bytes 294920 | tf_op jit(solution)/shard_map/ppermute | solution.py:159
  106.9 3.0 %collective-permute-done.10 = bf16[16,16,192]{2,1,0:T(8,128)(2,1)S(1)} collective-permute-done((bf16[16,16,192]{2,1,0:T(8,128)(2,1)S(1)}, bf16[16,16,192]{2,1,0:T(8,128)(2,1)S(1)}, u32[]{:S(2)}, u32[]{:S(2)}) %collective-permute-start.10) | collective-permute-done | bytes 98336 | tf_op jit(solution)/shard_map/ppermute | solution.py:159
  109.9 0.7 add_convert_fusion
  110.6 5.7 %collective-permute-start.11 = (bf16[16,16,192]{2,1,0:T(8,128)(2,1)}, bf16[16,16,192]{2,1,0:T(8,128)(2,1)}, u32[]{:S(2)}, u32[]{:S(2)}) collective-permute-start(bf16[16,16,192]{2,1,0:T(8,128)(2,1)} %add_convert_fusion), channel_id=1, source_target_pairs={{0,6},{1,3},{2,4},{3,1},{4,2},{5,7},{6,0},{7,5},{8,14},{9,11},{10,... | collective-permute-start | bytes 294920 | tf_op jit(solution)/shard_map/ppermute | solution.py:159
  116.4 1.4 copy-done.4
  118.4 4.3 %collective-permute-done.11 = bf16[16,16,192]{2,1,0:T(8,128)(2,1)} collective-permute-done((bf16[16,16,192]{2,1,0:T(8,128)(2,1)}, bf16[16,16,192]{2,1,0:T(8,128)(2,1)}, u32[]{:S(2)}, u32[]{:S(2)}) %collective-permute-start.11) | collective-permute-done | bytes 98336 | tf_op jit(solution)/shard_map/ppermute | solution.py:159
  122.6 1.0 multiply_subtract_fusion
  123.7 15.2 %all_gather.3 = f32[16,32,192]{2,1,0:T(8,128)S(1)} all-gather(f32[16,16,192]{2,1,0:T(8,128)S(1)} %multiply_subtract_fusion), channel_id=1, replica_groups=mesh['rows'=64,'aggs'=4,'vecs'=2] {'vecs'}, dimensions={1}, use_global_device_ids=true | all-gather | bytes 589824 | tf_op jit(solution)/shard_map/all_gather | solution.py:229
  140.2 0.8 inverse_factor.1
  142.0 1.6 fit.1.near_ref
  143.6 6.4 %collective-permute-start.13 = (bf16[16,2,16,192]{3,2,1,0:T(8,128)(2,1)S(1)}, bf16[16,2,16,192]{3,2,1,0:T(8,128)(2,1)S(1)}, u32[]{:S(2)}, u32[]{:S(2)}) collective-permute-start(bf16[16,2,16,192]{3,2,1,0:T(8,128)(2,1)S(1)} %fit.1.near_ref), channel_id=1, source_target_pairs={{0,2},{1,7},{2,0},{3,5},{4,6},{5,3},{6,4},{7,1},{8,10},{9,15},{10,... | collective-permute-start | bytes 589832 | tf_op jit(solution)/shard_map/ppermute | solution.py:159
  150.0 2.8 %collective-permute-start.12 = (s32[16,2]{1,0:T(8,128)S(1)}, s32[16,2]{1,0:T(8,128)S(1)}, u32[]{:S(2)}, u32[]{:S(2)}) collective-permute-start(s32[16,2]{1,0:T(8,128)S(1)} %broadcast_add_fusion.slot_ref), channel_id=1, source_target_pairs={{0,2},{1,7},{2,0},{3,5},{4,6},{5,3},{6,4},{7,1},{8,10},{9,15},{10,... | collective-permute-start | bytes 392 | tf_op jit(solution)/shard_map/ppermute | solution.py:159
  152.8 5.6 %collective-permute-done.12.far_slot_ref = s32[16,2]{1,0:T(8,128)S(1)} collective-permute-done((s32[16,2]{1,0:T(8,128)S(1)}, s32[16,2]{1,0:T(8,128)S(1)}, u32[]{:S(2)}, u32[]{:S(2)}) %collective-permute-start.12) | collective-permute-done | bytes 160 | tf_op jit(solution)/shard_map/ppermute | solution.py:159
  158.4 1.2 slots.1
  159.6 6.9 %collective-permute-start.14 = (bf16[16,4,16,192]{3,2,1,0:T(8,128)(2,1)S(1)}, bf16[16,4,16,192]{3,2,1,0:T(8,128)(2,1)S(1)}, u32[]{:S(2)}, u32[]{:S(2)}) collective-permute-start(bf16[16,4,16,192]{3,2,1,0:T(8,128)(2,1)S(1)} %slots.1), channel_id=1, source_target_pairs={{0,6},{1,3},{2,4},{3,1},{4,2},{5,7},{6,0},{7,5},{8,14},{9,11},{10,... | collective-permute-start | bytes 1179656 | tf_op jit(solution)/shard_map/ppermute | solution.py:159
  167.0 8.7 %collective-permute-done.14 = bf16[16,4,16,192]{3,2,1,0:T(8,128)(2,1)S(1)} collective-permute-done((bf16[16,4,16,192]{3,2,1,0:T(8,128)(2,1)S(1)}, bf16[16,4,16,192]{3,2,1,0:T(8,128)(2,1)S(1)}, u32[]{:S(2)}, u32[]{:S(2)}) %collective-permute-start.14) | collective-permute-done | bytes 393248 | tf_op jit(solution)/shard_map/ppermute | solution.py:159
  175.7 1.1 subtract_convert_fusion.own_ref
  176.8 16.5 %collective-permute-start.17 = (bf16[16,4,16,192]{3,2,1,0:T(8,128)(2,1)}, bf16[16,4,16,192]{3,2,1,0:T(8,128)(2,1)}, u32[]{:S(2)}, u32[]{:S(2)}) collective-permute-start(bf16[16,4,16,192]{3,2,1,0:T(8,128)(2,1)} %subtract_convert_fusion.own_ref), channel_id=1, source_target_pairs={{0,8},{8,16},{16,24},{24,32},{32,40},{40,48},{48,56},{56,64},{64,7... | collective-permute-start | bytes 1179656 | tf_op jit(solution)/shard_map/ppermute | solution.py:150
  193.4 1.9 collective-permute-start.18
  195.3 16.0 %collective-permute-start.19 = (bf16[16,4,16,192]{3,2,1,0:T(8,128)(2,1)}, bf16[16,4,16,192]{3,2,1,0:T(8,128)(2,1)}, u32[]{:S(2)}, u32[]{:S(2)}) collective-permute-start(bf16[16,4,16,192]{3,2,1,0:T(8,128)(2,1)} %subtract_convert_fusion.own_ref), channel_id=1, source_target_pairs={{0,1},{1,0},{2,3},{3,2},{4,5},{5,4},{6,7},{7,6},{8,9},{9,8},{10,11... | collective-permute-start | bytes 1179656 | tf_op jit(solution)/shard_map/ppermute | solution.py:272
  211.3 1.9 collective-permute-start.16
  213.2 3.4 %collective-permute-start.15 = (s32[16,4]{0,1:T(4,128)S(1)}, s32[16,4]{0,1:T(4,128)S(1)}, u32[]{:S(2)}, u32[]{:S(2)}) collective-permute-start(s32[16,4]{0,1:T(4,128)S(1)} %get-tuple-element.11), channel_id=1, source_target_pairs={{0,8},{8,16},{16,24},{24,32},{32,40},{40,48},{48,56},{56,64},{64,7... | collective-permute-start | bytes 776 | tf_op jit(solution)/shard_map/ppermute | solution.py:150
  216.7 5.3 %collective-permute-done.15 = s32[16,4]{0,1:T(4,128)S(1)} collective-permute-done((s32[16,4]{0,1:T(4,128)S(1)}, s32[16,4]{0,1:T(4,128)S(1)}, u32[]{:S(2)}, u32[]{:S(2)}) %collective-permute-start.15) | collective-permute-done | bytes 288 | tf_op jit(solution)/shard_map/ppermute | solution.py:150
  222.2 1.4 copy-done.6
  223.6 4.2 %coarse.1 = (f32[2,96,256]{2,1,0:T(8,128)S(1)}, bf16[2,96,256]{2,1,0:T(8,128)(2,1)S(1)}) custom-call(s32[6]{0:T(128)S(1)} %stack.24.where_ref, s32[16,2]{1,0:T(8,128)S(1)} %broadcast_add_fusion.1.col_ref, s32[48,4]{1,0:T(8,128)S(1)} %copy.42.place_ref, bf16[16,2,192,192]{3,2,1,0:T(8,128)(2,1)S(1)} %copy-done.1, bf16[16,192,192]{2,1,0:T(8,128)(2,1)S(1)} %copy-done.6, ...), custom_call_target="tpu_custom_call" | custom-call | tf_op jit(solution)/shard_map/coarse/pallas_call | solution.py:279
  227.7 6.3 %collective-permute-start.20 = (bf16[2,96,256]{2,1,0:T(8,128)(2,1)S(1)}, bf16[2,96,256]{2,1,0:T(8,128)(2,1)S(1)}, u32[]{:S(2)}, u32[]{:S(2)}) collective-permute-start(bf16[2,96,256]{2,1,0:T(8,128)(2,1)S(1)} %get-tuple-element.9), channel_id=1, source_target_pairs={{0,2},{1,7},{2,0},{3,5},{4,6},{5,3},{6,4},{7,1},{8,10},{9,15},{10,... | collective-permute-start | bytes 294920 | tf_op jit(solution)/shard_map/ppermute | solution.py:159
  234.1 2.9 %collective-permute-done.20 = bf16[2,96,256]{2,1,0:T(8,128)(2,1)S(1)} collective-permute-done((bf16[2,96,256]{2,1,0:T(8,128)(2,1)S(1)}, bf16[2,96,256]{2,1,0:T(8,128)(2,1)S(1)}, u32[]{:S(2)}, u32[]{:S(2)}) %collective-permute-start.20) | collective-permute-done | bytes 98336 | tf_op jit(solution)/shard_map/ppermute | solution.py:159
  237.1 8.8 %collective-permute-start.21 = (bf16[96,256]{1,0:T(8,128)(2,1)S(1)}, bf16[96,256]{1,0:T(8,128)(2,1)S(1)}, u32[]{:S(2)}, u32[]{:S(2)}) collective-permute-start(bf16[96,256]{1,0:T(8,128)(2,1)S(1)} %fusion.6), channel_id=1, source_target_pairs={{0,6},{1,3},{2,4},{3,1},{4,2},{5,7},{6,0},{7,5},{8,14},{9,11},{10,... | collective-permute-start | bytes 147464 | tf_op jit(solution)/shard_map/ppermute | solution.py:159
  245.8 1.5 collective-permute-done.21
  247.3 1.0 reshape.40
  248.4 0.9 constant_dynamic-slice_fusion.1
  249.6 4.7 %collective-permute-start.22 = (f32[6,16,8,16]{1,3,0,2:T(8,128)S(1)}, f32[6,16,8,16]{1,3,0,2:T(8,128)S(1)}, u32[]{:S(2)}, u32[]{:S(2)}) collective-permute-start(f32[6,16,8,16]{1,3,0,2:T(8,128)S(1)} %bitcast.27), channel_id=1, source_target_pairs={{0,1},{1,0},{2,3},{3,2},{4,5},{5,4},{6,7},{7,6},{8,9},{9,8},{10,11... | collective-permute-start | bytes 147464 | tf_op jit(solution)/shard_map/ppermute | solution.py:301
  254.3 1.6 constant_dynamic-slice_fusion.2
  256.3 0.9 maximum_bitcast_fusion
  (62 shorter events, 8.6 us)
Async XLA Ops:
  0.6 40.2 %copy-start.7 = (f32[16,16,192]{2,1,0:T(8,128)S(1)}, f32[16,16,192]{2,1,0:T(8,128)}, u32[]{:S(2)}) copy-start(f32[16,16,192]{2,1,0:T(8,128)} %x_ref.1) | copy-start | bytes 589828
  0.6 40.1 %copy-start.12 = (s32[16]{0:T(128)S(1)}, s32[16]{0:T(128)}, u32[]{:S(2)}) copy-start(s32[16]{0:T(128)} %param.9) | copy-start | bytes 196
  1.7 10.5 %collective-permute-start = (bf16[16,16,192]{2,1,0:T(8,128)(2,1)S(1)}, bf16[16,16,192]{2,1,0:T(8,128)(2,1)S(1)}, u32[]{:S(2)}, u32[]{:S(2)}) collective-permute-start(bf16[16,16,192]{2,1,0:T(8,128)(2,1)S(1)} %convert_element_type.77.own_ref), channel_id=1, source_target_pairs={{0,8},{8,16},{16,24},{24,32},{32,40},{40,48},{48,56},{56,64},{64,7... | collective-permute-start | bytes 294920 | tf_op jit(solution)/shard_map/ppermute | solution.py:150
  4.9 8.2 %collective-permute-start.1 = (bf16[16,16,192]{2,1,0:T(8,128)(2,1)S(1)}, bf16[16,16,192]{2,1,0:T(8,128)(2,1)S(1)}, u32[]{:S(2)}, u32[]{:S(2)}) collective-permute-start(bf16[16,16,192]{2,1,0:T(8,128)(2,1)S(1)} %convert_element_type.77.own_ref), channel_id=1, source_target_pairs={{8,0},{16,8},{24,16},{32,24},{40,32},{48,40},{56,48},{64,56},{72,6... | collective-permute-start | bytes 294920 | tf_op jit(solution)/shard_map/ppermute | solution.py:150
  12.2 0.7 copy-start.8
  13.1 0.7 copy-start.10
  13.8 1.9 copy-start
  15.7 0.9 copy-start.9
  16.6 0.9 copy-start.11
  17.5 44.3 %copy-start.1 = (bf16[16,2,192,192]{3,2,1,0:T(8,128)(2,1)S(1)}, bf16[16,2,192,192]{3,2,1,0:T(8,128)(2,1)}, u32[]{:S(2)}) copy-start(bf16[16,2,192,192]{3,2,1,0:T(8,128)(2,1)} %a_ref.9) | copy-start | bytes 7077892
  19.7 14.9 %collective-permute-start.2 = (bf16[16,16,192]{2,1,0:T(8,128)(2,1)}, bf16[16,16,192]{2,1,0:T(8,128)(2,1)S(1)}, u32[]{:S(2)}, u32[]{:S(2)}) collective-permute-start(bf16[16,16,192]{2,1,0:T(8,128)(2,1)} %couple.3), channel_id=1, source_target_pairs={{0,2},{1,7},{2,0},{3,5},{4,6},{5,3},{6,4},{7,1},{8,10},{9,15},{10,... | collective-permute-start | bytes 294920 | tf_op jit(solution)/shard_map/ppermute | solution.py:159
  36.2 13.1 %collective-permute-start.3 = (bf16[16,16,192]{2,1,0:T(8,128)(2,1)}, bf16[16,16,192]{2,1,0:T(8,128)(2,1)}, u32[]{:S(2)}, u32[]{:S(2)}) collective-permute-start(bf16[16,16,192]{2,1,0:T(8,128)(2,1)} %add_convert_fusion.2), channel_id=1, source_target_pairs={{0,6},{1,3},{2,4},{3,1},{4,2},{5,7},{6,0},{7,5},{8,14},{9,11},{10,... | collective-permute-start | bytes 294920 | tf_op jit(solution)/shard_map/ppermute | solution.py:159
  40.9 1.4 copy-start.2
  50.3 9.9 %collective-permute-start.4 = (bf16[16,16,192]{2,1,0:T(8,128)(2,1)S(1)}, bf16[16,16,192]{2,1,0:T(8,128)(2,1)S(1)}, u32[]{:S(2)}, u32[]{:S(2)}) collective-permute-start(bf16[16,16,192]{2,1,0:T(8,128)(2,1)S(1)} %get-tuple-element.14.own_ref), channel_id=1, source_target_pairs={{0,8},{8,16},{16,24},{24,32},{32,40},{40,48},{48,56},{56,64},{64,7... | collective-permute-start | bytes 294920 | tf_op jit(solution)/shard_map/ppermute | solution.py:150
  52.3 9.5 %collective-permute-start.5 = (bf16[16,16,192]{2,1,0:T(8,128)(2,1)S(1)}, bf16[16,16,192]{2,1,0:T(8,128)(2,1)S(1)}, u32[]{:S(2)}, u32[]{:S(2)}) collective-permute-start(bf16[16,16,192]{2,1,0:T(8,128)(2,1)S(1)} %get-tuple-element.14.own_ref), channel_id=1, source_target_pairs={{8,0},{16,8},{24,16},{32,24},{40,32},{48,40},{56,48},{64,56},{72,6... | collective-permute-start | bytes 294920 | tf_op jit(solution)/shard_map/ppermute | solution.py:150
  59.9 36.3 %copy-start.13 = (s32[16,3]{0,1:T(4,128)S(1)}, s32[16,3]{0,1:T(4,128)}, u32[]{:S(2)}) copy-start(s32[16,3]{0,1:T(4,128)} %param.10) | copy-start | bytes 580
  63.4 9.7 %collective-permute-start.6 = (bf16[16,16,192]{2,1,0:T(8,128)(2,1)S(1)}, bf16[16,16,192]{2,1,0:T(8,128)(2,1)S(1)}, u32[]{:S(2)}, u32[]{:S(2)}) collective-permute-start(bf16[16,16,192]{2,1,0:T(8,128)(2,1)S(1)} %couple.4), channel_id=1, source_target_pairs={{0,2},{1,7},{2,0},{3,5},{4,6},{5,3},{6,4},{7,1},{8,10},{9,15},{10,... | collective-permute-start | bytes 294920 | tf_op jit(solution)/shard_map/ppermute | solution.py:159
  73.8 9.9 %collective-permute-start.7 = (bf16[16,16,192]{2,1,0:T(8,128)(2,1)}, bf16[16,16,192]{2,1,0:T(8,128)(2,1)}, u32[]{:S(2)}, u32[]{:S(2)}) collective-permute-start(bf16[16,16,192]{2,1,0:T(8,128)(2,1)} %add_convert_fusion.1), channel_id=1, source_target_pairs={{0,6},{1,3},{2,4},{3,1},{4,2},{5,7},{6,0},{7,5},{8,14},{9,11},{10,... | collective-permute-start | bytes 294920 | tf_op jit(solution)/shard_map/ppermute | solution.py:159
  81.0 1.4 copy-start.3
  84.7 13.1 %collective-permute-start.8 = (bf16[16,16,192]{2,1,0:T(8,128)(2,1)S(1)}, bf16[16,16,192]{2,1,0:T(8,128)(2,1)S(1)}, u32[]{:S(2)}, u32[]{:S(2)}) collective-permute-start(bf16[16,16,192]{2,1,0:T(8,128)(2,1)S(1)} %get-tuple-element.12.own_ref), channel_id=1, source_target_pairs={{0,8},{8,16},{16,24},{24,32},{32,40},{40,48},{48,56},{56,64},{64,7... | collective-permute-start | bytes 294920 | tf_op jit(solution)/shard_map/ppermute | solution.py:150
  86.6 11.5 %collective-permute-start.9 = (bf16[16,16,192]{2,1,0:T(8,128)(2,1)S(1)}, bf16[16,16,192]{2,1,0:T(8,128)(2,1)S(1)}, u32[]{:S(2)}, u32[]{:S(2)}) collective-permute-start(bf16[16,16,192]{2,1,0:T(8,128)(2,1)S(1)} %get-tuple-element.12.own_ref), channel_id=1, source_target_pairs={{8,0},{16,8},{24,16},{32,24},{40,32},{48,40},{56,48},{64,56},{72,6... | collective-permute-start | bytes 294920 | tf_op jit(solution)/shard_map/ppermute | solution.py:150
  99.7 10.2 %collective-permute-start.10 = (bf16[16,16,192]{2,1,0:T(8,128)(2,1)S(1)}, bf16[16,16,192]{2,1,0:T(8,128)(2,1)S(1)}, u32[]{:S(2)}, u32[]{:S(2)}) collective-permute-start(bf16[16,16,192]{2,1,0:T(8,128)(2,1)S(1)} %couple.5), channel_id=1, source_target_pairs={{0,2},{1,7},{2,0},{3,5},{4,6},{5,3},{6,4},{7,1},{8,10},{9,15},{10,... | collective-permute-start | bytes 294920 | tf_op jit(solution)/shard_map/ppermute | solution.py:159
  110.6 12.0 %collective-permute-start.11 = (bf16[16,16,192]{2,1,0:T(8,128)(2,1)}, bf16[16,16,192]{2,1,0:T(8,128)(2,1)}, u32[]{:S(2)}, u32[]{:S(2)}) collective-permute-start(bf16[16,16,192]{2,1,0:T(8,128)(2,1)} %add_convert_fusion), channel_id=1, source_target_pairs={{0,6},{1,3},{2,4},{3,1},{4,2},{5,7},{6,0},{7,5},{8,14},{9,11},{10,... | collective-permute-start | bytes 294920 | tf_op jit(solution)/shard_map/ppermute | solution.py:159
  116.4 1.4 copy-start.4
  140.9 25.5 %copy-start.5 = (bf16[16,192,192]{2,1,0:T(8,128)(2,1)S(1)}, bf16[16,192,192]{2,1,0:T(8,128)(2,1)}, u32[]{:S(2)}) copy-start(bf16[16,192,192]{2,1,0:T(8,128)(2,1)} %diag_ref.9) | copy-start | bytes 3538948
  143.6 14.8 %collective-permute-start.13 = (bf16[16,2,16,192]{3,2,1,0:T(8,128)(2,1)S(1)}, bf16[16,2,16,192]{3,2,1,0:T(8,128)(2,1)S(1)}, u32[]{:S(2)}, u32[]{:S(2)}) collective-permute-start(bf16[16,2,16,192]{3,2,1,0:T(8,128)(2,1)S(1)} %fit.1.near_ref), channel_id=1, source_target_pairs={{0,2},{1,7},{2,0},{3,5},{4,6},{5,3},{6,4},{7,1},{8,10},{9,15},{10,... | collective-permute-start | bytes 589832 | tf_op jit(solution)/shard_map/ppermute | solution.py:159
  150.0 8.4 %collective-permute-start.12 = (s32[16,2]{1,0:T(8,128)S(1)}, s32[16,2]{1,0:T(8,128)S(1)}, u32[]{:S(2)}, u32[]{:S(2)}) collective-permute-start(s32[16,2]{1,0:T(8,128)S(1)} %broadcast_add_fusion.slot_ref), channel_id=1, source_target_pairs={{0,2},{1,7},{2,0},{3,5},{4,6},{5,3},{6,4},{7,1},{8,10},{9,15},{10,... | collective-permute-start | bytes 392 | tf_op jit(solution)/shard_map/ppermute | solution.py:159
  159.6 16.2 %collective-permute-start.14 = (bf16[16,4,16,192]{3,2,1,0:T(8,128)(2,1)S(1)}, bf16[16,4,16,192]{3,2,1,0:T(8,128)(2,1)S(1)}, u32[]{:S(2)}, u32[]{:S(2)}) collective-permute-start(bf16[16,4,16,192]{3,2,1,0:T(8,128)(2,1)S(1)} %slots.1), channel_id=1, source_target_pairs={{0,6},{1,3},{2,4},{3,1},{4,2},{5,7},{6,0},{7,5},{8,14},{9,11},{10,... | collective-permute-start | bytes 1179656 | tf_op jit(solution)/shard_map/ppermute | solution.py:159
  176.8 45.3 %collective-permute-start.17 = (bf16[16,4,16,192]{3,2,1,0:T(8,128)(2,1)}, bf16[16,4,16,192]{3,2,1,0:T(8,128)(2,1)}, u32[]{:S(2)}, u32[]{:S(2)}) collective-permute-start(bf16[16,4,16,192]{3,2,1,0:T(8,128)(2,1)} %subtract_convert_fusion.own_ref), channel_id=1, source_target_pairs={{0,8},{8,16},{16,24},{24,32},{32,40},{40,48},{48,56},{56,64},{64,7... | collective-permute-start | bytes 1179656 | tf_op jit(solution)/shard_map/ppermute | solution.py:150
  193.4 28.8 %collective-permute-start.18 = (bf16[16,4,16,192]{3,2,1,0:T(8,128)(2,1)}, bf16[16,4,16,192]{3,2,1,0:T(8,128)(2,1)}, u32[]{:S(2)}, u32[]{:S(2)}) collective-permute-start(bf16[16,4,16,192]{3,2,1,0:T(8,128)(2,1)} %subtract_convert_fusion.own_ref), channel_id=1, source_target_pairs={{8,0},{16,8},{24,16},{32,24},{40,32},{48,40},{56,48},{64,56},{72,6... | collective-permute-start | bytes 1179656 | tf_op jit(solution)/shard_map/ppermute | solution.py:150
  195.3 26.9 %collective-permute-start.19 = (bf16[16,4,16,192]{3,2,1,0:T(8,128)(2,1)}, bf16[16,4,16,192]{3,2,1,0:T(8,128)(2,1)}, u32[]{:S(2)}, u32[]{:S(2)}) collective-permute-start(bf16[16,4,16,192]{3,2,1,0:T(8,128)(2,1)} %subtract_convert_fusion.own_ref), channel_id=1, source_target_pairs={{0,1},{1,0},{2,3},{3,2},{4,5},{5,4},{6,7},{7,6},{8,9},{9,8},{10,11... | collective-permute-start | bytes 1179656 | tf_op jit(solution)/shard_map/ppermute | solution.py:272
  211.3 5.4 %collective-permute-start.16 = (s32[16,4]{0,1:T(4,128)S(1)}, s32[16,4]{0,1:T(4,128)S(1)}, u32[]{:S(2)}, u32[]{:S(2)}) collective-permute-start(s32[16,4]{0,1:T(4,128)S(1)} %get-tuple-element.11), channel_id=1, source_target_pairs={{8,0},{16,8},{24,16},{32,24},{40,32},{48,40},{56,48},{64,56},{72,6... | collective-permute-start | bytes 776 | tf_op jit(solution)/shard_map/ppermute | solution.py:150
  213.2 8.8 %collective-permute-start.15 = (s32[16,4]{0,1:T(4,128)S(1)}, s32[16,4]{0,1:T(4,128)S(1)}, u32[]{:S(2)}, u32[]{:S(2)}) collective-permute-start(s32[16,4]{0,1:T(4,128)S(1)} %get-tuple-element.11), channel_id=1, source_target_pairs={{0,8},{8,16},{16,24},{24,32},{32,40},{40,48},{48,56},{56,64},{64,7... | collective-permute-start | bytes 776 | tf_op jit(solution)/shard_map/ppermute | solution.py:150
  222.2 1.4 copy-start.6
  227.7 9.3 %collective-permute-start.20 = (bf16[2,96,256]{2,1,0:T(8,128)(2,1)S(1)}, bf16[2,96,256]{2,1,0:T(8,128)(2,1)S(1)}, u32[]{:S(2)}, u32[]{:S(2)}) collective-permute-start(bf16[2,96,256]{2,1,0:T(8,128)(2,1)S(1)} %get-tuple-element.9), channel_id=1, source_target_pairs={{0,2},{1,7},{2,0},{3,5},{4,6},{5,3},{6,4},{7,1},{8,10},{9,15},{10,... | collective-permute-start | bytes 294920 | tf_op jit(solution)/shard_map/ppermute | solution.py:159
  237.1 10.2 %collective-permute-start.21 = (bf16[96,256]{1,0:T(8,128)(2,1)S(1)}, bf16[96,256]{1,0:T(8,128)(2,1)S(1)}, u32[]{:S(2)}, u32[]{:S(2)}) collective-permute-start(bf16[96,256]{1,0:T(8,128)(2,1)S(1)} %fusion.6), channel_id=1, source_target_pairs={{0,6},{1,3},{2,4},{3,1},{4,2},{5,7},{6,0},{7,5},{8,14},{9,11},{10,... | collective-permute-start | bytes 147464 | tf_op jit(solution)/shard_map/ppermute | solution.py:159
  249.6 6.7 %collective-permute-start.22 = (f32[6,16,8,16]{1,3,0,2:T(8,128)S(1)}, f32[6,16,8,16]{1,3,0,2:T(8,128)S(1)}, u32[]{:S(2)}, u32[]{:S(2)}) collective-permute-start(f32[6,16,8,16]{1,3,0,2:T(8,128)S(1)} %bitcast.27), channel_id=1, source_target_pairs={{0,1},{1,0},{2,3},{3,2},{4,5},{5,4},{6,7},{7,6},{8,9},{9,8},{10,11... | collective-permute-start | bytes 147464 | tf_op jit(solution)/shard_map/ppermute | solution.py:301

commit v2 on v1

v2 whole, which is shorter than its diff:
```python
import jax
import jax.numpy as jnp
from jax import lax
from jax.experimental import pallas as pl
from jax.experimental.pallas import tpu as pltpu
from jax.sharding import PartitionSpec as P

VECTORS = 32
SWEEPS = 3
SLAB_AGGS = 8
SLOTS = 4
DAMPING = 2.0 / 3.0
HIGHEST_PRECISION = lax.Precision.HIGHEST
BF16 = jnp.bfloat16
F32 = jnp.float32

SMEM_SPEC = pl.BlockSpec(memory_space=pltpu.SMEM)
VMEM_SPEC = pl.BlockSpec(memory_space=pltpu.VMEM)


def dot_nt(left, right):
    return lax.dot_general(left, right, (((1,), (1,)), ((), ())), preferred_element_type=F32)


def center_kernel(diag_ref, x_ref, scale_ref, y_ref):
    for i in range(x_ref.shape[0]):
        x = x_ref[i]
        y_ref[i] = x - scale_ref[i : i + 1, :] * dot_nt(x.astype(BF16), diag_ref[i])


def first_center_kernel(diag_ref, x_ref, y_ref, scale_ref):
    width = x_ref.shape[2]
    on_diagonal = lax.broadcasted_iota(jnp.int32, (width, width), 0) == lax.broadcasted_iota(
        jnp.int32, (width, width), 1
    )
    for i in range(x_ref.shape[0]):
        x = x_ref[i]
        block = diag_ref[i]
        pivot = jnp.sum(jnp.where(on_diagonal, block.astype(F32), 0.0), axis=0, keepdims=True)
        scale = DAMPING / pivot
        scale_ref[i : i + 1, :] = scale
        y_ref[i] = x - scale * dot_nt(x.astype(BF16), block)


def fold_kernel(x_ref, out_ref):
    rows, _, width = x_ref.shape
    for m in range(rows // 2):
        out_ref[m, :, :width] = x_ref[m].astype(BF16)
        out_ref[m, :, width:] = x_ref[rows // 2 + m].astype(BF16)


def update_kernel(rest_ref, near_ref, far_ref, scale_ref, *refs):
    rows, _, width = rest_ref.shape
    half = rows // 2
    extra_ref = refs[0] if len(refs) == 3 else None
    x_ref, folded_ref = refs[-2:]
    for m in range(half):
        total = near_ref[m].astype(F32) + far_ref[m].astype(F32)
        low = rest_ref[m] - scale_ref[m : m + 1, :] * total[:, :width]
        high = rest_ref[half + m] - scale_ref[half + m : half + m + 1, :] * total[:, width:]
        x_ref[m] = low
        x_ref[half + m] = high
        folded_ref[m, :, :width] = low.astype(BF16)
        folded_ref[m, :, width:] = high.astype(BF16)
    if extra_ref is not None:
        folded_ref[half] = extra_ref[...]


def couple_kernel(col_ref, a_ref, before_ref, own_ref, after_ref, *refs):
    rows, stored, width = a_ref.shape[:3]
    half = rows // 2
    extra_ref = refs[0] if len(refs) == 3 else None
    out_ref, ext = refs[-2:]
    for s, ref in enumerate((before_ref, own_ref, after_ref)):
        for m in range(half):
            block = ref[m]
            ext[s * rows + m] = block[:, :width]
            ext[s * rows + half + m] = block[:, width:]

    def product(i):
        total = dot_nt(ext[col_ref[i, 0]], a_ref[i, 0])
        for k in range(1, stored):
            total = total + dot_nt(ext[col_ref[i, k]], a_ref[i, k])
        return total.astype(BF16)

    for m in range(half):
        out_ref[m, :, :width] = product(m)
        out_ref[m, :, width:] = product(half + m)
    if extra_ref is not None:
        out_ref[half] = extra_ref[...]


def fit_kernel(col_ref, a_ref, own_ref, out_ref):
    rows, stored, width = a_ref.shape[:3]
    for i in range(rows):
        for k in range(stored):
            row = jnp.clip(col_ref[i, k] - rows, 0, rows - 1)
            out_ref[i, :, k * width : (k + 1) * width] = dot_nt(own_ref[row], a_ref[i, k]).astype(
                BF16
            )


def slot_kernel(slot_ref, far_slot_ref, near_ref, far_ref, out_ref):
    rows, vectors, wide = near_ref.shape
    stored = slot_ref.shape[1]
    width = wide // stored
    for i in range(rows):
        near = near_ref[i].astype(F32)
        far = far_ref[i].astype(F32)
        for p in range(SLOTS):
            total = jnp.zeros((vectors, width), F32)
            for k in range(stored):
                lanes = slice(k * width, (k + 1) * width)
                total = total + jnp.where(slot_ref[i, k] == p, near[:, lanes], 0.0)
                total = total + jnp.where(far_slot_ref[i, k] == p, far[:, lanes], 0.0)
            lanes = slice((p % 2) * width, (p % 2 + 1) * width)
            out_ref[i, p // 2, :, lanes] = total.astype(BF16)


def finish_kernel(where_ref, rest_ref, near_ref, far_ref, scale_ref, out_ref, here_ref):
    rows, _, width = rest_ref.shape
    slot = where_ref[1]
    for i in range(rows):
        scale = scale_ref[i : i + 1, :]
        here = jnp.zeros(rest_ref.shape[1:], F32)
        for h in range(SLOTS // 2):
            total = near_ref[i, h].astype(F32) + far_ref[i, h].astype(F32)
            for q in range(2):
                lanes = slice(q * width, (q + 1) * width)
                value = -scale * total[:, lanes]
                if h == 0 and q == 0:
                    value = rest_ref[i] + value
                out_ref[i, h, :, lanes] = value.astype(BF16)
                here = jnp.where(slot == 2 * h + q, value, here)
        here_ref[i, 0] = here.astype(BF16)


def inverse_factor_kernel(m_ref, out_ref):
    size = m_ref.shape[0]
    rows = [m_ref[v] for v in range(size)]
    place = lax.broadcasted_iota(jnp.int32, rows[0].shape, 0)
    for k in range(size):
        root = lax.rsqrt(rows[k][k : k + 1, :])
        here = place == k
        pivot_row = jnp.where(here, root, rows[k] * root)
        rows[k] = jnp.where(place <= k, pivot_row, 0.0)
        out_ref[k] = rows[k]
        for v in range(k + 1, size):
            rows[v] = jnp.where(here, 0.0, rows[v]) - pivot_row[v : v + 1, :] * pivot_row


def coarse_kernel(
    where_ref, col_ref, place_ref, a_ref, diag_ref, before_ref, own_ref, after_ref, other_ref,
    keep_ref, send_ref, ext, reach, left, total,
):
    rows, stored, width = a_ref.shape[:3]
    vectors = own_ref.shape[2]
    share = rows // 4
    slot = where_ref[1]
    span = reach.shape[1]
    reach[...] = jnp.zeros_like(reach)
    left[...] = jnp.zeros_like(left)

    for s, ref in enumerate((before_ref, own_ref, after_ref)):
        for i in range(rows):
            for h in range(SLOTS // 2):
                block = ref[i, h]
                ext[s * rows + i, 2 * h] = block[:, :width]
                ext[s * rows + i, 2 * h + 1] = block[:, width:]

    def add(i, row, block):
        image = dot_nt(ext[row].reshape(SLOTS * vectors, width), block)
        for q in range(SLOTS):
            at = place_ref[row, q]
            reach[i, at] = reach[i, at] + image[q * vectors : (q + 1) * vectors]

    for i in range(rows):
        for h in range(SLOTS // 2):
            other = other_ref[i, h]
            for q in range(2):
                group = place_ref[rows + i, 2 * h + q] - SLAB_AGGS
                left[i, 0, group] = ext[rows + i, 2 * h + q]
                left[i, 1, group] = other[:, q * width : (q + 1) * width]
        for k in range(stored):
            add(i, col_ref[i, k], a_ref[i, k])

    for r in range(share):
        i = slot * share + r
        add(i, rows + i, diag_ref[i])

    for i in range(rows):
        product = dot_nt(
            reach[i].astype(BF16).reshape(span * vectors, width),
            left[i].reshape(2 * SLAB_AGGS * vectors, width),
        )
        if i == 0:
            total[...] = product
        else:
            total[...] = total[...] + product
    quarter = span * vectors // 4
    for n in range(2):
        start = pl.multiple_of(where_ref[2 + n] * quarter, 32)
        keep_ref[n] = total[pl.ds(start, quarter), :] * (1.0 / width)
        start = pl.multiple_of(where_ref[4 + n] * quarter, 32)
        send_ref[n] = (total[pl.ds(start, quarter), :] * (1.0 / width)).astype(BF16)


def shift(x, by):
    size = lax.axis_size("rows")
    return lax.ppermute(x, "rows", [(i, i + by) for i in range(size) if 0 <= i + by < size])


def partner(slot, core, phase):
    return slot ^ 1 if (core + phase) % 2 == 0 else 3 - slot


def exchange(x, phase):
    pairs = [(2 * s + c, 2 * partner(s, c, phase) + c) for s in range(4) for c in range(2)]
    return lax.ppermute(x, ("aggs", "vecs"), pairs)


def kernel_call(body, name, shapes, operands, scratch=(), limit=12):
    several = isinstance(shapes, list)
    specs = [
        SMEM_SPEC if x.dtype == jnp.int32 else VMEM_SPEC for x in operands
    ]
    return pl.pallas_call(
        body,
        out_shape=shapes,
        in_specs=specs,
        out_specs=[VMEM_SPEC] * len(shapes) if several else VMEM_SPEC,
        scratch_shapes=list(scratch),
        compiler_params=pltpu.CompilerParams(vmem_limit_bytes=limit * 1024 * 1024),
        name=name,
    )(*operands)


def as_block(values, shape):
    padding = [(0, n - m) for n, m in zip(shape, values.shape)]
    return jnp.pad(values, padding).astype(BF16)


def from_block(block, columns):
    return block[:, :columns].astype(F32).astype(jnp.int32)


def on_device(couplings, diag_blocks, coupling_cols, aggregate, pattern, tests):
    rows, vectors, width = tests.shape
    stored = couplings.shape[1]
    half = rows // 2
    slab = lax.axis_index("rows")
    slot = lax.axis_index("aggs")
    core = lax.axis_index("vecs")
    whole_shape = jax.ShapeDtypeStruct((rows, vectors, width), F32)
    extra_shape = (vectors, 2 * width)

    def folded(blocks):
        return jax.ShapeDtypeStruct((blocks, vectors, 2 * width), BF16)

    cols = coupling_cols - slab * rows + rows
    local_aggs = aggregate - slab * SLAB_AGGS
    slot_aggs = jnp.concatenate([aggregate[:, None], pattern], axis=1) - slab * SLAB_AGGS
    inside = cols[:, :, None] == jnp.arange(rows, 2 * rows, dtype=jnp.int32)
    column_aggs = jnp.sum(jnp.where(inside, local_aggs + 1, 0), axis=2) - 1
    hits = column_aggs[:, :, None] == slot_aggs[:, None, :]
    near_slot = jnp.sum(jnp.where(hits, jnp.arange(1, SLOTS + 1, dtype=jnp.int32), 0), axis=2) - 1
    ids_block = as_block(slot_aggs, extra_shape)
    slot_block = as_block(near_slot, extra_shape)
    first = jnp.where(core == 0, slot ^ 1, 3 - slot)
    second = jnp.where(core == 0, 3 - slot, slot ^ 1)
    where = jnp.stack([core, slot, slot, second, first, slot ^ 2]).astype(jnp.int32)

    rounded = kernel_call(fold_kernel, "fold", folded(half), [tests])
    current, scale, places, far_slot = tests, None, None, None
    for sweep in range(SWEEPS):
        before = shift(rounded, 1)
        after = shift(rounded, -1)
        if sweep == 0:
            rest, scale = kernel_call(
                first_center_kernel,
                "first_center",
                [whole_shape, jax.ShapeDtypeStruct((rows, width), F32)],
                [diag_blocks, current],
            )
        else:
            rest = kernel_call(center_kernel, "center", whole_shape, [diag_blocks, current, scale])
        if sweep == 1:
            places = jnp.concatenate(
                [
                    from_block(before[half], SLOTS),
                    slot_aggs + SLAB_AGGS,
                    from_block(after[half], SLOTS) + 2 * SLAB_AGGS,
                ],
                axis=0,
            )
        last = sweep == SWEEPS - 1
        part = kernel_call(
            couple_kernel,
            "couple",
            folded(half + last),
            [cols, couplings, before, rounded, after] + [slot_block] * last,
            [pltpu.VMEM((3 * rows, vectors, width), BF16)],
        )
        far = exchange(part, 0)
        if last:
            far_slot = from_block(far[half], stored)
            part, far = part[:half], far[:half]
        pair = (part.astype(F32) + far.astype(F32)).astype(BF16)
        far = exchange(pair, 1)
        current, rounded = kernel_call(
            update_kernel,
            "update",
            [whole_shape, folded(half + (sweep == 0))],
            [rest, pair, far, scale] + [ids_block] * (sweep == 0),
        )

    every = lax.all_gather(current, "vecs", axis=1, tiled=True)
    grams = jnp.einsum("ivb,iwb->ivw", every, every, precision=HIGHEST_PRECISION)
    members = (local_aggs[:, None] == jnp.arange(SLAB_AGGS, dtype=jnp.int32)[None, :]).astype(F32)
    totals = jnp.einsum("ig,ivw->vwg", members, grams, precision=HIGHEST_PRECISION) / width
    inverse = kernel_call(
        inverse_factor_kernel,
        "inverse_factor",
        jax.ShapeDtypeStruct((VECTORS, VECTORS, SLAB_AGGS), F32),
        [totals],
    )
    own_inverse = lax.dynamic_slice_in_dim(inverse, core * vectors, vectors, 0)
    row_inverse = jnp.einsum("ig,cvg->icv", members, own_inverse, precision=HIGHEST_PRECISION)
    tentative = jnp.einsum("icv,ivb->icb", row_inverse, every, precision=HIGHEST_PRECISION)

    moved = kernel_call(
        fit_kernel, "fit", folded(rows), [cols, couplings, tentative.astype(BF16)]
    )
    rest = kernel_call(center_kernel, "center", whole_shape, [diag_blocks, tentative, scale])
    slots_shape = jax.ShapeDtypeStruct((rows, SLOTS // 2, vectors, 2 * width), BF16)
    pair = kernel_call(
        slot_kernel, "slots", slots_shape, [near_slot, far_slot, moved, exchange(moved, 0)]
    )
    prolong, prolong_here = kernel_call(
        finish_kernel,
        "finish",
        [slots_shape, jax.ShapeDtypeStruct((rows, 1, vectors, width), BF16)],
        [where, rest, pair, exchange(pair, 1), scale],
    )

    before = shift(prolong, 1)
    after = shift(prolong, -1)
    other = lax.ppermute(prolong, "vecs", [(0, 1), (1, 0)])
    span = 3 * SLAB_AGGS
    quarter = span * vectors // 4
    wide = SLAB_AGGS * 2 * vectors
    keep, send = kernel_call(
        coarse_kernel,
        "coarse",
        [
            jax.ShapeDtypeStruct((2, quarter, wide), F32),
            jax.ShapeDtypeStruct((2, quarter, wide), BF16),
        ],
        [where, cols, places, couplings, diag_blocks, before, prolong, after, other],
        [
            pltpu.VMEM((3 * rows, SLOTS, vectors, width), BF16),
            pltpu.VMEM((rows, span, vectors, width), F32),
            pltpu.VMEM((rows, 2, SLAB_AGGS, vectors, width), BF16),
            pltpu.VMEM((span * vectors, wide), F32),
        ],
        limit=28,
    )
    merged = keep + exchange(send, 0).astype(F32)
    owned = merged[0] + exchange(merged[1].astype(BF16), 1).astype(F32)
    mine, theirs = owned[:, : wide // 2], owned[:, wide // 2 :]
    theirs = lax.ppermute(theirs, "vecs", [(0, 1), (1, 0)])
    low = jnp.where(core == 0, mine, theirs).reshape(span // 4, vectors, -1)
    high = jnp.where(core == 0, theirs, mine).reshape(span // 4, vectors, -1)
    coarse = jnp.concatenate([low, high], axis=1).reshape(span // 4, VECTORS, SLAB_AGGS, vectors)
    return (prolong_here, coarse.transpose(2, 0, 3, 1))


def solution(mesh):
    return jax.shard_map(
        on_device,
        mesh=mesh,
        in_specs=(
            P("rows", "aggs", None, None),
            P("rows", None, None),
            P("rows", "aggs"),
            P("rows"),
            P("rows", None),
            P("rows", "vecs", None),
        ),
        out_specs=(P("rows", "aggs", "vecs", None), P("rows", "aggs", "vecs", None)),
        check_vma=False,
    )
```

time: 258 us -> 243 us (0.942)
  the two profiles are of different devices: /device:TPU:65 before, /device:TPU:33 now
where the time goes in v2:
time: 243 us; the launch traced here: 241 us
  starting transfers between devices  101 us (42%)
  waiting for transfers between devices  75.5 us (31%)
  Pallas kernels  20.8 us (9%)
  local copies, waits for them, and re-layouts  20.7 us (9%)
  blocking collectives  13.8 us (6%)
  other arithmetic  6.29 us (3%)
    ppermute x10, starting transfers between devices, exchange(): return lax.ppermute(x, ('aggs', 'vecs'), pairs)  63.8 us
    ppermute x10, waiting for transfers between devices, exchange(): return lax.ppermute(x, ('aggs', 'vecs'), pairs)  43.7 us
    ppermute x8, waiting for transfers between devices, shift(): lax.ppermute(x, 'rows', [(i, i + by) for i in range(size) if 0 <= i + by...  31 us
    ppermute x8, starting transfers between devices, shift(): lax.ppermute(x, 'rows', [(i, i + by) for i in range(size) if 0 <= i + by...  30.2 us
    pallas_call x16, Pallas kernels, kernel_call(): pl.pallas_call(body, out_shape=shapes, in_specs=specs, out_specs=[VMEM_SP...  20.8 us
    unnamed x48, local copies, waits for them, and re-layouts  18.1 us
    all_gather x1, blocking collectives, on_device(): every = lax.all_gather(current, 'vecs', axis=1, tiled=True)  13.8 us
    ppermute x1, starting transfers between devices, on_device(): theirs = lax.ppermute(theirs, 'vecs', [(0, 1), (1, 0)])  5.05 us
  transfers between devices with their start and end apart: 20, of which 16 were waited for; matrix products, arithmetic and copies ran while one was open for 2% of the time, Pallas kernels for 1%

profile of v2, /device:TPU:33, one launch (start us, length us, event | category | flops | bytes accessed | tf_op | source)
XLA Modules:
  0.0 241.5 jit_solution(18065469854197458268)
XLA Ops:
  0.6 0.9 copy-done.6
  1.7 6.4 %collective-permute-start.1 = (bf16[8,16,384]{2,1,0:T(8,128)(2,1)S(1)}, bf16[8,16,384]{2,1,0:T(8,128)(2,1)S(1)}, u32[]{:S(2)}, u32[]{:S(2)}) collective-permute-start(bf16[8,16,384]{2,1,0:T(8,128)(2,1)S(1)} %fold.1.own_ref), channel_id=1, source_target_pairs={{8,0},{16,8},{24,16},{32,24},{40,32},{48,40},{56,48},{64,56},{72,6... | collective-permute-start | bytes 294920 | tf_op jit(solution)/shard_map/ppermute | solution.py:210
  8.1 1.9 collective-permute-start
  10.0 0.7 pad_add_fusion.1
  12.8 4.9 %collective-permute-done.before_ref = bf16[8,16,384]{2,1,0:T(8,128)(2,1)S(1)} collective-permute-done((bf16[8,16,384]{2,1,0:T(8,128)(2,1)S(1)}, bf16[8,16,384]{2,1,0:T(8,128)(2,1)S(1)}, u32[]{:S(2)}, u32[]{:S(2)}) %collective-permute-start) | collective-permute-done | bytes 98336 | tf_op jit(solution)/shard_map/ppermute | solution.py:210
  18.3 1.9 copy-done
  20.2 0.9 copy-done.17
  21.1 0.9 copy-done.19
  22.0 2.4 %couple.3 = bf16[8,16,384]{2,1,0:T(8,128)(2,1)} custom-call(s32[16,2]{1,0:T(8,128)S(1)} %broadcast_add_fusion.2.col_ref, bf16[16,2,192,192]{3,2,1,0:T(8,128)(2,1)S(1)} %copy-done, bf16[8,16,384]{2,1,0:T(8,128)(2,1)S(1)} %copy-done.19, bf16[8,16,384]{2,1,0:T(8,128)(2,1)S(1)} %fold.1.own_ref, bf16[8,16,384]{2,1,0:T(8,128)(2,1)S(1)} %copy-done.17), custom_call_target="tpu_custom_call" | custom-call | tf_op jit(solution)/shard_map/couple/pallas_call | solution.py:227
  24.4 12.4 %collective-permute-start.2 = (bf16[8,16,384]{2,1,0:T(8,128)(2,1)}, bf16[8,16,384]{2,1,0:T(8,128)(2,1)S(1)}, u32[]{:S(2)}, u32[]{:S(2)}) collective-permute-start(bf16[8,16,384]{2,1,0:T(8,128)(2,1)} %couple.3), channel_id=1, source_target_pairs={{0,2},{1,7},{2,0},{3,5},{4,6},{5,3},{6,4},{7,1},{8,10},{9,15},{10,... | collective-permute-start | bytes 294920 | tf_op jit(solution)/shard_map/ppermute | solution.py:219
  37.5 1.4 copy-done.2
  39.4 2.5 %collective-permute-done.2 = bf16[8,16,384]{2,1,0:T(8,128)(2,1)S(1)} collective-permute-done((bf16[8,16,384]{2,1,0:T(8,128)(2,1)}, bf16[8,16,384]{2,1,0:T(8,128)(2,1)S(1)}, u32[]{:S(2)}, u32[]{:S(2)}) %collective-permute-start.2) | collective-permute-done | bytes 98336 | tf_op jit(solution)/shard_map/ppermute | solution.py:219
  41.9 0.9 add_convert_fusion.2.near_ref
  42.8 4.7 %collective-permute-start.3 = (bf16[8,16,384]{2,1,0:T(8,128)(2,1)S(1)}, bf16[8,16,384]{2,1,0:T(8,128)(2,1)S(1)}, u32[]{:S(2)}, u32[]{:S(2)}) collective-permute-start(bf16[8,16,384]{2,1,0:T(8,128)(2,1)S(1)} %add_convert_fusion.2.near_ref), channel_id=1, source_target_pairs={{0,6},{1,3},{2,4},{3,1},{4,2},{5,7},{6,0},{7,5},{8,14},{9,11},{10,... | collective-permute-start | bytes 294920 | tf_op jit(solution)/shard_map/ppermute | solution.py:219
  47.6 0.8 select_reduce_fusion
  48.4 5.5 %collective-permute-done.3.far_ref = bf16[8,16,384]{2,1,0:T(8,128)(2,1)S(1)} collective-permute-done((bf16[8,16,384]{2,1,0:T(8,128)(2,1)S(1)}, bf16[8,16,384]{2,1,0:T(8,128)(2,1)S(1)}, u32[]{:S(2)}, u32[]{:S(2)}) %collective-permute-start.3) | collective-permute-done | bytes 98336 | tf_op jit(solution)/shard_map/ppermute | solution.py:219
  54.8 1.9 collective-permute-start.5
  56.7 3.4 %collective-permute-start.4 = (bf16[9,16,384]{2,1,0:T(8,128)(2,1)S(1)}, bf16[9,16,384]{2,1,0:T(8,128)(2,1)S(1)}, u32[]{:S(2)}, u32[]{:S(2)}) collective-permute-start(bf16[9,16,384]{2,1,0:T(8,128)(2,1)S(1)} %get-tuple-element.16.own_ref), channel_id=1, source_target_pairs={{0,8},{8,16},{16,24},{24,32},{32,40},{40,48},{48,56},{56,64},{64,7... | collective-permute-start | bytes 331784 | tf_op jit(solution)/shard_map/ppermute | solution.py:210
  60.8 5.6 %collective-permute-done.4.before_ref = bf16[9,16,384]{2,1,0:T(8,128)(2,1)S(1)} collective-permute-done((bf16[9,16,384]{2,1,0:T(8,128)(2,1)S(1)}, bf16[9,16,384]{2,1,0:T(8,128)(2,1)S(1)}, u32[]{:S(2)}, u32[]{:S(2)}) %collective-permute-start.4) | collective-permute-done | bytes 110624 | tf_op jit(solution)/shard_map/ppermute | solution.py:210
  67.1 0.9 copy-done.13
  68.0 0.9 copy-done.15
  68.9 1.8 couple.4
  70.7 6.3 %collective-permute-start.6 = (bf16[8,16,384]{2,1,0:T(8,128)(2,1)S(1)}, bf16[8,16,384]{2,1,0:T(8,128)(2,1)S(1)}, u32[]{:S(2)}, u32[]{:S(2)}) collective-permute-start(bf16[8,16,384]{2,1,0:T(8,128)(2,1)S(1)} %couple.4), channel_id=1, source_target_pairs={{0,2},{1,7},{2,0},{3,5},{4,6},{5,3},{6,4},{7,1},{8,10},{9,15},{10,... | collective-permute-start | bytes 294920 | tf_op jit(solution)/shard_map/ppermute | solution.py:219
  77.0 3.1 %collective-permute-done.6 = bf16[8,16,384]{2,1,0:T(8,128)(2,1)S(1)} collective-permute-done((bf16[8,16,384]{2,1,0:T(8,128)(2,1)S(1)}, bf16[8,16,384]{2,1,0:T(8,128)(2,1)S(1)}, u32[]{:S(2)}, u32[]{:S(2)}) %collective-permute-start.6) | collective-permute-done | bytes 98336 | tf_op jit(solution)/shard_map/ppermute | solution.py:219
  80.2 6.6 %collective-permute-start.7 = (bf16[8,16,384]{2,1,0:T(8,128)(2,1)S(1)}, bf16[8,16,384]{2,1,0:T(8,128)(2,1)S(1)}, u32[]{:S(2)}, u32[]{:S(2)}) collective-permute-start(bf16[8,16,384]{2,1,0:T(8,128)(2,1)S(1)} %add_convert_fusion.1.near_ref), channel_id=1, source_target_pairs={{0,6},{1,3},{2,4},{3,1},{4,2},{5,7},{6,0},{7,5},{8,14},{9,11},{10,... | collective-permute-start | bytes 294920 | tf_op jit(solution)/shard_map/ppermute | solution.py:219
  87.0 1.4 copy-done.3
  88.4 0.9 copy-done.11
  90.6 0.9 copy-done.21
  91.6 0.7 copy-done.8
  92.3 1.9 collective-permute-start.9
  94.2 3.4 %collective-permute-start.8 = (bf16[8,16,384]{2,1,0:T(8,128)(2,1)S(1)}, bf16[8,16,384]{2,1,0:T(8,128)(2,1)S(1)}, u32[]{:S(2)}, u32[]{:S(2)}) collective-permute-start(bf16[8,16,384]{2,1,0:T(8,128)(2,1)S(1)} %get-tuple-element.18.own_ref), channel_id=1, source_target_pairs={{0,8},{8,16},{16,24},{24,32},{32,40},{40,48},{48,56},{56,64},{64,7... | collective-permute-start | bytes 294920 | tf_op jit(solution)/shard_map/ppermute | solution.py:210
  98.0 5.9 %collective-permute-done.8.before_ref = bf16[8,16,384]{2,1,0:T(8,128)(2,1)S(1)} collective-permute-done((bf16[8,16,384]{2,1,0:T(8,128)(2,1)S(1)}, bf16[8,16,384]{2,1,0:T(8,128)(2,1)S(1)}, u32[]{:S(2)}, u32[]{:S(2)}) %collective-permute-start.8) | collective-permute-done | bytes 98336 | tf_op jit(solution)/shard_map/ppermute | solution.py:210
  103.8 1.8 couple.5
  105.6 7.1 %collective-permute-start.10 = (bf16[9,16,384]{2,1,0:T(8,128)(2,1)S(1)}, bf16[9,16,384]{2,1,0:T(8,128)(2,1)}, u32[]{:S(2)}, u32[]{:S(2)}) collective-permute-start(bf16[9,16,384]{2,1,0:T(8,128)(2,1)S(1)} %couple.5), channel_id=1, source_target_pairs={{0,2},{1,7},{2,0},{3,5},{4,6},{5,3},{6,4},{7,1},{8,10},{9,15},{10,... | collective-permute-start | bytes 331784 | tf_op jit(solution)/shard_map/ppermute | solution.py:219
  112.8 1.4 copy-done.4
  114.2 0.9 copy-done.9
  116.3 0.9 add_convert_fusion.near_ref
  117.2 6.0 %collective-permute-start.11 = (bf16[8,16,384]{2,1,0:T(8,128)(2,1)S(1)}, bf16[8,16,384]{2,1,0:T(8,128)(2,1)S(1)}, u32[]{:S(2)}, u32[]{:S(2)}) collective-permute-start(bf16[8,16,384]{2,1,0:T(8,128)(2,1)S(1)} %add_convert_fusion.near_ref), channel_id=1, source_target_pairs={{0,6},{1,3},{2,4},{3,1},{4,2},{5,7},{6,0},{7,5},{8,14},{9,11},{10,... | collective-permute-start | bytes 294920 | tf_op jit(solution)/shard_map/ppermute | solution.py:219
  123.2 0.7 slice_bitcast_fusion.3
  123.9 7.1 %collective-permute-done.11.far_ref = bf16[8,16,384]{2,1,0:T(8,128)(2,1)S(1)} collective-permute-done((bf16[8,16,384]{2,1,0:T(8,128)(2,1)S(1)}, bf16[8,16,384]{2,1,0:T(8,128)(2,1)S(1)}, u32[]{:S(2)}, u32[]{:S(2)}) %collective-permute-start.11) | collective-permute-done | bytes 98336 | tf_op jit(solution)/shard_map/ppermute | solution.py:219
  131.1 0.8 update.5
  131.9 13.8 %all_gather.3 = f32[16,32,192]{2,1,0:T(8,128)S(1)} all-gather(f32[16,16,192]{2,1,0:T(8,128)S(1)} %get-tuple-element.19), channel_id=1, replica_groups=mesh['rows'=64,'aggs'=4,'vecs'=2] {'vecs'}, dimensions={1}, use_global_device_ids=true | all-gather | bytes 589824 | tf_op jit(solution)/shard_map/all_gather | solution.py:317
  146.9 0.8 inverse_factor.1
  148.8 1.7 fit.1.near_ref
  150.5 3.2 %collective-permute-start.12 = (bf16[16,16,384]{2,1,0:T(8,128)(2,1)S(1)}, bf16[16,16,384]{2,1,0:T(8,128)(2,1)S(1)}, u32[]{:S(2)}, u32[]{:S(2)}) collective-permute-start(bf16[16,16,384]{2,1,0:T(8,128)(2,1)S(1)} %fit.1.near_ref), channel_id=1, source_target_pairs={{0,2},{1,7},{2,0},{3,5},{4,6},{5,3},{6,4},{7,1},{8,10},{9,15},{10,... | collective-permute-start | bytes 589832 | tf_op jit(solution)/shard_map/ppermute | solution.py:219
  153.7 10.9 %collective-permute-done.12.far_ref = bf16[16,16,384]{2,1,0:T(8,128)(2,1)S(1)} collective-permute-done((bf16[16,16,384]{2,1,0:T(8,128)(2,1)S(1)}, bf16[16,16,384]{2,1,0:T(8,128)(2,1)S(1)}, u32[]{:S(2)}, u32[]{:S(2)}) %collective-permute-start.12) | collective-permute-done | bytes 196640 | tf_op jit(solution)/shard_map/ppermute | solution.py:219
  164.6 2.8 %slots.1.near_ref = bf16[16,2,16,384]{3,2,1,0:T(8,128)(2,1)S(1)} custom-call(s32[16,2]{1,0:T(8,128)S(1)} %get-tuple-element.30.slot_ref, s32[16,2]{1,0:T(8,128)S(1)} %convert_convert_fusion.1.far_slot_ref, bf16[16,16,384]{2,1,0:T(8,128)(2,1)S(1)} %fit.1.near_ref, bf16[16,16,384]{2,1,0:T(8,128)(2,1)S(1)} %collective-permute-done.12.far_ref), custom_call_target="tpu_custom_call" | custom-call | tf_op jit(solution)/shard_map/slots/pallas_call | solution.py:227
  167.4 3.2 %collective-permute-start.13 = (bf16[16,2,16,384]{3,2,1,0:T(8,128)(2,1)S(1)}, bf16[16,2,16,384]{3,2,1,0:T(8,128)(2,1)S(1)}, u32[]{:S(2)}, u32[]{:S(2)}) collective-permute-start(bf16[16,2,16,384]{3,2,1,0:T(8,128)(2,1)S(1)} %slots.1.near_ref), channel_id=1, source_target_pairs={{0,6},{1,3},{2,4},{3,1},{4,2},{5,7},{6,0},{7,5},{8,14},{9,11},{10,... | collective-permute-start | bytes 1179656 | tf_op jit(solution)/shard_map/ppermute | solution.py:219
  170.6 0.7 slice_bitcast_fusion.2
  171.9 9.4 %collective-permute-done.13.far_ref = bf16[16,2,16,384]{3,2,1,0:T(8,128)(2,1)S(1)} collective-permute-done((bf16[16,2,16,384]{3,2,1,0:T(8,128)(2,1)S(1)}, bf16[16,2,16,384]{3,2,1,0:T(8,128)(2,1)S(1)}, u32[]{:S(2)}, u32[]{:S(2)}) %collective-permute-start.13) | collective-permute-done | bytes 393248 | tf_op jit(solution)/shard_map/ppermute | solution.py:219
  181.3 2.0 finish.1
  183.3 1.9 collective-permute-start.16
  185.2 9.3 %collective-permute-start.15 = (bf16[16,2,16,384]{3,2,1,0:T(8,128)(2,1)S(1)}, bf16[16,2,16,384]{3,2,1,0:T(8,128)(2,1)S(1)}, u32[]{:S(2)}, u32[]{:S(2)}) collective-permute-start(bf16[16,2,16,384]{3,2,1,0:T(8,128)(2,1)S(1)} %get-tuple-element.21.own_ref), channel_id=1, source_target_pairs={{8,0},{16,8},{24,16},{32,24},{40,32},{48,40},{56,48},{64,56},{72,6... | collective-permute-start | bytes 1179656 | tf_op jit(solution)/shard_map/ppermute | solution.py:210
  194.5 2.1 collective-permute-start.14
  196.7 7.4 %collective-permute-done.15.after_ref = bf16[16,2,16,384]{3,2,1,0:T(8,128)(2,1)S(1)} collective-permute-done((bf16[16,2,16,384]{3,2,1,0:T(8,128)(2,1)S(1)}, bf16[16,2,16,384]{3,2,1,0:T(8,128)(2,1)S(1)}, u32[]{:S(2)}, u32[]{:S(2)}) %collective-permute-start.15) | collective-permute-done | bytes 393248 | tf_op jit(solution)/shard_map/ppermute | solution.py:210
  204.1 7.0 %collective-permute-done.14.before_ref = bf16[16,2,16,384]{3,2,1,0:T(8,128)(2,1)S(1)} collective-permute-done((bf16[16,2,16,384]{3,2,1,0:T(8,128)(2,1)S(1)}, bf16[16,2,16,384]{3,2,1,0:T(8,128)(2,1)S(1)}, u32[]{:S(2)}, u32[]{:S(2)}) %collective-permute-start.14) | collective-permute-done | bytes 393248 | tf_op jit(solution)/shard_map/ppermute | solution.py:210
  211.0 4.3 %coarse.1 = (f32[2,96,256]{2,1,0:T(8,128)S(1)}, bf16[2,96,256]{2,1,0:T(8,128)(2,1)S(1)}) custom-call(s32[6]{0:T(128)S(1)} %stack.24.where_ref, s32[16,2]{1,0:T(8,128)S(1)} %broadcast_add_fusion.2.col_ref, s32[48,4]{1,0:T(8,128)S(1)} %pad_add_fusion.place_ref, bf16[16,2,192,192]{3,2,1,0:T(8,128)(2,1)S(1)} %copy-done.1, bf16[16,192,192]{2,1,0:T(8,128)(2,1)S(1)} %copy-done.5, ...), custom_call_target="tpu_custom_call" | custom-call | tf_op jit(solution)/shard_map/coarse/pallas_call | solution.py:227
  215.3 6.4 %collective-permute-start.17 = (bf16[2,96,256]{2,1,0:T(8,128)(2,1)S(1)}, bf16[2,96,256]{2,1,0:T(8,128)(2,1)S(1)}, u32[]{:S(2)}, u32[]{:S(2)}) collective-permute-start(bf16[2,96,256]{2,1,0:T(8,128)(2,1)S(1)} %get-tuple-element.23), channel_id=1, source_target_pairs={{0,2},{1,7},{2,0},{3,5},{4,6},{5,3},{6,4},{7,1},{8,10},{9,15},{10,... | collective-permute-start | bytes 294920 | tf_op jit(solution)/shard_map/ppermute | solution.py:219
  221.7 2.9 %collective-permute-done.17 = bf16[2,96,256]{2,1,0:T(8,128)(2,1)S(1)} collective-permute-done((bf16[2,96,256]{2,1,0:T(8,128)(2,1)S(1)}, bf16[2,96,256]{2,1,0:T(8,128)(2,1)S(1)}, u32[]{:S(2)}, u32[]{:S(2)}) %collective-permute-start.17) | collective-permute-done | bytes 98336 | tf_op jit(solution)/shard_map/ppermute | solution.py:219
  224.6 7.8 %collective-permute-start.18 = (bf16[96,256]{1,0:T(8,128)(2,1)S(1)}, bf16[96,256]{1,0:T(8,128)(2,1)S(1)}, u32[]{:S(2)}, u32[]{:S(2)}) collective-permute-start(bf16[96,256]{1,0:T(8,128)(2,1)S(1)} %fusion.6), channel_id=1, source_target_pairs={{0,6},{1,3},{2,4},{3,1},{4,2},{5,7},{6,0},{7,5},{8,14},{9,11},{10,... | collective-permute-start | bytes 147464 | tf_op jit(solution)/shard_map/ppermute | solution.py:219
  232.4 1.5 collective-permute-done.18
  233.9 5.0 %collective-permute-start.19 = (f32[96,128]{1,0:T(8,128)S(1)}, f32[96,128]{1,0:T(8,128)S(1)}, u32[]{:S(2)}, u32[]{:S(2)}) collective-permute-start(f32[96,128]{1,0:T(8,128)S(1)} %slice.60), channel_id=1, source_target_pairs={{0,1},{1,0},{2,3},{3,2},{4,5},{5,4},{6,7},{7,6},{8,9},{9,8},{10,11... | collective-permute-start | bytes 147464 | tf_op jit(solution)/shard_map/ppermute | solution.py:371
  239.0 0.9 collective-permute-done.19
  240.5 0.9 maximum_bitcast_fusion
  (84 shorter events, 13.0 us)
Async XLA Ops:
  0.6 1.0 copy-start.6
  1.6 35.3 %copy-start.23 = (s32[16]{0:T(128)S(1)}, s32[16]{0:T(128)}, u32[]{:S(2)}) copy-start(s32[16]{0:T(128)} %param.9) | copy-start | bytes 196
  1.6 35.9 %copy-start.7 = (f32[16,16,192]{2,1,0:T(8,128)S(1)}, f32[16,16,192]{2,1,0:T(8,128)}, u32[]{:S(2)}) copy-start(f32[16,16,192]{2,1,0:T(8,128)} %x_ref.3) | copy-start | bytes 589828
  1.7 10.5 %collective-permute-start.1 = (bf16[8,16,384]{2,1,0:T(8,128)(2,1)S(1)}, bf16[8,16,384]{2,1,0:T(8,128)(2,1)S(1)}, u32[]{:S(2)}, u32[]{:S(2)}) collective-permute-start(bf16[8,16,384]{2,1,0:T(8,128)(2,1)S(1)} %fold.1.own_ref), channel_id=1, source_target_pairs={{8,0},{16,8},{24,16},{32,24},{40,32},{48,40},{56,48},{64,56},{72,6... | collective-permute-start | bytes 294920 | tf_op jit(solution)/shard_map/ppermute | solution.py:210
  8.1 9.6 %collective-permute-start = (bf16[8,16,384]{2,1,0:T(8,128)(2,1)S(1)}, bf16[8,16,384]{2,1,0:T(8,128)(2,1)S(1)}, u32[]{:S(2)}, u32[]{:S(2)}) collective-permute-start(bf16[8,16,384]{2,1,0:T(8,128)(2,1)S(1)} %fold.1.own_ref), channel_id=1, source_target_pairs={{0,8},{8,16},{16,24},{24,32},{32,40},{40,48},{48,56},{56,64},{64,7... | collective-permute-start | bytes 294920 | tf_op jit(solution)/shard_map/ppermute | solution.py:210
  12.2 0.6 copy-start.16
  17.6 0.6 copy-start.18
  18.3 1.9 copy-start
  20.2 0.9 copy-start.17
  21.1 0.9 copy-start.19
  22.0 45.1 %copy-start.1 = (bf16[16,2,192,192]{3,2,1,0:T(8,128)(2,1)S(1)}, bf16[16,2,192,192]{3,2,1,0:T(8,128)(2,1)}, u32[]{:S(2)}) copy-start(bf16[16,2,192,192]{3,2,1,0:T(8,128)(2,1)} %a_ref.9) | copy-start | bytes 7077892
  24.4 17.5 %collective-permute-start.2 = (bf16[8,16,384]{2,1,0:T(8,128)(2,1)}, bf16[8,16,384]{2,1,0:T(8,128)(2,1)S(1)}, u32[]{:S(2)}, u32[]{:S(2)}) collective-permute-start(bf16[8,16,384]{2,1,0:T(8,128)(2,1)} %couple.3), channel_id=1, source_target_pairs={{0,2},{1,7},{2,0},{3,5},{4,6},{5,3},{6,4},{7,1},{8,10},{9,15},{10,... | collective-permute-start | bytes 294920 | tf_op jit(solution)/shard_map/ppermute | solution.py:219
  37.5 1.4 copy-start.2
  42.8 11.1 %collective-permute-start.3 = (bf16[8,16,384]{2,1,0:T(8,128)(2,1)S(1)}, bf16[8,16,384]{2,1,0:T(8,128)(2,1)S(1)}, u32[]{:S(2)}, u32[]{:S(2)}) collective-permute-start(bf16[8,16,384]{2,1,0:T(8,128)(2,1)S(1)} %add_convert_fusion.2.near_ref), channel_id=1, source_target_pairs={{0,6},{1,3},{2,4},{3,1},{4,2},{5,7},{6,0},{7,5},{8,14},{9,11},{10,... | collective-permute-start | bytes 294920 | tf_op jit(solution)/shard_map/ppermute | solution.py:219
  54.1 0.7 copy-start.10
  54.8 6.0 %collective-permute-start.5 = (bf16[9,16,384]{2,1,0:T(8,128)(2,1)S(1)}, bf16[9,16,384]{2,1,0:T(8,128)(2,1)S(1)}, u32[]{:S(2)}, u32[]{:S(2)}) collective-permute-start(bf16[9,16,384]{2,1,0:T(8,128)(2,1)S(1)} %get-tuple-element.16.own_ref), channel_id=1, source_target_pairs={{8,0},{16,8},{24,16},{32,24},{40,32},{48,40},{56,48},{64,56},{72,6... | collective-permute-start | bytes 331784 | tf_op jit(solution)/shard_map/ppermute | solution.py:210
  56.7 9.7 %collective-permute-start.4 = (bf16[9,16,384]{2,1,0:T(8,128)(2,1)S(1)}, bf16[9,16,384]{2,1,0:T(8,128)(2,1)S(1)}, u32[]{:S(2)}, u32[]{:S(2)}) collective-permute-start(bf16[9,16,384]{2,1,0:T(8,128)(2,1)S(1)} %get-tuple-element.16.own_ref), channel_id=1, source_target_pairs={{0,8},{8,16},{16,24},{24,32},{32,40},{40,48},{48,56},{56,64},{64,7... | collective-permute-start | bytes 331784 | tf_op jit(solution)/shard_map/ppermute | solution.py:210
  60.1 0.6 copy-start.14
  66.5 0.6 copy-start.12
  67.1 0.9 copy-start.13
  68.0 0.9 copy-start.15
  70.7 9.5 %collective-permute-start.6 = (bf16[8,16,384]{2,1,0:T(8,128)(2,1)S(1)}, bf16[8,16,384]{2,1,0:T(8,128)(2,1)S(1)}, u32[]{:S(2)}, u32[]{:S(2)}) collective-permute-start(bf16[8,16,384]{2,1,0:T(8,128)(2,1)S(1)} %couple.4), channel_id=1, source_target_pairs={{0,2},{1,7},{2,0},{3,5},{4,6},{5,3},{6,4},{7,1},{8,10},{9,15},{10,... | collective-permute-start | bytes 294920 | tf_op jit(solution)/shard_map/ppermute | solution.py:219
  80.2 9.7 %collective-permute-start.7 = (bf16[8,16,384]{2,1,0:T(8,128)(2,1)S(1)}, bf16[8,16,384]{2,1,0:T(8,128)(2,1)S(1)}, u32[]{:S(2)}, u32[]{:S(2)}) collective-permute-start(bf16[8,16,384]{2,1,0:T(8,128)(2,1)S(1)} %add_convert_fusion.1.near_ref), channel_id=1, source_target_pairs={{0,6},{1,3},{2,4},{3,1},{4,2},{5,7},{6,0},{7,5},{8,14},{9,11},{10,... | collective-permute-start | bytes 294920 | tf_op jit(solution)/shard_map/ppermute | solution.py:219
  87.0 1.4 copy-start.3
  88.4 0.9 copy-start.11
  89.9 0.7 copy-start.20
  90.5 0.9 copy-start.21
  91.6 0.7 copy-start.8
  92.3 5.6 %collective-permute-start.9 = (bf16[8,16,384]{2,1,0:T(8,128)(2,1)S(1)}, bf16[8,16,384]{2,1,0:T(8,128)(2,1)S(1)}, u32[]{:S(2)}, u32[]{:S(2)}) collective-permute-start(bf16[8,16,384]{2,1,0:T(8,128)(2,1)S(1)} %get-tuple-element.18.own_ref), channel_id=1, source_target_pairs={{8,0},{16,8},{24,16},{32,24},{40,32},{48,40},{56,48},{64,56},{72,6... | collective-permute-start | bytes 294920 | tf_op jit(solution)/shard_map/ppermute | solution.py:210
  94.2 9.6 %collective-permute-start.8 = (bf16[8,16,384]{2,1,0:T(8,128)(2,1)S(1)}, bf16[8,16,384]{2,1,0:T(8,128)(2,1)S(1)}, u32[]{:S(2)}, u32[]{:S(2)}) collective-permute-start(bf16[8,16,384]{2,1,0:T(8,128)(2,1)S(1)} %get-tuple-element.18.own_ref), channel_id=1, source_target_pairs={{0,8},{8,16},{16,24},{24,32},{32,40},{40,48},{48,56},{56,64},{64,7... | collective-permute-start | bytes 294920 | tf_op jit(solution)/shard_map/ppermute | solution.py:210
  105.6 10.7 %collective-permute-start.10 = (bf16[9,16,384]{2,1,0:T(8,128)(2,1)S(1)}, bf16[9,16,384]{2,1,0:T(8,128)(2,1)}, u32[]{:S(2)}, u32[]{:S(2)}) collective-permute-start(bf16[9,16,384]{2,1,0:T(8,128)(2,1)S(1)} %couple.5), channel_id=1, source_target_pairs={{0,2},{1,7},{2,0},{3,5},{4,6},{5,3},{6,4},{7,1},{8,10},{9,15},{10,... | collective-permute-start | bytes 331784 | tf_op jit(solution)/shard_map/ppermute | solution.py:219
  112.8 1.4 copy-start.4
  114.2 0.9 copy-start.9
  117.2 13.8 %collective-permute-start.11 = (bf16[8,16,384]{2,1,0:T(8,128)(2,1)S(1)}, bf16[8,16,384]{2,1,0:T(8,128)(2,1)S(1)}, u32[]{:S(2)}, u32[]{:S(2)}) collective-permute-start(bf16[8,16,384]{2,1,0:T(8,128)(2,1)S(1)} %add_convert_fusion.near_ref), channel_id=1, source_target_pairs={{0,6},{1,3},{2,4},{3,1},{4,2},{5,7},{6,0},{7,5},{8,14},{9,11},{10,... | collective-permute-start | bytes 294920 | tf_op jit(solution)/shard_map/ppermute | solution.py:219
  147.7 23.7 %copy-start.5 = (bf16[16,192,192]{2,1,0:T(8,128)(2,1)S(1)}, bf16[16,192,192]{2,1,0:T(8,128)(2,1)}, u32[]{:S(2)}) copy-start(bf16[16,192,192]{2,1,0:T(8,128)(2,1)} %diag_ref.9) | copy-start | bytes 3538948
  148.8 47.8 %copy-start.22 = (s32[16,4]{1,0:T(8,128)S(1)}, s32[16,4]{1,0:T(8,128)}, u32[]{:S(2)}) copy-start(s32[16,4]{1,0:T(8,128)} %get-tuple-element.24) | copy-start | bytes 772
  150.5 14.2 %collective-permute-start.12 = (bf16[16,16,384]{2,1,0:T(8,128)(2,1)S(1)}, bf16[16,16,384]{2,1,0:T(8,128)(2,1)S(1)}, u32[]{:S(2)}, u32[]{:S(2)}) collective-permute-start(bf16[16,16,384]{2,1,0:T(8,128)(2,1)S(1)} %fit.1.near_ref), channel_id=1, source_target_pairs={{0,2},{1,7},{2,0},{3,5},{4,6},{5,3},{6,4},{7,1},{8,10},{9,15},{10,... | collective-permute-start | bytes 589832 | tf_op jit(solution)/shard_map/ppermute | solution.py:219
  167.4 13.9 %collective-permute-start.13 = (bf16[16,2,16,384]{3,2,1,0:T(8,128)(2,1)S(1)}, bf16[16,2,16,384]{3,2,1,0:T(8,128)(2,1)S(1)}, u32[]{:S(2)}, u32[]{:S(2)}) collective-permute-start(bf16[16,2,16,384]{3,2,1,0:T(8,128)(2,1)S(1)} %slots.1.near_ref), channel_id=1, source_target_pairs={{0,6},{1,3},{2,4},{3,1},{4,2},{5,7},{6,0},{7,5},{8,14},{9,11},{10,... | collective-permute-start | bytes 1179656 | tf_op jit(solution)/shard_map/ppermute | solution.py:219
  183.3 13.3 %collective-permute-start.16 = (bf16[16,2,16,384]{3,2,1,0:T(8,128)(2,1)S(1)}, bf16[16,2,16,384]{3,2,1,0:T(8,128)(2,1)S(1)}, u32[]{:S(2)}, u32[]{:S(2)}) collective-permute-start(bf16[16,2,16,384]{3,2,1,0:T(8,128)(2,1)S(1)} %get-tuple-element.21.own_ref), channel_id=1, source_target_pairs={{0,1},{1,0},{2,3},{3,2},{4,5},{5,4},{6,7},{7,6},{8,9},{9,8},{10,11... | collective-permute-start | bytes 1179656 | tf_op jit(solution)/shard_map/ppermute | solution.py:348
  185.2 18.8 %collective-permute-start.15 = (bf16[16,2,16,384]{3,2,1,0:T(8,128)(2,1)S(1)}, bf16[16,2,16,384]{3,2,1,0:T(8,128)(2,1)S(1)}, u32[]{:S(2)}, u32[]{:S(2)}) collective-permute-start(bf16[16,2,16,384]{3,2,1,0:T(8,128)(2,1)S(1)} %get-tuple-element.21.own_ref), channel_id=1, source_target_pairs={{8,0},{16,8},{24,16},{32,24},{40,32},{48,40},{56,48},{64,56},{72,6... | collective-permute-start | bytes 1179656 | tf_op jit(solution)/shard_map/ppermute | solution.py:210
  194.5 16.5 %collective-permute-start.14 = (bf16[16,2,16,384]{3,2,1,0:T(8,128)(2,1)S(1)}, bf16[16,2,16,384]{3,2,1,0:T(8,128)(2,1)S(1)}, u32[]{:S(2)}, u32[]{:S(2)}) collective-permute-start(bf16[16,2,16,384]{3,2,1,0:T(8,128)(2,1)S(1)} %get-tuple-element.21.own_ref), channel_id=1, source_target_pairs={{0,8},{8,16},{16,24},{24,32},{32,40},{40,48},{48,56},{56,64},{64,7... | collective-permute-start | bytes 1179656 | tf_op jit(solution)/shard_map/ppermute | solution.py:210
  215.3 9.3 %collective-permute-start.17 = (bf16[2,96,256]{2,1,0:T(8,128)(2,1)S(1)}, bf16[2,96,256]{2,1,0:T(8,128)(2,1)S(1)}, u32[]{:S(2)}, u32[]{:S(2)}) collective-permute-start(bf16[2,96,256]{2,1,0:T(8,128)(2,1)S(1)} %get-tuple-element.23), channel_id=1, source_target_pairs={{0,2},{1,7},{2,0},{3,5},{4,6},{5,3},{6,4},{7,1},{8,10},{9,15},{10,... | collective-permute-start | bytes 294920 | tf_op jit(solution)/shard_map/ppermute | solution.py:219
  224.6 9.2 %collective-permute-start.18 = (bf16[96,256]{1,0:T(8,128)(2,1)S(1)}, bf16[96,256]{1,0:T(8,128)(2,1)S(1)}, u32[]{:S(2)}, u32[]{:S(2)}) collective-permute-start(bf16[96,256]{1,0:T(8,128)(2,1)S(1)} %fusion.6), channel_id=1, source_target_pairs={{0,6},{1,3},{2,4},{3,1},{4,2},{5,7},{6,0},{7,5},{8,14},{9,11},{10,... | collective-permute-start | bytes 147464 | tf_op jit(solution)/shard_map/ppermute | solution.py:219
  233.9 5.9 %collective-permute-start.19 = (f32[96,128]{1,0:T(8,128)S(1)}, f32[96,128]{1,0:T(8,128)S(1)}, u32[]{:S(2)}, u32[]{:S(2)}) collective-permute-start(f32[96,128]{1,0:T(8,128)S(1)} %slice.60), channel_id=1, source_target_pairs={{0,1},{1,0},{2,3},{3,2},{4,5},{5,4},{6,7},{7,6},{8,9},{9,8},{10,11... | collective-permute-start | bytes 147464 | tf_op jit(solution)/shard_map/ppermute | solution.py:371

commit v3 on v2

--- a/solution.py
+++ b/solution.py
@@ -22,117 +22,169 @@
     return lax.dot_general(left, right, (((1,), (1,)), ((), ())), preferred_element_type=F32)
 
 
+LANES = 128
+
+
+def put(ref, low, high):
+    width = low.shape[-1]
+    ref[:, :width] = low.astype(ref.dtype)
+    ref[:, width : 2 * width - LANES] = high[:, LANES:].astype(ref.dtype)
+    ref[:, 2 * width - LANES :] = high[:, :LANES].astype(ref.dtype)
+
+
+def take_into(low_ref, high_ref, block):
+    width = block.shape[-1] // 2
+    low_ref[...] = block[:, :width]
+    high_ref[:, :LANES] = block[:, 2 * width - LANES :]
+    high_ref[:, LANES:] = block[:, width : 2 * width - LANES]
+
+
 def center_kernel(diag_ref, x_ref, scale_ref, y_ref):
-    for i in range(x_ref.shape[0]):
+    half = x_ref.shape[0] // 2
+
+    def rest(i):
         x = x_ref[i]
-        y_ref[i] = x - scale_ref[i : i + 1, :] * dot_nt(x.astype(BF16), diag_ref[i])
-
-
-def first_center_kernel(diag_ref, x_ref, y_ref, scale_ref):
-    width = x_ref.shape[2]
+        return x - scale_ref[i : i + 1, :] * dot_nt(x.astype(BF16), diag_ref[i])
+
+    for m in range(half):
+        put(y_ref.at[m], rest(m), rest(half + m))
+
+
+def folded_center_kernel(diag_ref, x_ref, scale_ref, y_ref, rows):
+    half = x_ref.shape[0]
+    for m in range(half):
+        take_into(rows.at[m], rows.at[half + m], x_ref[m])
+    center_kernel(diag_ref, rows, scale_ref, y_ref)
+
+
+def first_center_kernel(diag_ref, x_ref, y_ref, scale_ref, folded_scale_ref):
+    rows, _, width = x_ref.shape
     on_diagonal = lax.broadcasted_iota(jnp.int32, (width, width), 0) == lax.broadcasted_iota(
         jnp.int32, (width, width), 1
     )
-    for i in range(x_ref.shape[0]):
-        x = x_ref[i]
-        block = diag_ref[i]
-        pivot = jnp.sum(jnp.where(on_diagonal, block.astype(F32), 0.0), axis=0, keepdims=True)
-        scale = DAMPING / pivot
-        scale_ref[i : i + 1, :] = scale
-        y_ref[i] = x - scale * dot_nt(x.astype(BF16), block)
+    for i in range(rows):
+        block = diag_ref[i].astype(F32)
+        pivot = jnp.sum(jnp.where(on_diagonal, block, 0.0), axis=0, keepdims=True)
+        scale_ref[i : i + 1, :] = DAMPING / pivot
+    for m in range(rows // 2):
+        put(
+            folded_scale_ref.at[m : m + 1],
+            scale_ref[m : m + 1, :],
+            scale_ref[rows // 2 + m : rows // 2 + m + 1, :],
+        )
+    center_kernel(diag_ref, x_ref, scale_ref, y_ref)
 
 
 def fold_kernel(x_ref, out_ref):
-    rows, _, width = x_ref.shape
-    for m in range(rows // 2):
-        out_ref[m, :, :width] = x_ref[m].astype(BF16)
-        out_ref[m, :, width:] = x_ref[rows // 2 + m].astype(BF16)
+    half = out_ref.shape[0]
+    for m in range(half):
+        put(out_ref.at[m], x_ref[m], x_ref[half + m])
+
+
+def stage_kernel(a_ref, diag_ref, a_out_ref, diag_out_ref, sems):
+    copies = [
+        pltpu.make_async_copy(a_ref, a_out_ref, sems.at[0]),
+        pltpu.make_async_copy(diag_ref, diag_out_ref, sems.at[1]),
+    ]
+    for copy in copies:
+        copy.start()
+    for copy in copies:
+        copy.wait()
+
+
+def pair_kernel(near_ref, far_ref, out_ref):
+    for m in range(out_ref.shape[0]):
+        out_ref[m] = (near_ref[m].astype(F32) + far_ref[m].astype(F32)).astype(BF16)
+
+
+def updated(m, rest_ref, near_ref, far_ref, scale_ref):
+    total = near_ref[m].astype(F32) + far_ref[m].astype(F32)
+    return rest_ref[m] - scale_ref[m : m + 1, :] * total
 
 
 def update_kernel(rest_ref, near_ref, far_ref, scale_ref, *refs):
-    rows, _, width = rest_ref.shape
-    half = rows // 2
+    half = rest_ref.shape[0]
     extra_ref = refs[0] if len(refs) == 3 else None
-    x_ref, folded_ref = refs[-2:]
-    for m in range(half):
-        total = near_ref[m].astype(F32) + far_ref[m].astype(F32)
-        low = rest_ref[m] - scale_ref[m : m + 1, :] * total[:, :width]
-        high = rest_ref[half + m] - scale_ref[half + m : half + m + 1, :] * total[:, width:]
-        x_ref[m] = low
-        x_ref[half + m] = high
-        folded_ref[m, :, :width] = low.astype(BF16)
-        folded_ref[m, :, width:] = high.astype(BF16)
+    x_ref, rounded_ref = refs[-2:]
+    for m in range(half):
+        x = updated(m, rest_ref, near_ref, far_ref, scale_ref)
+        x_ref[m] = x
+        rounded_ref[m] = x.astype(BF16)
     if extra_ref is not None:
-        folded_ref[half] = extra_ref[...]
+        rounded_ref[half] = extra_ref[...]
+
+
+def last_update_kernel(rest_ref, near_ref, far_ref, scale_ref, x_ref):
+    half = rest_ref.shape[0]
+    for m in range(half):
+        x = updated(m, rest_ref, near_ref, far_ref, scale_ref)
+        take_into(x_ref.at[m], x_ref.at[half + m], x)
 
 
 def couple_kernel(col_ref, a_ref, before_ref, own_ref, after_ref, *refs):
-    rows, stored, width = a_ref.shape[:3]
+    rows, stored = a_ref.shape[:2]
     half = rows // 2
     extra_ref = refs[0] if len(refs) == 3 else None
     out_ref, ext = refs[-2:]
     for s, ref in enumerate((before_ref, own_ref, after_ref)):
         for m in range(half):
-            block = ref[m]
-            ext[s * rows + m] = block[:, :width]
-            ext[s * rows + half + m] = block[:, width:]
+            take_into(ext.at[s * rows + m], ext.at[s * rows + half + m], ref[m])
 
     def product(i):
         total = dot_nt(ext[col_ref[i, 0]], a_ref[i, 0])
         for k in range(1, stored):
             total = total + dot_nt(ext[col_ref[i, k]], a_ref[i, k])
-        return total.astype(BF16)
-
-    for m in range(half):
-        out_ref[m, :, :width] = product(m)
-        out_ref[m, :, width:] = product(half + m)
+        return total
+
+    for m in range(half):
+        put(out_ref.at[m], product(m), product(half + m))
     if extra_ref is not None:
         out_ref[half] = extra_ref[...]
 
 
 def fit_kernel(col_ref, a_ref, own_ref, out_ref):
-    rows, stored, width = a_ref.shape[:3]
-    for i in range(rows):
+    rows, stored = a_ref.shape[:2]
+    half = rows // 2
+
+    def product(i, k):
+        row = jnp.clip(col_ref[i, k] - rows, 0, rows - 1)
+        return dot_nt(own_ref[row], a_ref[i, k])
+
+    for m in range(half):
         for k in range(stored):
-            row = jnp.clip(col_ref[i, k] - rows, 0, rows - 1)
-            out_ref[i, :, k * width : (k + 1) * width] = dot_nt(own_ref[row], a_ref[i, k]).astype(
-                BF16
-            )
+            put(out_ref.at[m, k], product(m, k), product(half + m, k))
 
 
 def slot_kernel(slot_ref, far_slot_ref, near_ref, far_ref, out_ref):
-    rows, vectors, wide = near_ref.shape
-    stored = slot_ref.shape[1]
-    width = wide // stored
-    for i in range(rows):
-        near = near_ref[i].astype(F32)
-        far = far_ref[i].astype(F32)
+    half, stored, vectors, wide = near_ref.shape
+    is_low = lax.broadcasted_iota(jnp.int32, (vectors, wide), 1) < wide // 2
+    for m in range(half):
+        terms = []
+        for ids_ref, ref in ((slot_ref, near_ref), (far_slot_ref, far_ref)):
+            for k in range(stored):
+                ids = jnp.where(is_low, ids_ref[m, k], ids_ref[half + m, k])
+                terms.append((ids, ref[m, k].astype(F32)))
         for p in range(SLOTS):
-            total = jnp.zeros((vectors, width), F32)
-            for k in range(stored):
-                lanes = slice(k * width, (k + 1) * width)
-                total = total + jnp.where(slot_ref[i, k] == p, near[:, lanes], 0.0)
-                total = total + jnp.where(far_slot_ref[i, k] == p, far[:, lanes], 0.0)
-            lanes = slice((p % 2) * width, (p % 2 + 1) * width)
-            out_ref[i, p // 2, :, lanes] = total.astype(BF16)
+            total = jnp.zeros((vectors, wide), F32)
+            for ids, value in terms:
+                total = total + jnp.where(ids == p, value, 0.0)
+            out_ref[m, p] = total.astype(BF16)
 
 
 def finish_kernel(where_ref, rest_ref, near_ref, far_ref, scale_ref, out_ref, here_ref):
-    rows, _, width = rest_ref.shape
+    half = rest_ref.shape[0]
     slot = where_ref[1]
-    for i in range(rows):
-        scale = scale_ref[i : i + 1, :]
+    for m in range(half):
+        scale = scale_ref[m : m + 1, :]
         here = jnp.zeros(rest_ref.shape[1:], F32)
-        for h in range(SLOTS // 2):
-            total = near_ref[i, h].astype(F32) + far_ref[i, h].astype(F32)
-            for q in range(2):
-                lanes = slice(q * width, (q + 1) * width)
-                value = -scale * total[:, lanes]
-                if h == 0 and q == 0:
-                    value = rest_ref[i] + value
-                out_ref[i, h, :, lanes] = value.astype(BF16)
-                here = jnp.where(slot == 2 * h + q, value, here)
-        here_ref[i, 0] = here.astype(BF16)
+        for p in range(SLOTS):
+            total = near_ref[m, p].astype(F32) + far_ref[m, p].astype(F32)
+            value = -scale * total
+            if p == 0:
+                value = rest_ref[m] + value
+            out_ref[m, p] = value.astype(BF16)
+            here = jnp.where(slot == p, value, here)
+        take_into(here_ref.at[m, 0], here_ref.at[half + m, 0], here.astype(BF16))
 
 
 def inverse_factor_kernel(m_ref, out_ref):
@@ -161,12 +213,12 @@
     reach[...] = jnp.zeros_like(reach)
     left[...] = jnp.zeros_like(left)
 
+    half = rows // 2
     for s, ref in enumerate((before_ref, own_ref, after_ref)):
-        for i in range(rows):
-            for h in range(SLOTS // 2):
-                block = ref[i, h]
-                ext[s * rows + i, 2 * h] = block[:, :width]
-                ext[s * rows + i, 2 * h + 1] = block[:, width:]
+        for m in range(half):
+            for p in range(SLOTS):
+                low, high = s * rows + m, s * rows + half + m
+                take_into(ext.at[low, p], ext.at[high, p], ref[m, p])
 
     def add(i, row, block):
         image = dot_nt(ext[row].reshape(SLOTS * vectors, width), block)
@@ -174,13 +226,14 @@
             at = place_ref[row, q]
             reach[i, at] = reach[i, at] + image[q * vectors : (q + 1) * vectors]
 
+    for m in range(half):
+        for p in range(SLOTS):
+            low = place_ref[rows + m, p] - SLAB_AGGS
+            high = place_ref[rows + half + m, p] - SLAB_AGGS
+            left[m, 0, low] = ext[rows + m, p]
+            left[half + m, 0, high] = ext[rows + half + m, p]
+            take_into(left.at[m, 1, low], left.at[half + m, 1, high], other_ref[m, p])
     for i in range(rows):
-        for h in range(SLOTS // 2):
-            other = other_ref[i, h]
-            for q in range(2):
-                group = place_ref[rows + i, 2 * h + q] - SLAB_AGGS
-                left[i, 0, group] = ext[rows + i, 2 * h + q]
-                left[i, 1, group] = other[:, q * width : (q + 1) * width]
         for k in range(stored):
             add(i, col_ref[i, k], a_ref[i, k])
 
@@ -270,20 +323,42 @@
     second = jnp.where(core == 0, 3 - slot, slot ^ 1)
     where = jnp.stack([core, slot, slot, second, first, slot ^ 2]).astype(jnp.int32)
 
+    folded_whole = jax.ShapeDtypeStruct((half, vectors, 2 * width), F32)
+    couplings, diag_blocks = pl.pallas_call(
+        stage_kernel,
+        out_shape=[pltpu.VMEM(x.shape, x.dtype) for x in (couplings, diag_blocks)],
+        in_specs=[pl.BlockSpec(memory_space=pl.ANY)] * 2,
+        out_specs=[VMEM_SPEC] * 2,
+        scratch_shapes=[pltpu.SemaphoreType.DMA((2,))],
+        compiler_params=pltpu.CompilerParams(vmem_limit_bytes=8 * 1024 * 1024),
+        cost_estimate=pl.CostEstimate(flops=0, bytes_accessed=16000000, transcendentals=0),
+        name="stage",
+    )(couplings, diag_blocks)
     rounded = kernel_call(fold_kernel, "fold", folded(half), [tests])
-    current, scale, places, far_slot = tests, None, None, None
+    current, scale, folded_scale, places, far_slot = tests, None, None, None, None
     for sweep in range(SWEEPS):
+        last = sweep == SWEEPS - 1
         before = shift(rounded, 1)
         after = shift(rounded, -1)
         if sweep == 0:
-            rest, scale = kernel_call(
+            rest, scale, folded_scale = kernel_call(
                 first_center_kernel,
                 "first_center",
-                [whole_shape, jax.ShapeDtypeStruct((rows, width), F32)],
+                [
+                    folded_whole,
+                    jax.ShapeDtypeStruct((rows, width), F32),
+                    jax.ShapeDtypeStruct((half, 2 * width), F32),
+                ],
                 [diag_blocks, current],
             )
         else:
-            rest = kernel_call(center_kernel, "center", whole_shape, [diag_blocks, current, scale])
+            rest = kernel_call(
+                folded_center_kernel,
+                "center",
+                folded_whole,
+                [diag_blocks, current, scale],
+                [pltpu.VMEM((rows, vectors, width), F32)],
+            )
         if sweep == 1:
             places = jnp.concatenate(
                 [
@@ -293,7 +368,6 @@
                 ],
                 axis=0,
             )
-        last = sweep == SWEEPS - 1
         part = kernel_call(
             couple_kernel,
             "couple",
@@ -304,15 +378,17 @@
         far = exchange(part, 0)
         if last:
             far_slot = from_block(far[half], stored)
-            part, far = part[:half], far[:half]
-        pair = (part.astype(F32) + far.astype(F32)).astype(BF16)
-        far = exchange(pair, 1)
-        current, rounded = kernel_call(
-            update_kernel,
-            "update",
-            [whole_shape, folded(half + (sweep == 0))],
-            [rest, pair, far, scale] + [ids_block] * (sweep == 0),
-        )
+        pair = kernel_call(pair_kernel, "pair", folded(half), [part, far])
+        operands = [rest, pair, exchange(pair, 1), folded_scale]
+        if last:
+            current = kernel_call(last_update_kernel, "last_update", whole_shape, operands)
+        else:
+            current, rounded = kernel_call(
+                update_kernel,
+                "update",
+                [folded_whole, folded(half + (sweep == 0))],
+                operands + [ids_block] * (sweep == 0),
+            )
 
     every = lax.all_gather(current, "vecs", axis=1, tiled=True)
     grams = jnp.einsum("ivb,iwb->ivw", every, every, precision=HIGHEST_PRECISION)
@@ -329,10 +405,13 @@
     tentative = jnp.einsum("icv,ivb->icb", row_inverse, every, precision=HIGHEST_PRECISION)
 
     moved = kernel_call(
-        fit_kernel, "fit", folded(rows), [cols, couplings, tentative.astype(BF16)]
-    )
-    rest = kernel_call(center_kernel, "center", whole_shape, [diag_blocks, tentative, scale])
-    slots_shape = jax.ShapeDtypeStruct((rows, SLOTS // 2, vectors, 2 * width), BF16)
+        fit_kernel,
+        "fit",
+        jax.ShapeDtypeStruct((half, stored, vectors, 2 * width), BF16),
+        [cols, couplings, tentative.astype(BF16)]
+    )
+    rest = kernel_call(center_kernel, "center", folded_whole, [diag_blocks, tentative, scale])
+    slots_shape = jax.ShapeDtypeStruct((half, SLOTS, vectors, 2 * width), BF16)
     pair = kernel_call(
         slot_kernel, "slots", slots_shape, [near_slot, far_slot, moved, exchange(moved, 0)]
     )
@@ -340,7 +419,7 @@
         finish_kernel,
         "finish",
         [slots_shape, jax.ShapeDtypeStruct((rows, 1, vectors, width), BF16)],
-        [where, rest, pair, exchange(pair, 1), scale],
+        [where, rest, pair, exchange(pair, 1), folded_scale],
     )
 
     before = shift(prolong, 1)

time: 243 us -> 235 us (0.967)
  the two profiles are of different devices: /device:TPU:33 before, /device:TPU:39 now
where the time goes in v3:
time: 235 us; the launch traced here: 234 us
  starting transfers between devices  104 us (44%)
  waiting for transfers between devices  69 us (29%)
  local copies, waits for them, and re-layouts  20 us (9%)
  Pallas kernels  19.3 us (8%)
  blocking collectives  13.5 us (6%)
  other arithmetic  4.49 us (2%)
    ppermute x10, starting transfers between devices, exchange(): return lax.ppermute(x, ('aggs', 'vecs'), pairs)  57.5 us
    ppermute x10, waiting for transfers between devices, exchange(): return lax.ppermute(x, ('aggs', 'vecs'), pairs)  47.8 us
    ppermute x8, starting transfers between devices, shift(): lax.ppermute(x, 'rows', [(i, i + by) for i in range(size) if 0 <= i + by...  24.8 us
    ppermute x8, waiting for transfers between devices, shift(): lax.ppermute(x, 'rows', [(i, i + by) for i in range(size) if 0 <= i + by...  20.3 us
    pallas_call x19, Pallas kernels, kernel_call(): pl.pallas_call(body, out_shape=shapes, in_specs=specs, out_specs=[VMEM_SP...  18.9 us
    unnamed x42, local copies, waits for them, and re-layouts  17.5 us
    ppermute x1, starting transfers between devices, on_device(): other = lax.ppermute(prolong, 'vecs', [(0, 1), (1, 0)])  16.7 us
    all_gather x1, blocking collectives, on_device(): every = lax.all_gather(current, 'vecs', axis=1, tiled=True)  13.5 us
  transfers between devices with their start and end apart: 20, of which 14 were waited for; matrix products, arithmetic and copies ran while one was open for 2% of the time, Pallas kernels for 1%

profile of v3, /device:TPU:39, one launch (start us, length us, event | category | flops | bytes accessed | tf_op | source)
XLA Modules:
  0.0 233.9 jit_solution(14145485115937822632)
XLA Ops:
  0.6 0.9 copy-done.7
  1.7 4.9 %collective-permute-start.1 = (bf16[8,16,384]{2,1,0:T(8,128)(2,1)S(1)}, bf16[8,16,384]{2,1,0:T(8,128)(2,1)}, u32[]{:S(2)}, u32[]{:S(2)}) collective-permute-start(bf16[8,16,384]{2,1,0:T(8,128)(2,1)S(1)} %fold.1.own_ref), channel_id=1, source_target_pairs={{8,0},{16,8},{24,16},{32,24},{40,32},{48,40},{56,48},{64,56},{72,6... | collective-permute-start | bytes 294920 | tf_op jit(solution)/shard_map/ppermute | solution.py:263
  6.6 1.9 collective-permute-start
  8.5 0.7 pad_add_fusion.1
  9.3 0.7 broadcast_subtract_fusion.1
  10.7 1.9 copy-done.5
  12.6 1.4 copy-done.6
  14.3 1.2 copy-done
  15.5 2.7 %couple.3.near_ref = bf16[8,16,384]{2,1,0:T(8,128)(2,1)} custom-call(s32[16,2]{1,0:T(8,128)S(1)} %broadcast_add_fusion.2.col_ref, bf16[16,2,192,192]{3,2,1,0:T(8,128)(2,1)S(1)} %get-tuple-element.17.a_ref, bf16[8,16,384]{2,1,0:T(8,128)(2,1)} %collective-permute-done.before_ref, bf16[8,16,384]{2,1,0:T(8,128)(2,1)S(1)} %fold.1.own_ref, ...), custom_call_target="tpu_custom_call" | custom-call | tf_op jit(solution)/shard_map/couple/pallas_call | solution.py:280
  18.2 11.5 %collective-permute-start.2 = (bf16[8,16,384]{2,1,0:T(8,128)(2,1)}, bf16[8,16,384]{2,1,0:T(8,128)(2,1)S(1)}, u32[]{:S(2)}, u32[]{:S(2)}) collective-permute-start(bf16[8,16,384]{2,1,0:T(8,128)(2,1)} %couple.3.near_ref), channel_id=1, source_target_pairs={{0,2},{1,7},{2,0},{3,5},{4,6},{5,3},{6,4},{7,1},{8,10},{9,15},{10,... | collective-permute-start | bytes 294920 | tf_op jit(solution)/shard_map/ppermute | solution.py:272
  30.9 1.4 copy-done.1
  32.3 0.7 first_center.1
  33.0 0.7 collective-permute-done.2.far_ref
  33.8 0.9 pair.3.near_ref
  34.7 5.6 %collective-permute-start.3 = (bf16[8,16,384]{2,1,0:T(8,128)(2,1)S(1)}, bf16[8,16,384]{2,1,0:T(8,128)(2,1)S(1)}, u32[]{:S(2)}, u32[]{:S(2)}) collective-permute-start(bf16[8,16,384]{2,1,0:T(8,128)(2,1)S(1)} %pair.3.near_ref), channel_id=1, source_target_pairs={{0,6},{1,3},{2,4},{3,1},{4,2},{5,7},{6,0},{7,5},{8,14},{9,11},{10,... | collective-permute-start | bytes 294920 | tf_op jit(solution)/shard_map/ppermute | solution.py:272
  40.3 0.9 select_reduce_fusion
  41.2 3.9 %collective-permute-done.3.far_ref = bf16[8,16,384]{2,1,0:T(8,128)(2,1)S(1)} collective-permute-done((bf16[8,16,384]{2,1,0:T(8,128)(2,1)S(1)}, bf16[8,16,384]{2,1,0:T(8,128)(2,1)S(1)}, u32[]{:S(2)}, u32[]{:S(2)}) %collective-permute-start.3) | collective-permute-done | bytes 98336 | tf_op jit(solution)/shard_map/ppermute | solution.py:272
  45.2 0.7 copy-done.11
  45.8 5.5 %collective-permute-start.5 = (bf16[9,16,384]{2,1,0:T(8,128)(2,1)S(1)}, bf16[9,16,384]{2,1,0:T(8,128)(2,1)S(1)}, u32[]{:S(2)}, u32[]{:S(2)}) collective-permute-start(bf16[9,16,384]{2,1,0:T(8,128)(2,1)S(1)} %get-tuple-element.21.own_ref), channel_id=1, source_target_pairs={{8,0},{16,8},{24,16},{32,24},{40,32},{48,40},{56,48},{64,56},{72,6... | collective-permute-start | bytes 331784 | tf_op jit(solution)/shard_map/ppermute | solution.py:263
  51.3 1.9 collective-permute-start.4
  54.0 4.9 %collective-permute-done.4.before_ref = bf16[9,16,384]{2,1,0:T(8,128)(2,1)S(1)} collective-permute-done((bf16[9,16,384]{2,1,0:T(8,128)(2,1)S(1)}, bf16[9,16,384]{2,1,0:T(8,128)(2,1)S(1)}, u32[]{:S(2)}, u32[]{:S(2)}) %collective-permute-start.4) | collective-permute-done | bytes 110624 | tf_op jit(solution)/shard_map/ppermute | solution.py:263
  59.6 0.9 copy-done.14
  60.5 0.9 copy-done.16
  61.4 1.7 couple.4.near_ref
  63.1 6.8 %collective-permute-start.6 = (bf16[8,16,384]{2,1,0:T(8,128)(2,1)S(1)}, bf16[8,16,384]{2,1,0:T(8,128)(2,1)S(1)}, u32[]{:S(2)}, u32[]{:S(2)}) collective-permute-start(bf16[8,16,384]{2,1,0:T(8,128)(2,1)S(1)} %couple.4.near_ref), channel_id=1, source_target_pairs={{0,2},{1,7},{2,0},{3,5},{4,6},{5,3},{6,4},{7,1},{8,10},{9,15},{10,... | collective-permute-start | bytes 294920 | tf_op jit(solution)/shard_map/ppermute | solution.py:272
  69.9 3.4 %collective-permute-done.6.far_ref = bf16[8,16,384]{2,1,0:T(8,128)(2,1)S(1)} collective-permute-done((bf16[8,16,384]{2,1,0:T(8,128)(2,1)S(1)}, bf16[8,16,384]{2,1,0:T(8,128)(2,1)S(1)}, u32[]{:S(2)}, u32[]{:S(2)}) %collective-permute-start.6) | collective-permute-done | bytes 98336 | tf_op jit(solution)/shard_map/ppermute | solution.py:272
  73.3 5.8 %collective-permute-start.7 = (bf16[8,16,384]{2,1,0:T(8,128)(2,1)S(1)}, bf16[8,16,384]{2,1,0:T(8,128)(2,1)S(1)}, u32[]{:S(2)}, u32[]{:S(2)}) collective-permute-start(bf16[8,16,384]{2,1,0:T(8,128)(2,1)S(1)} %pair.4.near_ref), channel_id=1, source_target_pairs={{0,6},{1,3},{2,4},{3,1},{4,2},{5,7},{6,0},{7,5},{8,14},{9,11},{10,... | collective-permute-start | bytes 294920 | tf_op jit(solution)/shard_map/ppermute | solution.py:272
  79.3 1.4 copy-done.2
  80.7 0.9 copy-done.12
  82.3 1.3 collective-permute-done.7.far_ref
  84.2 0.9 copy-done.18
  85.8 1.9 collective-permute-start.9
  87.7 3.4 %collective-permute-start.8 = (bf16[8,16,384]{2,1,0:T(8,128)(2,1)S(1)}, bf16[8,16,384]{2,1,0:T(8,128)(2,1)S(1)}, u32[]{:S(2)}, u32[]{:S(2)}) collective-permute-start(bf16[8,16,384]{2,1,0:T(8,128)(2,1)S(1)} %get-tuple-element.23.own_ref), channel_id=1, source_target_pairs={{0,8},{8,16},{16,24},{24,32},{32,40},{40,48},{48,56},{56,64},{64,7... | collective-permute-start | bytes 294920 | tf_op jit(solution)/shard_map/ppermute | solution.py:263
  91.2 4.0 %collective-permute-done.8.before_ref = bf16[8,16,384]{2,1,0:T(8,128)(2,1)S(1)} collective-permute-done((bf16[8,16,384]{2,1,0:T(8,128)(2,1)S(1)}, bf16[8,16,384]{2,1,0:T(8,128)(2,1)S(1)}, u32[]{:S(2)}, u32[]{:S(2)}) %collective-permute-start.8) | collective-permute-done | bytes 98336 | tf_op jit(solution)/shard_map/ppermute | solution.py:263
  95.2 1.7 couple.5.near_ref
  96.9 6.9 %collective-permute-start.10 = (bf16[9,16,384]{2,1,0:T(8,128)(2,1)S(1)}, bf16[9,16,384]{2,1,0:T(8,128)(2,1)S(1)}, u32[]{:S(2)}, u32[]{:S(2)}) collective-permute-start(bf16[9,16,384]{2,1,0:T(8,128)(2,1)S(1)} %couple.5.near_ref), channel_id=1, source_target_pairs={{0,2},{1,7},{2,0},{3,5},{4,6},{5,3},{6,4},{7,1},{8,10},{9,15},{10,... | collective-permute-start | bytes 331784 | tf_op jit(solution)/shard_map/ppermute | solution.py:272
  103.9 1.4 copy-done.3
  105.3 0.9 copy-done.10
  106.9 6.1 %collective-permute-start.11 = (bf16[8,16,384]{2,1,0:T(8,128)(2,1)S(1)}, bf16[8,16,384]{2,1,0:T(8,128)(2,1)S(1)}, u32[]{:S(2)}, u32[]{:S(2)}) collective-permute-start(bf16[8,16,384]{2,1,0:T(8,128)(2,1)S(1)} %pair.5.near_ref), channel_id=1, source_target_pairs={{0,6},{1,3},{2,4},{3,1},{4,2},{5,7},{6,0},{7,5},{8,14},{9,11},{10,... | collective-permute-start | bytes 294920 | tf_op jit(solution)/shard_map/ppermute | solution.py:272
  113.1 8.2 %collective-permute-done.11.far_ref = bf16[8,16,384]{2,1,0:T(8,128)(2,1)S(1)} collective-permute-done((bf16[8,16,384]{2,1,0:T(8,128)(2,1)S(1)}, bf16[8,16,384]{2,1,0:T(8,128)(2,1)S(1)}, u32[]{:S(2)}, u32[]{:S(2)}) %collective-permute-start.11) | collective-permute-done | bytes 98336 | tf_op jit(solution)/shard_map/ppermute | solution.py:272
  121.4 13.5 %all_gather.3 = f32[16,32,192]{2,1,0:T(8,128)S(1)} all-gather(f32[16,16,192]{2,1,0:T(8,128)S(1)} %last_update.1), channel_id=1, replica_groups=mesh['rows'=64,'aggs'=4,'vecs'=2] {'vecs'}, dimensions={1}, use_global_device_ids=true | all-gather | bytes 589824 | tf_op jit(solution)/shard_map/all_gather | solution.py:393
  135.5 0.7 convolution_multiply_fusion.m_ref
  136.2 0.8 inverse_factor.1
  138.0 1.7 fit.1.near_ref
  139.7 5.4 %collective-permute-start.12 = (bf16[8,2,16,384]{3,2,1,0:T(8,128)(2,1)S(1)}, bf16[8,2,16,384]{3,2,1,0:T(8,128)(2,1)S(1)}, u32[]{:S(2)}, u32[]{:S(2)}) collective-permute-start(bf16[8,2,16,384]{3,2,1,0:T(8,128)(2,1)S(1)} %fit.1.near_ref), channel_id=1, source_target_pairs={{0,2},{1,7},{2,0},{3,5},{4,6},{5,3},{6,4},{7,1},{8,10},{9,15},{10,... | collective-permute-start | bytes 589832 | tf_op jit(solution)/shard_map/ppermute | solution.py:272
  145.1 5.2 %collective-permute-done.12.far_ref = bf16[8,2,16,384]{3,2,1,0:T(8,128)(2,1)S(1)} collective-permute-done((bf16[8,2,16,384]{3,2,1,0:T(8,128)(2,1)S(1)}, bf16[8,2,16,384]{3,2,1,0:T(8,128)(2,1)S(1)}, u32[]{:S(2)}, u32[]{:S(2)}) %collective-permute-start.12) | collective-permute-done | bytes 196640 | tf_op jit(solution)/shard_map/ppermute | solution.py:272
  150.3 1.1 slots.1.near_ref
  151.4 1.9 collective-permute-start.13
  153.4 0.7 slice_bitcast_fusion.2
  154.7 13.8 %collective-permute-done.13.far_ref = bf16[8,4,16,384]{3,2,1,0:T(8,128)(2,1)S(1)} collective-permute-done((bf16[8,4,16,384]{3,2,1,0:T(8,128)(2,1)S(1)}, bf16[8,4,16,384]{3,2,1,0:T(8,128)(2,1)S(1)}, u32[]{:S(2)}, u32[]{:S(2)}) %collective-permute-start.13) | collective-permute-done | bytes 393248 | tf_op jit(solution)/shard_map/ppermute | solution.py:272
  168.5 1.4 finish.1
  169.9 16.7 %collective-permute-start.16 = (bf16[8,4,16,384]{3,2,1,0:T(8,128)(2,1)S(1)}, bf16[8,4,16,384]{3,2,1,0:T(8,128)(2,1)S(1)}, u32[]{:S(2)}, u32[]{:S(2)}) collective-permute-start(bf16[8,4,16,384]{3,2,1,0:T(8,128)(2,1)S(1)} %get-tuple-element.25.own_ref), channel_id=1, source_target_pairs={{0,1},{1,0},{2,3},{3,2},{4,5},{5,4},{6,7},{7,6},{8,9},{9,8},{10,11... | collective-permute-start | bytes 1179656 | tf_op jit(solution)/shard_map/ppermute | solution.py:427
  186.7 1.9 collective-permute-start.15
  188.6 3.4 %collective-permute-start.14 = (bf16[8,4,16,384]{3,2,1,0:T(8,128)(2,1)S(1)}, bf16[8,4,16,384]{3,2,1,0:T(8,128)(2,1)S(1)}, u32[]{:S(2)}, u32[]{:S(2)}) collective-permute-start(bf16[8,4,16,384]{3,2,1,0:T(8,128)(2,1)S(1)} %get-tuple-element.25.own_ref), channel_id=1, source_target_pairs={{0,8},{8,16},{16,24},{24,32},{32,40},{40,48},{48,56},{56,64},{64,7... | collective-permute-start | bytes 1179656 | tf_op jit(solution)/shard_map/ppermute | solution.py:263
  192.0 7.3 %collective-permute-done.15.after_ref = bf16[8,4,16,384]{3,2,1,0:T(8,128)(2,1)S(1)} collective-permute-done((bf16[8,4,16,384]{3,2,1,0:T(8,128)(2,1)S(1)}, bf16[8,4,16,384]{3,2,1,0:T(8,128)(2,1)S(1)}, u32[]{:S(2)}, u32[]{:S(2)}) %collective-permute-start.15) | collective-permute-done | bytes 393248 | tf_op jit(solution)/shard_map/ppermute | solution.py:263
  199.3 4.0 %collective-permute-done.14.before_ref = bf16[8,4,16,384]{3,2,1,0:T(8,128)(2,1)S(1)} collective-permute-done((bf16[8,4,16,384]{3,2,1,0:T(8,128)(2,1)S(1)}, bf16[8,4,16,384]{3,2,1,0:T(8,128)(2,1)S(1)}, u32[]{:S(2)}, u32[]{:S(2)}) %collective-permute-start.14) | collective-permute-done | bytes 393248 | tf_op jit(solution)/shard_map/ppermute | solution.py:263
  203.3 4.1 %coarse.1 = (f32[2,96,256]{2,1,0:T(8,128)S(1)}, bf16[2,96,256]{2,1,0:T(8,128)(2,1)S(1)}) custom-call(s32[6]{0:T(128)S(1)} %stack.24.where_ref, s32[16,2]{1,0:T(8,128)S(1)} %broadcast_add_fusion.2.col_ref, s32[48,4]{1,0:T(8,128)S(1)} %pad_add_fusion.place_ref, bf16[16,2,192,192]{3,2,1,0:T(8,128)(2,1)S(1)} %get-tuple-element.17.a_ref, ...), custom_call_target="tpu_custom_call" | custom-call | tf_op jit(solution)/shard_map/coarse/pallas_call | solution.py:280
  207.5 5.5 %collective-permute-start.17 = (bf16[2,96,256]{2,1,0:T(8,128)(2,1)S(1)}, bf16[2,96,256]{2,1,0:T(8,128)(2,1)S(1)}, u32[]{:S(2)}, u32[]{:S(2)}) collective-permute-start(bf16[2,96,256]{2,1,0:T(8,128)(2,1)S(1)} %get-tuple-element.27), channel_id=1, source_target_pairs={{0,2},{1,7},{2,0},{3,5},{4,6},{5,3},{6,4},{7,1},{8,10},{9,15},{10,... | collective-permute-start | bytes 294920 | tf_op jit(solution)/shard_map/ppermute | solution.py:272
  212.9 3.8 %collective-permute-done.17 = bf16[2,96,256]{2,1,0:T(8,128)(2,1)S(1)} collective-permute-done((bf16[2,96,256]{2,1,0:T(8,128)(2,1)S(1)}, bf16[2,96,256]{2,1,0:T(8,128)(2,1)S(1)}, u32[]{:S(2)}, u32[]{:S(2)}) %collective-permute-start.17) | collective-permute-done | bytes 98336 | tf_op jit(solution)/shard_map/ppermute | solution.py:272
  216.8 1.9 collective-permute-start.18
  218.7 7.3 %collective-permute-done.18 = bf16[96,256]{1,0:T(8,128)(2,1)S(1)} collective-permute-done((bf16[96,256]{1,0:T(8,128)(2,1)S(1)}, bf16[96,256]{1,0:T(8,128)(2,1)S(1)}, u32[]{:S(2)}, u32[]{:S(2)}) %collective-permute-start.18) | collective-permute-done | bytes 49184 | tf_op jit(solution)/shard_map/ppermute | solution.py:272
  226.1 5.3 %collective-permute-start.19 = (f32[96,128]{1,0:T(8,128)S(1)}, f32[96,128]{1,0:T(8,128)S(1)}, u32[]{:S(2)}, u32[]{:S(2)}) collective-permute-start(f32[96,128]{1,0:T(8,128)S(1)} %slice.50), channel_id=1, source_target_pairs={{0,1},{1,0},{2,3},{3,2},{4,5},{5,4},{6,7},{7,6},{8,9},{9,8},{10,11... | collective-permute-start | bytes 147464 | tf_op jit(solution)/shard_map/ppermute | solution.py:450
  231.3 0.9 collective-permute-done.19
  232.9 0.9 maximum_bitcast_fusion
  (79 shorter events, 10.0 us)
Async XLA Ops:
  0.6 1.0 copy-start.7
  1.7 13.8 %collective-permute-start.1 = (bf16[8,16,384]{2,1,0:T(8,128)(2,1)S(1)}, bf16[8,16,384]{2,1,0:T(8,128)(2,1)}, u32[]{:S(2)}, u32[]{:S(2)}) collective-permute-start(bf16[8,16,384]{2,1,0:T(8,128)(2,1)S(1)} %fold.1.own_ref), channel_id=1, source_target_pairs={{8,0},{16,8},{24,16},{32,24},{40,32},{48,40},{56,48},{64,56},{72,6... | collective-permute-start | bytes 294920 | tf_op jit(solution)/shard_map/ppermute | solution.py:263
  6.6 8.9 %collective-permute-start = (bf16[8,16,384]{2,1,0:T(8,128)(2,1)S(1)}, bf16[8,16,384]{2,1,0:T(8,128)(2,1)}, u32[]{:S(2)}, u32[]{:S(2)}) collective-permute-start(bf16[8,16,384]{2,1,0:T(8,128)(2,1)S(1)} %fold.1.own_ref), channel_id=1, source_target_pairs={{0,8},{8,16},{16,24},{24,32},{32,40},{40,48},{48,56},{56,64},{64,7... | collective-permute-start | bytes 294920 | tf_op jit(solution)/shard_map/ppermute | solution.py:263
  10.7 1.9 copy-start.5
  12.6 1.4 copy-start.6
  14.0 15.8 %copy-start.20 = (s32[16]{0:T(128)S(1)}, s32[16]{0:T(128)}, u32[]{:S(2)}) copy-start(s32[16]{0:T(128)} %param.9) | copy-start | bytes 196
  14.0 17.0 %copy-start.8 = (f32[16,16,192]{2,1,0:T(8,128)S(1)}, f32[16,16,192]{2,1,0:T(8,128)}, u32[]{:S(2)}) copy-start(f32[16,16,192]{2,1,0:T(8,128)} %x_ref.3) | copy-start | bytes 589828
  14.3 1.2 copy-start
  18.2 15.6 %collective-permute-start.2 = (bf16[8,16,384]{2,1,0:T(8,128)(2,1)}, bf16[8,16,384]{2,1,0:T(8,128)(2,1)S(1)}, u32[]{:S(2)}, u32[]{:S(2)}) collective-permute-start(bf16[8,16,384]{2,1,0:T(8,128)(2,1)} %couple.3.near_ref), channel_id=1, source_target_pairs={{0,2},{1,7},{2,0},{3,5},{4,6},{5,3},{6,4},{7,1},{8,10},{9,15},{10,... | collective-permute-start | bytes 294920 | tf_op jit(solution)/shard_map/ppermute | solution.py:272
  30.9 1.4 copy-start.1
  34.7 10.4 %collective-permute-start.3 = (bf16[8,16,384]{2,1,0:T(8,128)(2,1)S(1)}, bf16[8,16,384]{2,1,0:T(8,128)(2,1)S(1)}, u32[]{:S(2)}, u32[]{:S(2)}) collective-permute-start(bf16[8,16,384]{2,1,0:T(8,128)(2,1)S(1)} %pair.3.near_ref), channel_id=1, source_target_pairs={{0,6},{1,3},{2,4},{3,1},{4,2},{5,7},{6,0},{7,5},{8,14},{9,11},{10,... | collective-permute-start | bytes 294920 | tf_op jit(solution)/shard_map/ppermute | solution.py:272
  45.2 0.7 copy-start.11
  45.8 8.1 %collective-permute-start.5 = (bf16[9,16,384]{2,1,0:T(8,128)(2,1)S(1)}, bf16[9,16,384]{2,1,0:T(8,128)(2,1)S(1)}, u32[]{:S(2)}, u32[]{:S(2)}) collective-permute-start(bf16[9,16,384]{2,1,0:T(8,128)(2,1)S(1)} %get-tuple-element.21.own_ref), channel_id=1, source_target_pairs={{8,0},{16,8},{24,16},{32,24},{40,32},{48,40},{56,48},{64,56},{72,6... | collective-permute-start | bytes 331784 | tf_op jit(solution)/shard_map/ppermute | solution.py:263
  51.3 7.6 %collective-permute-start.4 = (bf16[9,16,384]{2,1,0:T(8,128)(2,1)S(1)}, bf16[9,16,384]{2,1,0:T(8,128)(2,1)S(1)}, u32[]{:S(2)}, u32[]{:S(2)}) collective-permute-start(bf16[9,16,384]{2,1,0:T(8,128)(2,1)S(1)} %get-tuple-element.21.own_ref), channel_id=1, source_target_pairs={{0,8},{8,16},{16,24},{24,32},{32,40},{40,48},{48,56},{56,64},{64,7... | collective-permute-start | bytes 331784 | tf_op jit(solution)/shard_map/ppermute | solution.py:263
  53.2 0.6 copy-start.15
  58.9 0.6 copy-start.13
  59.6 0.9 copy-start.14
  60.5 0.9 copy-start.16
  63.1 10.2 %collective-permute-start.6 = (bf16[8,16,384]{2,1,0:T(8,128)(2,1)S(1)}, bf16[8,16,384]{2,1,0:T(8,128)(2,1)S(1)}, u32[]{:S(2)}, u32[]{:S(2)}) collective-permute-start(bf16[8,16,384]{2,1,0:T(8,128)(2,1)S(1)} %couple.4.near_ref), channel_id=1, source_target_pairs={{0,2},{1,7},{2,0},{3,5},{4,6},{5,3},{6,4},{7,1},{8,10},{9,15},{10,... | collective-permute-start | bytes 294920 | tf_op jit(solution)/shard_map/ppermute | solution.py:272
  73.3 10.2 %collective-permute-start.7 = (bf16[8,16,384]{2,1,0:T(8,128)(2,1)S(1)}, bf16[8,16,384]{2,1,0:T(8,128)(2,1)S(1)}, u32[]{:S(2)}, u32[]{:S(2)}) collective-permute-start(bf16[8,16,384]{2,1,0:T(8,128)(2,1)S(1)} %pair.4.near_ref), channel_id=1, source_target_pairs={{0,6},{1,3},{2,4},{3,1},{4,2},{5,7},{6,0},{7,5},{8,14},{9,11},{10,... | collective-permute-start | bytes 294920 | tf_op jit(solution)/shard_map/ppermute | solution.py:272
  79.3 1.4 copy-start.2
  80.7 0.9 copy-start.12
  83.6 0.6 copy-start.17
  84.2 0.9 copy-start.18
  85.1 0.7 copy-start.9
  85.8 5.3 %collective-permute-start.9 = (bf16[8,16,384]{2,1,0:T(8,128)(2,1)S(1)}, bf16[8,16,384]{2,1,0:T(8,128)(2,1)S(1)}, u32[]{:S(2)}, u32[]{:S(2)}) collective-permute-start(bf16[8,16,384]{2,1,0:T(8,128)(2,1)S(1)} %get-tuple-element.23.own_ref), channel_id=1, source_target_pairs={{8,0},{16,8},{24,16},{32,24},{40,32},{48,40},{56,48},{64,56},{72,6... | collective-permute-start | bytes 294920 | tf_op jit(solution)/shard_map/ppermute | solution.py:263
  87.7 7.5 %collective-permute-start.8 = (bf16[8,16,384]{2,1,0:T(8,128)(2,1)S(1)}, bf16[8,16,384]{2,1,0:T(8,128)(2,1)S(1)}, u32[]{:S(2)}, u32[]{:S(2)}) collective-permute-start(bf16[8,16,384]{2,1,0:T(8,128)(2,1)S(1)} %get-tuple-element.23.own_ref), channel_id=1, source_target_pairs={{0,8},{8,16},{16,24},{24,32},{32,40},{40,48},{48,56},{56,64},{64,7... | collective-permute-start | bytes 294920 | tf_op jit(solution)/shard_map/ppermute | solution.py:263
  96.9 9.9 %collective-permute-start.10 = (bf16[9,16,384]{2,1,0:T(8,128)(2,1)S(1)}, bf16[9,16,384]{2,1,0:T(8,128)(2,1)S(1)}, u32[]{:S(2)}, u32[]{:S(2)}) collective-permute-start(bf16[9,16,384]{2,1,0:T(8,128)(2,1)S(1)} %couple.5.near_ref), channel_id=1, source_target_pairs={{0,2},{1,7},{2,0},{3,5},{4,6},{5,3},{6,4},{7,1},{8,10},{9,15},{10,... | collective-permute-start | bytes 331784 | tf_op jit(solution)/shard_map/ppermute | solution.py:272
  103.9 1.4 copy-start.3
  105.3 0.9 copy-start.10
  106.9 14.4 %collective-permute-start.11 = (bf16[8,16,384]{2,1,0:T(8,128)(2,1)S(1)}, bf16[8,16,384]{2,1,0:T(8,128)(2,1)S(1)}, u32[]{:S(2)}, u32[]{:S(2)}) collective-permute-start(bf16[8,16,384]{2,1,0:T(8,128)(2,1)S(1)} %pair.5.near_ref), channel_id=1, source_target_pairs={{0,6},{1,3},{2,4},{3,1},{4,2},{5,7},{6,0},{7,5},{8,14},{9,11},{10,... | collective-permute-start | bytes 294920 | tf_op jit(solution)/shard_map/ppermute | solution.py:272
  136.9 17.2 %copy-start.4 = (bf16[16,192,192]{2,1,0:T(8,128)(2,1)S(1)}, bf16[16,192,192]{2,1,0:T(8,128)(2,1)}, u32[]{:S(2)}) copy-start(bf16[16,192,192]{2,1,0:T(8,128)(2,1)} %copy-done) | copy-start | bytes 3538948
  138.0 54.0 %copy-start.19 = (s32[16,4]{1,0:T(8,128)S(1)}, s32[16,4]{1,0:T(8,128)}, u32[]{:S(2)}) copy-start(s32[16,4]{1,0:T(8,128)} %get-tuple-element.28) | copy-start | bytes 772
  139.7 10.7 %collective-permute-start.12 = (bf16[8,2,16,384]{3,2,1,0:T(8,128)(2,1)S(1)}, bf16[8,2,16,384]{3,2,1,0:T(8,128)(2,1)S(1)}, u32[]{:S(2)}, u32[]{:S(2)}) collective-permute-start(bf16[8,2,16,384]{3,2,1,0:T(8,128)(2,1)S(1)} %fit.1.near_ref), channel_id=1, source_target_pairs={{0,2},{1,7},{2,0},{3,5},{4,6},{5,3},{6,4},{7,1},{8,10},{9,15},{10,... | collective-permute-start | bytes 589832 | tf_op jit(solution)/shard_map/ppermute | solution.py:272
  151.4 17.1 %collective-permute-start.13 = (bf16[8,4,16,384]{3,2,1,0:T(8,128)(2,1)S(1)}, bf16[8,4,16,384]{3,2,1,0:T(8,128)(2,1)S(1)}, u32[]{:S(2)}, u32[]{:S(2)}) collective-permute-start(bf16[8,4,16,384]{3,2,1,0:T(8,128)(2,1)S(1)} %slots.1.near_ref), channel_id=1, source_target_pairs={{0,6},{1,3},{2,4},{3,1},{4,2},{5,7},{6,0},{7,5},{8,14},{9,11},{10,... | collective-permute-start | bytes 1179656 | tf_op jit(solution)/shard_map/ppermute | solution.py:272
  169.9 22.1 %collective-permute-start.16 = (bf16[8,4,16,384]{3,2,1,0:T(8,128)(2,1)S(1)}, bf16[8,4,16,384]{3,2,1,0:T(8,128)(2,1)S(1)}, u32[]{:S(2)}, u32[]{:S(2)}) collective-permute-start(bf16[8,4,16,384]{3,2,1,0:T(8,128)(2,1)S(1)} %get-tuple-element.25.own_ref), channel_id=1, source_target_pairs={{0,1},{1,0},{2,3},{3,2},{4,5},{5,4},{6,7},{7,6},{8,9},{9,8},{10,11... | collective-permute-start | bytes 1179656 | tf_op jit(solution)/shard_map/ppermute | solution.py:427
  186.7 12.6 %collective-permute-start.15 = (bf16[8,4,16,384]{3,2,1,0:T(8,128)(2,1)S(1)}, bf16[8,4,16,384]{3,2,1,0:T(8,128)(2,1)S(1)}, u32[]{:S(2)}, u32[]{:S(2)}) collective-permute-start(bf16[8,4,16,384]{3,2,1,0:T(8,128)(2,1)S(1)} %get-tuple-element.25.own_ref), channel_id=1, source_target_pairs={{8,0},{16,8},{24,16},{32,24},{40,32},{48,40},{56,48},{64,56},{72,6... | collective-permute-start | bytes 1179656 | tf_op jit(solution)/shard_map/ppermute | solution.py:263
  188.6 14.7 %collective-permute-start.14 = (bf16[8,4,16,384]{3,2,1,0:T(8,128)(2,1)S(1)}, bf16[8,4,16,384]{3,2,1,0:T(8,128)(2,1)S(1)}, u32[]{:S(2)}, u32[]{:S(2)}) collective-permute-start(bf16[8,4,16,384]{3,2,1,0:T(8,128)(2,1)S(1)} %get-tuple-element.25.own_ref), channel_id=1, source_target_pairs={{0,8},{8,16},{16,24},{24,32},{32,40},{40,48},{48,56},{56,64},{64,7... | collective-permute-start | bytes 1179656 | tf_op jit(solution)/shard_map/ppermute | solution.py:263
  207.5 9.3 %collective-permute-start.17 = (bf16[2,96,256]{2,1,0:T(8,128)(2,1)S(1)}, bf16[2,96,256]{2,1,0:T(8,128)(2,1)S(1)}, u32[]{:S(2)}, u32[]{:S(2)}) collective-permute-start(bf16[2,96,256]{2,1,0:T(8,128)(2,1)S(1)} %get-tuple-element.27), channel_id=1, source_target_pairs={{0,2},{1,7},{2,0},{3,5},{4,6},{5,3},{6,4},{7,1},{8,10},{9,15},{10,... | collective-permute-start | bytes 294920 | tf_op jit(solution)/shard_map/ppermute | solution.py:272
  216.8 9.3 %collective-permute-start.18 = (bf16[96,256]{1,0:T(8,128)(2,1)S(1)}, bf16[96,256]{1,0:T(8,128)(2,1)S(1)}, u32[]{:S(2)}, u32[]{:S(2)}) collective-permute-start(bf16[96,256]{1,0:T(8,128)(2,1)S(1)} %fusion.6), channel_id=1, source_target_pairs={{0,6},{1,3},{2,4},{3,1},{4,2},{5,7},{6,0},{7,5},{8,14},{9,11},{10,... | collective-permute-start | bytes 147464 | tf_op jit(solution)/shard_map/ppermute | solution.py:272
  226.1 6.1 %collective-permute-start.19 = (f32[96,128]{1,0:T(8,128)S(1)}, f32[96,128]{1,0:T(8,128)S(1)}, u32[]{:S(2)}, u32[]{:S(2)}) collective-permute-start(f32[96,128]{1,0:T(8,128)S(1)} %slice.50), channel_id=1, source_target_pairs={{0,1},{1,0},{2,3},{3,2},{4,5},{5,4},{6,7},{7,6},{8,9},{9,8},{10,11... | collective-permute-start | bytes 147464 | tf_op jit(solution)/shard_map/ppermute | solution.py:450

commit v4 on v3

--- a/solution.py
+++ b/solution.py
@@ -16,6 +16,7 @@
 
 SMEM_SPEC = pl.BlockSpec(memory_space=pltpu.SMEM)
 VMEM_SPEC = pl.BlockSpec(memory_space=pltpu.VMEM)
+HBM_SPEC = pl.BlockSpec(memory_space=pltpu.HBM)
 
 
 def dot_nt(left, right):
@@ -39,26 +40,58 @@
     high_ref[:, LANES:] = block[:, width : 2 * width - LANES]
 
 
-def center_kernel(diag_ref, x_ref, scale_ref, y_ref):
+CHUNK = 2
+
+
+def fetches(source_ref, held_ref, sems):
+    half = source_ref.shape[0] // 2
+    copies = []
+    for c in range(half // CHUNK):
+        for start in (c * CHUNK, half + c * CHUNK):
+            rows = pl.ds(start, CHUNK)
+            copies.append(
+                pltpu.make_async_copy(
+                    source_ref.at[rows], held_ref.at[rows], sems.at[len(copies)]
+                )
+            )
+    for copy in copies:
+        copy.start()
+
+    def ready(m):
+        if m % CHUNK == 0:
+            for copy in copies[2 * (m // CHUNK) : 2 * (m // CHUNK) + 2]:
+                copy.wait()
+
+    return ready
+
+
+def center_kernel(source_ref, x_ref, scale_ref, y_ref, diag_ref, sems, ready=None):
     half = x_ref.shape[0] // 2
+    if ready is None:
+        ready = fetches(source_ref, diag_ref, sems)
 
     def rest(i):
         x = x_ref[i]
         return x - scale_ref[i : i + 1, :] * dot_nt(x.astype(BF16), diag_ref[i])
 
     for m in range(half):
+        ready(m)
         put(y_ref.at[m], rest(m), rest(half + m))
 
 
-def folded_center_kernel(diag_ref, x_ref, scale_ref, y_ref, rows):
+def folded_center_kernel(source_ref, x_ref, scale_ref, y_ref, diag_ref, sems, rows):
     half = x_ref.shape[0]
+    ready = fetches(source_ref, diag_ref, sems)
     for m in range(half):
         take_into(rows.at[m], rows.at[half + m], x_ref[m])
-    center_kernel(diag_ref, rows, scale_ref, y_ref)
-
-
-def first_center_kernel(diag_ref, x_ref, y_ref, scale_ref, folded_scale_ref):
+    center_kernel(source_ref, rows, scale_ref, y_ref, diag_ref, sems, ready)
+
+
+def first_center_kernel(source_ref, x_ref, y_ref, scale_ref, folded_scale_ref, diag_ref, sems):
     rows, _, width = x_ref.shape
+    copy = pltpu.make_async_copy(source_ref, diag_ref, sems.at[0])
+    copy.start()
+    copy.wait()
     on_diagonal = lax.broadcasted_iota(jnp.int32, (width, width), 0) == lax.broadcasted_iota(
         jnp.int32, (width, width), 1
     )
@@ -72,7 +105,7 @@
             scale_ref[m : m + 1, :],
             scale_ref[rows // 2 + m : rows // 2 + m + 1, :],
         )
-    center_kernel(diag_ref, x_ref, scale_ref, y_ref)
+    center_kernel(source_ref, x_ref, scale_ref, y_ref, diag_ref, sems, lambda m: None)
 
 
 def fold_kernel(x_ref, out_ref):
@@ -81,15 +114,46 @@
         put(out_ref.at[m], x_ref[m], x_ref[half + m])
 
 
-def stage_kernel(a_ref, diag_ref, a_out_ref, diag_out_ref, sems):
-    copies = [
-        pltpu.make_async_copy(a_ref, a_out_ref, sems.at[0]),
-        pltpu.make_async_copy(diag_ref, diag_out_ref, sems.at[1]),
-    ]
-    for copy in copies:
-        copy.start()
-    for copy in copies:
-        copy.wait()
+def stage_kernel(source_ref, out_ref, a_ref, sems):
+    half = source_ref.shape[0] // 2
+    ready = fetches(source_ref, a_ref, sems)
+    for m in range(half):
+        ready(m)
+        for i in (m, half + m):
+            put(out_ref.at[i], a_ref[i, 0], a_ref[i, 1])
+
+
+def spread(low_ref, high_ref, main, rest):
+    zero = jnp.zeros_like(rest)
+    low_ref[:, :LANES] = main
+    low_ref[:, LANES:] = jnp.concatenate([rest, zero], axis=1)
+    high_ref[:, LANES:] = main
+    high_ref[:, :LANES] = jnp.concatenate([zero, rest], axis=1)
+
+
+def spread_folded(low_ref, high_ref, first, second, block):
+    wide = block.shape[-1]
+    width = wide // 2
+    spread(low_ref.at[first], high_ref.at[first], block[:, :LANES], block[:, LANES:width])
+    spread(
+        low_ref.at[second],
+        high_ref.at[second],
+        block[:, wide - LANES :],
+        block[:, width : wide - LANES],
+    )
+
+
+def joined(low, high):
+    return jnp.concatenate(
+        [low[:, :LANES], low[:, LANES:] + high[:, :LANES], high[:, LANES:]], axis=1
+    )
+
+
+def stacked(low, high):
+    zero = jnp.zeros((low.shape[0], LANES), low.dtype)
+    return jnp.concatenate(
+        [jnp.concatenate([low, zero], axis=1), jnp.concatenate([zero, high], axis=1)], axis=0
+    )
 
 
 def pair_kernel(near_ref, far_ref, out_ref):
@@ -122,19 +186,16 @@
 
 
 def couple_kernel(col_ref, a_ref, before_ref, own_ref, after_ref, *refs):
-    rows, stored = a_ref.shape[:2]
+    rows = a_ref.shape[0]
     half = rows // 2
-    extra_ref = refs[0] if len(refs) == 3 else None
-    out_ref, ext = refs[-2:]
+    extra_ref = refs[0] if len(refs) == 4 else None
+    out_ref, low, high = refs[-3:]
     for s, ref in enumerate((before_ref, own_ref, after_ref)):
         for m in range(half):
-            take_into(ext.at[s * rows + m], ext.at[s * rows + half + m], ref[m])
+            spread_folded(low, high, s * rows + m, s * rows + half + m, ref[m])
 
     def product(i):
-        total = dot_nt(ext[col_ref[i, 0]], a_ref[i, 0])
-        for k in range(1, stored):
-            total = total + dot_nt(ext[col_ref[i, k]], a_ref[i, k])
-        return total
+        return dot_nt(joined(low[col_ref[i, 0]], high[col_ref[i, 1]]), a_ref[i])
 
     for m in range(half):
         put(out_ref.at[m], product(m), product(half + m))
@@ -142,17 +203,22 @@
         out_ref[half] = extra_ref[...]
 
 
-def fit_kernel(col_ref, a_ref, own_ref, out_ref):
-    rows, stored = a_ref.shape[:2]
+def fit_kernel(col_ref, a_ref, own_ref, out_ref, low, high):
+    rows, vectors, width = own_ref.shape
     half = rows // 2
-
-    def product(i, k):
-        row = jnp.clip(col_ref[i, k] - rows, 0, rows - 1)
-        return dot_nt(own_ref[row], a_ref[i, k])
-
-    for m in range(half):
-        for k in range(stored):
-            put(out_ref.at[m, k], product(m, k), product(half + m, k))
+    for i in range(rows):
+        own = own_ref[i]
+        spread(low.at[i], high.at[i], own[:, :LANES], own[:, LANES:])
+
+    def products(i):
+        first, second = (jnp.clip(col_ref[i, k] - rows, 0, rows - 1) for k in range(2))
+        return dot_nt(stacked(low[first], high[second]), a_ref[i])
+
+    for m in range(half):
+        near, far = products(m), products(half + m)
+        for k in range(2):
+            part = slice(k * vectors, (k + 1) * vectors)
+            put(out_ref.at[m, k], near[part], far[part])
 
 
 def slot_kernel(slot_ref, far_slot_ref, near_ref, far_ref, out_ref):
@@ -202,14 +268,18 @@
 
 
 def coarse_kernel(
-    where_ref, col_ref, place_ref, a_ref, diag_ref, before_ref, own_ref, after_ref, other_ref,
-    keep_ref, send_ref, ext, reach, left, total,
+    where_ref, col_ref, place_ref, a_ref, diag_source_ref, before_ref, own_ref, after_ref, other_ref,
+    keep_ref, send_ref, low, high, reach, left, total, diag_ref, diag_sem,
 ):
-    rows, stored, width = a_ref.shape[:3]
+    rows, width = a_ref.shape[:2]
     vectors = own_ref.shape[2]
     share = rows // 4
     slot = where_ref[1]
     span = reach.shape[1]
+    diag_copy = pltpu.make_async_copy(
+        diag_source_ref.at[pl.ds(slot * share, share)], diag_ref, diag_sem.at[0]
+    )
+    diag_copy.start()
     reach[...] = jnp.zeros_like(reach)
     left[...] = jnp.zeros_like(left)
 
@@ -217,29 +287,41 @@
     for s, ref in enumerate((before_ref, own_ref, after_ref)):
         for m in range(half):
             for p in range(SLOTS):
-                low, high = s * rows + m, s * rows + half + m
-                take_into(ext.at[low, p], ext.at[high, p], ref[m, p])
-
-    def add(i, row, block):
-        image = dot_nt(ext[row].reshape(SLOTS * vectors, width), block)
+                spread_folded(
+                    low.at[:, p], high.at[:, p], s * rows + m, s * rows + half + m, ref[m, p]
+                )
+
+    span_rows = SLOTS * vectors
+
+    def add(i, row, image):
         for q in range(SLOTS):
             at = place_ref[row, q]
             reach[i, at] = reach[i, at] + image[q * vectors : (q + 1) * vectors]
 
     for m in range(half):
         for p in range(SLOTS):
-            low = place_ref[rows + m, p] - SLAB_AGGS
-            high = place_ref[rows + half + m, p] - SLAB_AGGS
-            left[m, 0, low] = ext[rows + m, p]
-            left[half + m, 0, high] = ext[rows + half + m, p]
-            take_into(left.at[m, 1, low], left.at[half + m, 1, high], other_ref[m, p])
-    for i in range(rows):
-        for k in range(stored):
-            add(i, col_ref[i, k], a_ref[i, k])
-
+            first = place_ref[rows + m, p] - SLAB_AGGS
+            second = place_ref[rows + half + m, p] - SLAB_AGGS
+            for side, ref in enumerate((own_ref, other_ref)):
+                take_into(left.at[m, side, first], left.at[half + m, side, second], ref[m, p])
+    for m in range(half):
+        for i in (m, half + m):
+            first, second = col_ref[i, 0], col_ref[i, 1]
+            images = dot_nt(
+                stacked(
+                    low[first].reshape(span_rows, 2 * LANES),
+                    high[second].reshape(span_rows, 2 * LANES),
+                ),
+                a_ref[i],
+            )
+            add(i, first, images[:span_rows])
+            add(i, second, images[span_rows:])
+
+    diag_copy.wait()
     for r in range(share):
         i = slot * share + r
-        add(i, rows + i, diag_ref[i])
+        own = low[rows + i].reshape(span_rows, 2 * LANES)[:, :width]
+        add(i, rows + i, dot_nt(own, diag_ref[r]))
 
     for i in range(rows):
         product = dot_nt(
@@ -274,8 +356,14 @@
 
 def kernel_call(body, name, shapes, operands, scratch=(), limit=12):
     several = isinstance(shapes, list)
+    is_block = [x.ndim == 3 and x.shape[-1] == x.shape[-2] and x.dtype == BF16 for x in operands]
     specs = [
-        SMEM_SPEC if x.dtype == jnp.int32 else VMEM_SPEC for x in operands
+        SMEM_SPEC if x.dtype == jnp.int32 else HBM_SPEC if block else VMEM_SPEC
+        for x, block in zip(operands, is_block)
+    ]
+    operands = [
+        pltpu.with_memory_space_constraint(x, pltpu.HBM) if block else x
+        for x, block in zip(operands, is_block)
     ]
     return pl.pallas_call(
         body,
@@ -286,6 +374,13 @@
         compiler_params=pltpu.CompilerParams(vmem_limit_bytes=limit * 1024 * 1024),
         name=name,
     )(*operands)
+
+
+def held(blocks):
+    return [
+        pltpu.VMEM(blocks.shape, blocks.dtype),
+        pltpu.SemaphoreType.DMA((blocks.shape[0] // CHUNK,)),
+    ]
 
 
 def as_block(values, shape):
@@ -324,16 +419,16 @@
     where = jnp.stack([core, slot, slot, second, first, slot ^ 2]).astype(jnp.int32)
 
     folded_whole = jax.ShapeDtypeStruct((half, vectors, 2 * width), F32)
-    couplings, diag_blocks = pl.pallas_call(
+    couplings = pl.pallas_call(
         stage_kernel,
-        out_shape=[pltpu.VMEM(x.shape, x.dtype) for x in (couplings, diag_blocks)],
-        in_specs=[pl.BlockSpec(memory_space=pl.ANY)] * 2,
-        out_specs=[VMEM_SPEC] * 2,
-        scratch_shapes=[pltpu.SemaphoreType.DMA((2,))],
-        compiler_params=pltpu.CompilerParams(vmem_limit_bytes=8 * 1024 * 1024),
-        cost_estimate=pl.CostEstimate(flops=0, bytes_accessed=16000000, transcendentals=0),
+        out_shape=pltpu.VMEM((rows, width, stored * width), BF16),
+        in_specs=[HBM_SPEC],
+        out_specs=VMEM_SPEC,
+        scratch_shapes=held(couplings),
+        compiler_params=pltpu.CompilerParams(vmem_limit_bytes=12 * 1024 * 1024),
+        cost_estimate=pl.CostEstimate(flops=0, bytes_accessed=8000000, transcendentals=0),
         name="stage",
-    )(couplings, diag_blocks)
+    )(pltpu.with_memory_space_constraint(couplings, pltpu.HBM))
     rounded = kernel_call(fold_kernel, "fold", folded(half), [tests])
     current, scale, folded_scale, places, far_slot = tests, None, None, None, None
     for sweep in range(SWEEPS):
@@ -350,6 +445,7 @@
                     jax.ShapeDtypeStruct((half, 2 * width), F32),
                 ],
                 [diag_blocks, current],
+                held(diag_blocks),
             )
         else:
             rest = kernel_call(
@@ -357,7 +453,7 @@
                 "center",
                 folded_whole,
                 [diag_blocks, current, scale],
-                [pltpu.VMEM((rows, vectors, width), F32)],
+                held(diag_blocks) + [pltpu.VMEM((rows, vectors, width), F32)],
             )
         if sweep == 1:
             places = jnp.concatenate(
@@ -373,7 +469,7 @@
             "couple",
             folded(half + last),
             [cols, couplings, before, rounded, after] + [slot_block] * last,
-            [pltpu.VMEM((3 * rows, vectors, width), BF16)],
+            [pltpu.VMEM((3 * rows, vectors, 2 * LANES), BF16)] * 2,
         )
         far = exchange(part, 0)
         if last:
@@ -408,9 +504,16 @@
         fit_kernel,
         "fit",
         jax.ShapeDtypeStruct((half, stored, vectors, 2 * width), BF16),
-        [cols, couplings, tentative.astype(BF16)]
-    )
-    rest = kernel_call(center_kernel, "center", folded_whole, [diag_blocks, tentative, scale])
+        [cols, couplings, tentative.astype(BF16)],
+        [pltpu.VMEM((rows, vectors, 2 * LANES), BF16)] * 2,
+    )
+    rest = kernel_call(
+        center_kernel,
+        "center",
+        folded_whole,
+        [diag_blocks, tentative, scale],
+        held(diag_blocks),
+    )
     slots_shape = jax.ShapeDtypeStruct((half, SLOTS, vectors, 2 * width), BF16)
     pair = kernel_call(
         slot_kernel, "slots", slots_shape, [near_slot, far_slot, moved, exchange(moved, 0)]
@@ -422,9 +525,9 @@
         [where, rest, pair, exchange(pair, 1), folded_scale],
     )
 
+    other = lax.ppermute(prolong, "vecs", [(0, 1), (1, 0)])
     before = shift(prolong, 1)
     after = shift(prolong, -1)
-    other = lax.ppermute(prolong, "vecs", [(0, 1), (1, 0)])
     span = 3 * SLAB_AGGS
     quarter = span * vectors // 4
     wide = SLAB_AGGS * 2 * vectors
@@ -437,10 +540,15 @@
         ],
         [where, cols, places, couplings, diag_blocks, before, prolong, after, other],
         [
-            pltpu.VMEM((3 * rows, SLOTS, vectors, width), BF16),
+            pltpu.VMEM((3 * rows, SLOTS, vectors, 2 * LANES), BF16),
+            pltpu.VMEM((3 * rows, SLOTS, vectors, 2 * LANES), BF16),
             pltpu.VMEM((rows, span, vectors, width), F32),
             pltpu.VMEM((rows, 2, SLAB_AGGS, vectors, width), BF16),
             pltpu.VMEM((span * vectors, wide), F32),
+        ]
+        + [
+            pltpu.VMEM((rows // 4, width, width), BF16),
+            pltpu.SemaphoreType.DMA((1,)),
         ],
         limit=28,
     )

time: 235 us -> 227 us (0.966)
  the two profiles are of different devices: /device:TPU:39 before, /device:TPU:3 now
where the time goes in v4:
time: 227 us; the launch traced here: 226 us
  waiting for transfers between devices  92.7 us (41%)
  starting transfers between devices  85.2 us (38%)
  Pallas kernels  26.8 us (12%)
  blocking collectives  12.9 us (6%)
  other arithmetic  2.66 us (1%)
  matrix products  2.34 us (1%)
    ppermute x10, waiting for transfers between devices, exchange(): return lax.ppermute(x, ('aggs', 'vecs'), pairs)  68.9 us
    ppermute x10, starting transfers between devices, exchange(): return lax.ppermute(x, ('aggs', 'vecs'), pairs)  49.7 us
    pallas_call x19, Pallas kernels, kernel_call(): pl.pallas_call(body, out_shape=shapes, in_specs=specs, out_specs=[VMEM_SP...  24.7 us
    ppermute x8, waiting for transfers between devices, shift(): lax.ppermute(x, 'rows', [(i, i + by) for i in range(size) if 0 <= i + by...  23 us
    ppermute x8, starting transfers between devices, shift(): lax.ppermute(x, 'rows', [(i, i + by) for i in range(size) if 0 <= i + by...  22.8 us
    all_gather x1, blocking collectives, on_device(): every = lax.all_gather(current, 'vecs', axis=1, tiled=True)  12.9 us
    ppermute x1, starting transfers between devices, on_device(): theirs = lax.ppermute(theirs, 'vecs', [(0, 1), (1, 0)])  6.41 us
    ppermute x1, starting transfers between devices, on_device(): other = lax.ppermute(prolong, 'vecs', [(0, 1), (1, 0)])  6.32 us
  transfers between devices with their start and end apart: 20, of which 16 were waited for; matrix products, arithmetic and copies ran while one was open for 1% of the time, Pallas kernels for 5%

profile of v4, /device:TPU:3, one launch (start us, length us, event | category | flops | bytes accessed | tf_op | source)
XLA Modules:
  0.0 225.9 jit_solution(11176891604702006867)
XLA Ops:
  0.6 0.9 copy-done
  1.7 4.6 %collective-permute-start.1 = (bf16[8,16,384]{2,1,0:T(8,128)(2,1)S(1)}, bf16[8,16,384]{2,1,0:T(8,128)(2,1)S(1)}, u32[]{:S(2)}, u32[]{:S(2)}) collective-permute-start(bf16[8,16,384]{2,1,0:T(8,128)(2,1)S(1)} %fold.1.own_ref), channel_id=1, source_target_pairs={{8,0},{16,8},{24,16},{32,24},{40,32},{48,40},{56,48},{64,56},{72,6... | collective-permute-start | bytes 294920 | tf_op jit(solution)/shard_map/ppermute | solution.py:345
  6.3 1.9 collective-permute-start
  8.2 0.7 pad_add_fusion.1
  9.0 0.7 broadcast_subtract_fusion.1
  9.8 2.1 stage.1.a_ref
  11.9 1.9 collective-permute-done.before_ref
  13.8 1.7 couple.3.near_ref
  15.5 12.5 %collective-permute-start.2 = (bf16[8,16,384]{2,1,0:T(8,128)(2,1)S(1)}, bf16[8,16,384]{2,1,0:T(8,128)(2,1)S(1)}, u32[]{:S(2)}, u32[]{:S(2)}) collective-permute-start(bf16[8,16,384]{2,1,0:T(8,128)(2,1)S(1)} %couple.3.near_ref), channel_id=1, source_target_pairs={{0,2},{1,7},{2,0},{3,5},{4,6},{5,3},{6,4},{7,1},{8,10},{9,15},{10,... | collective-permute-start | bytes 294920 | tf_op jit(solution)/shard_map/ppermute | solution.py:354
  28.1 2.2 first_center.1
  30.2 2.4 %collective-permute-done.2.far_ref = bf16[8,16,384]{2,1,0:T(8,128)(2,1)S(1)} collective-permute-done((bf16[8,16,384]{2,1,0:T(8,128)(2,1)S(1)}, bf16[8,16,384]{2,1,0:T(8,128)(2,1)S(1)}, u32[]{:S(2)}, u32[]{:S(2)}) %collective-permute-start.2) | collective-permute-done | bytes 98336 | tf_op jit(solution)/shard_map/ppermute | solution.py:354
  32.7 5.6 %collective-permute-start.3 = (bf16[8,16,384]{2,1,0:T(8,128)(2,1)S(1)}, bf16[8,16,384]{2,1,0:T(8,128)(2,1)S(1)}, u32[]{:S(2)}, u32[]{:S(2)}) collective-permute-start(bf16[8,16,384]{2,1,0:T(8,128)(2,1)S(1)} %pair.3.near_ref), channel_id=1, source_target_pairs={{0,6},{1,3},{2,4},{3,1},{4,2},{5,7},{6,0},{7,5},{8,14},{9,11},{10,... | collective-permute-start | bytes 294920 | tf_op jit(solution)/shard_map/ppermute | solution.py:354
  38.3 0.2 select_reduce_fusion
  38.5 6.3 %collective-permute-done.3.far_ref = bf16[8,16,384]{2,1,0:T(8,128)(2,1)S(1)} collective-permute-done((bf16[8,16,384]{2,1,0:T(8,128)(2,1)S(1)}, bf16[8,16,384]{2,1,0:T(8,128)(2,1)S(1)}, u32[]{:S(2)}, u32[]{:S(2)}) %collective-permute-start.3) | collective-permute-done | bytes 98336 | tf_op jit(solution)/shard_map/ppermute | solution.py:354
  44.9 3.6 %collective-permute-start.5 = (bf16[9,16,384]{2,1,0:T(8,128)(2,1)S(1)}, bf16[9,16,384]{2,1,0:T(8,128)(2,1)S(1)}, u32[]{:S(2)}, u32[]{:S(2)}) collective-permute-start(bf16[9,16,384]{2,1,0:T(8,128)(2,1)S(1)} %get-tuple-element.17.own_ref), channel_id=1, source_target_pairs={{8,0},{16,8},{24,16},{32,24},{40,32},{48,40},{56,48},{64,56},{72,6... | collective-permute-start | bytes 331784 | tf_op jit(solution)/shard_map/ppermute | solution.py:345
  48.5 1.9 collective-permute-start.4
  50.5 5.6 %collective-permute-done.4.before_ref = bf16[9,16,384]{2,1,0:T(8,128)(2,1)S(1)} collective-permute-done((bf16[9,16,384]{2,1,0:T(8,128)(2,1)S(1)}, bf16[9,16,384]{2,1,0:T(8,128)(2,1)S(1)}, u32[]{:S(2)}, u32[]{:S(2)}) %collective-permute-start.4) | collective-permute-done | bytes 110624 | tf_op jit(solution)/shard_map/ppermute | solution.py:345
  56.1 1.7 couple.4.near_ref
  57.8 5.1 %collective-permute-start.6 = (bf16[8,16,384]{2,1,0:T(8,128)(2,1)S(1)}, bf16[8,16,384]{2,1,0:T(8,128)(2,1)S(1)}, u32[]{:S(2)}, u32[]{:S(2)}) collective-permute-start(bf16[8,16,384]{2,1,0:T(8,128)(2,1)S(1)} %couple.4.near_ref), channel_id=1, source_target_pairs={{0,2},{1,7},{2,0},{3,5},{4,6},{5,3},{6,4},{7,1},{8,10},{9,15},{10,... | collective-permute-start | bytes 294920 | tf_op jit(solution)/shard_map/ppermute | solution.py:354
  63.0 4.1 %collective-permute-done.6.far_ref = bf16[8,16,384]{2,1,0:T(8,128)(2,1)S(1)} collective-permute-done((bf16[8,16,384]{2,1,0:T(8,128)(2,1)S(1)}, bf16[8,16,384]{2,1,0:T(8,128)(2,1)S(1)}, u32[]{:S(2)}, u32[]{:S(2)}) %collective-permute-start.6) | collective-permute-done | bytes 98336 | tf_op jit(solution)/shard_map/ppermute | solution.py:354
  67.1 6.7 %collective-permute-start.7 = (bf16[8,16,384]{2,1,0:T(8,128)(2,1)S(1)}, bf16[8,16,384]{2,1,0:T(8,128)(2,1)S(1)}, u32[]{:S(2)}, u32[]{:S(2)}) collective-permute-start(bf16[8,16,384]{2,1,0:T(8,128)(2,1)S(1)} %pair.4.near_ref), channel_id=1, source_target_pairs={{0,6},{1,3},{2,4},{3,1},{4,2},{5,7},{6,0},{7,5},{8,14},{9,11},{10,... | collective-permute-start | bytes 294920 | tf_op jit(solution)/shard_map/ppermute | solution.py:354
  74.1 2.3 center.3.rest_ref
  76.3 3.1 %collective-permute-done.7.far_ref = bf16[8,16,384]{2,1,0:T(8,128)(2,1)S(1)} collective-permute-done((bf16[8,16,384]{2,1,0:T(8,128)(2,1)S(1)}, bf16[8,16,384]{2,1,0:T(8,128)(2,1)S(1)}, u32[]{:S(2)}, u32[]{:S(2)}) %collective-permute-start.7) | collective-permute-done | bytes 98336 | tf_op jit(solution)/shard_map/ppermute | solution.py:354
  79.5 1.9 collective-permute-start.9
  81.4 3.4 %collective-permute-start.8 = (bf16[8,16,384]{2,1,0:T(8,128)(2,1)S(1)}, bf16[8,16,384]{2,1,0:T(8,128)(2,1)S(1)}, u32[]{:S(2)}, u32[]{:S(2)}) collective-permute-start(bf16[8,16,384]{2,1,0:T(8,128)(2,1)S(1)} %get-tuple-element.19.own_ref), channel_id=1, source_target_pairs={{0,8},{8,16},{16,24},{24,32},{32,40},{40,48},{48,56},{56,64},{64,7... | collective-permute-start | bytes 294920 | tf_op jit(solution)/shard_map/ppermute | solution.py:345
  84.9 4.3 %collective-permute-done.8.before_ref = bf16[8,16,384]{2,1,0:T(8,128)(2,1)S(1)} collective-permute-done((bf16[8,16,384]{2,1,0:T(8,128)(2,1)S(1)}, bf16[8,16,384]{2,1,0:T(8,128)(2,1)S(1)}, u32[]{:S(2)}, u32[]{:S(2)}) %collective-permute-start.8) | collective-permute-done | bytes 98336 | tf_op jit(solution)/shard_map/ppermute | solution.py:345
  89.2 1.7 couple.5.near_ref
  90.9 4.4 %collective-permute-start.10 = (bf16[9,16,384]{2,1,0:T(8,128)(2,1)S(1)}, bf16[9,16,384]{2,1,0:T(8,128)(2,1)S(1)}, u32[]{:S(2)}, u32[]{:S(2)}) collective-permute-start(bf16[9,16,384]{2,1,0:T(8,128)(2,1)S(1)} %couple.5.near_ref), channel_id=1, source_target_pairs={{0,2},{1,7},{2,0},{3,5},{4,6},{5,3},{6,4},{7,1},{8,10},{9,15},{10,... | collective-permute-start | bytes 331784 | tf_op jit(solution)/shard_map/ppermute | solution.py:354
  95.4 2.3 center.4.rest_ref
  97.7 2.7 %collective-permute-done.10.far_ref = bf16[9,16,384]{2,1,0:T(8,128)(2,1)S(1)} collective-permute-done((bf16[9,16,384]{2,1,0:T(8,128)(2,1)S(1)}, bf16[9,16,384]{2,1,0:T(8,128)(2,1)S(1)}, u32[]{:S(2)}, u32[]{:S(2)}) %collective-permute-start.10) | collective-permute-done | bytes 110624 | tf_op jit(solution)/shard_map/ppermute | solution.py:354
  100.4 3.5 %collective-permute-start.11 = (bf16[8,16,384]{2,1,0:T(8,128)(2,1)S(1)}, bf16[8,16,384]{2,1,0:T(8,128)(2,1)S(1)}, u32[]{:S(2)}, u32[]{:S(2)}) collective-permute-start(bf16[8,16,384]{2,1,0:T(8,128)(2,1)S(1)} %pair.5.near_ref), channel_id=1, source_target_pairs={{0,6},{1,3},{2,4},{3,1},{4,2},{5,7},{6,0},{7,5},{8,14},{9,11},{10,... | collective-permute-start | bytes 294920 | tf_op jit(solution)/shard_map/ppermute | solution.py:354
  103.9 9.9 %collective-permute-done.11.far_ref = bf16[8,16,384]{2,1,0:T(8,128)(2,1)S(1)} collective-permute-done((bf16[8,16,384]{2,1,0:T(8,128)(2,1)S(1)}, bf16[8,16,384]{2,1,0:T(8,128)(2,1)S(1)}, u32[]{:S(2)}, u32[]{:S(2)}) %collective-permute-start.11) | collective-permute-done | bytes 98336 | tf_op jit(solution)/shard_map/ppermute | solution.py:354
  113.8 0.1 last_update.1
  113.9 12.9 %all_gather.3 = f32[16,32,192]{2,1,0:T(8,128)S(1)} all-gather(f32[16,16,192]{2,1,0:T(8,128)S(1)} %last_update.1), channel_id=1, replica_groups=mesh['rows'=64,'aggs'=4,'vecs'=2] {'vecs'}, dimensions={1}, use_global_device_ids=true | all-gather | bytes 589824 | tf_op jit(solution)/shard_map/all_gather | solution.py:489
  126.8 0.6 fusion.16
  127.4 0.7 convolution_multiply_fusion.m_ref
  128.1 0.8 inverse_factor.1
  128.8 0.6 fusion.1
  129.5 0.4 fusion.15
  129.9 1.8 fit.1.near_ref
  131.7 5.3 %collective-permute-start.12 = (bf16[8,2,16,384]{3,2,1,0:T(8,128)(2,1)S(1)}, bf16[8,2,16,384]{3,2,1,0:T(8,128)(2,1)S(1)}, u32[]{:S(2)}, u32[]{:S(2)}) collective-permute-start(bf16[8,2,16,384]{3,2,1,0:T(8,128)(2,1)S(1)} %fit.1.near_ref), channel_id=1, source_target_pairs={{0,2},{1,7},{2,0},{3,5},{4,6},{5,3},{6,4},{7,1},{8,10},{9,15},{10,... | collective-permute-start | bytes 589832 | tf_op jit(solution)/shard_map/ppermute | solution.py:354
  137.0 10.3 %collective-permute-done.12.far_ref = bf16[8,2,16,384]{3,2,1,0:T(8,128)(2,1)S(1)} collective-permute-done((bf16[8,2,16,384]{3,2,1,0:T(8,128)(2,1)S(1)}, bf16[8,2,16,384]{3,2,1,0:T(8,128)(2,1)S(1)}, u32[]{:S(2)}, u32[]{:S(2)}) %collective-permute-start.12) | collective-permute-done | bytes 196640 | tf_op jit(solution)/shard_map/ppermute | solution.py:354
  147.3 1.1 slots.1.near_ref
  148.4 2.2 collective-permute-start.13
  150.6 2.3 center.5.rest_ref
  152.9 14.9 %collective-permute-done.13.far_ref = bf16[8,4,16,384]{3,2,1,0:T(8,128)(2,1)S(1)} collective-permute-done((bf16[8,4,16,384]{3,2,1,0:T(8,128)(2,1)S(1)}, bf16[8,4,16,384]{3,2,1,0:T(8,128)(2,1)S(1)}, u32[]{:S(2)}, u32[]{:S(2)}) %collective-permute-start.13) | collective-permute-done | bytes 393248 | tf_op jit(solution)/shard_map/ppermute | solution.py:354
  167.8 1.4 finish.1
  169.2 6.3 %collective-permute-start.16 = (bf16[8,4,16,384]{3,2,1,0:T(8,128)(2,1)S(1)}, bf16[8,4,16,384]{3,2,1,0:T(8,128)(2,1)S(1)}, u32[]{:S(2)}, u32[]{:S(2)}) collective-permute-start(bf16[8,4,16,384]{3,2,1,0:T(8,128)(2,1)S(1)} %get-tuple-element.21.own_ref), channel_id=1, source_target_pairs={{0,1},{1,0},{2,3},{3,2},{4,5},{5,4},{6,7},{7,6},{8,9},{9,8},{10,11... | collective-permute-start | bytes 1179656 | tf_op jit(solution)/shard_map/ppermute | solution.py:528
  175.5 1.9 collective-permute-start.15
  177.5 3.5 %collective-permute-start.14 = (bf16[8,4,16,384]{3,2,1,0:T(8,128)(2,1)S(1)}, bf16[8,4,16,384]{3,2,1,0:T(8,128)(2,1)S(1)}, u32[]{:S(2)}, u32[]{:S(2)}) collective-permute-start(bf16[8,4,16,384]{3,2,1,0:T(8,128)(2,1)S(1)} %get-tuple-element.21.own_ref), channel_id=1, source_target_pairs={{0,8},{8,16},{16,24},{24,32},{32,40},{40,48},{48,56},{56,64},{64,7... | collective-permute-start | bytes 1179656 | tf_op jit(solution)/shard_map/ppermute | solution.py:345
  181.1 7.1 %collective-permute-done.15.after_ref = bf16[8,4,16,384]{3,2,1,0:T(8,128)(2,1)S(1)} collective-permute-done((bf16[8,4,16,384]{3,2,1,0:T(8,128)(2,1)S(1)}, bf16[8,4,16,384]{3,2,1,0:T(8,128)(2,1)S(1)}, u32[]{:S(2)}, u32[]{:S(2)}) %collective-permute-start.15) | collective-permute-done | bytes 393248 | tf_op jit(solution)/shard_map/ppermute | solution.py:345
  188.2 4.0 %collective-permute-done.14.before_ref = bf16[8,4,16,384]{3,2,1,0:T(8,128)(2,1)S(1)} collective-permute-done((bf16[8,4,16,384]{3,2,1,0:T(8,128)(2,1)S(1)}, bf16[8,4,16,384]{3,2,1,0:T(8,128)(2,1)S(1)}, u32[]{:S(2)}, u32[]{:S(2)}) %collective-permute-start.14) | collective-permute-done | bytes 393248 | tf_op jit(solution)/shard_map/ppermute | solution.py:345
  192.2 5.2 %coarse.1 = (f32[2,96,256]{2,1,0:T(8,128)S(1)}, bf16[2,96,256]{2,1,0:T(8,128)(2,1)S(1)}) custom-call(s32[6]{0:T(128)S(1)} %stack.24.where_ref, s32[16,2]{1,0:T(8,128)S(1)} %broadcast_add_fusion.2.col_ref, s32[48,4]{1,0:T(8,128)S(1)} %pad_add_fusion.place_ref, bf16[16,192,384]{2,1,0:T(8,128)(2,1)S(1)} %stage.1.a_ref, bf16[16,192,192]{2,1,0:T(8,128)(2,1)} %diag_source_ref.1, ...), custom_call_target="tpu_custom_call" | custom-call | tf_op jit(solution)/shard_map/coarse/pallas_call | solution.py:368
  197.4 2.4 %collective-permute-start.17 = (bf16[2,96,256]{2,1,0:T(8,128)(2,1)S(1)}, bf16[2,96,256]{2,1,0:T(8,128)(2,1)S(1)}, u32[]{:S(2)}, u32[]{:S(2)}) collective-permute-start(bf16[2,96,256]{2,1,0:T(8,128)(2,1)S(1)} %get-tuple-element.23), channel_id=1, source_target_pairs={{0,2},{1,7},{2,0},{3,5},{4,6},{5,3},{6,4},{7,1},{8,10},{9,15},{10,... | collective-permute-start | bytes 294920 | tf_op jit(solution)/shard_map/ppermute | solution.py:354
  199.9 8.2 %collective-permute-done.17 = bf16[2,96,256]{2,1,0:T(8,128)(2,1)S(1)} collective-permute-done((bf16[2,96,256]{2,1,0:T(8,128)(2,1)S(1)}, bf16[2,96,256]{2,1,0:T(8,128)(2,1)S(1)}, u32[]{:S(2)}, u32[]{:S(2)}) %collective-permute-start.17) | collective-permute-done | bytes 98336 | tf_op jit(solution)/shard_map/ppermute | solution.py:354
  208.1 1.9 collective-permute-start.18
  210.1 6.8 %collective-permute-done.18 = bf16[96,256]{1,0:T(8,128)(2,1)S(1)} collective-permute-done((bf16[96,256]{1,0:T(8,128)(2,1)S(1)}, bf16[96,256]{1,0:T(8,128)(2,1)S(1)}, u32[]{:S(2)}, u32[]{:S(2)}) %collective-permute-start.18) | collective-permute-done | bytes 49184 | tf_op jit(solution)/shard_map/ppermute | solution.py:354
  216.9 6.4 %collective-permute-start.19 = (f32[96,128]{1,0:T(8,128)S(1)}, f32[96,128]{1,0:T(8,128)S(1)}, u32[]{:S(2)}, u32[]{:S(2)}) collective-permute-start(f32[96,128]{1,0:T(8,128)S(1)} %slice.50), channel_id=1, source_target_pairs={{0,1},{1,0},{2,3},{3,2},{4,5},{5,4},{6,7},{7,6},{8,9},{9,8},{10,11... | collective-permute-start | bytes 147464 | tf_op jit(solution)/shard_map/ppermute | solution.py:558
  223.3 0.9 collective-permute-done.19
  224.2 0.2 concatenate.20
  224.4 0.2 copy.49
  224.6 0.2 concatenate.21
  224.7 0.2 copy.50
  224.9 0.9 maximum_bitcast_fusion
  (43 shorter events, 1.0 us)
Async XLA Ops:
  0.6 1.0 copy-start
  1.7 10.2 %collective-permute-start.1 = (bf16[8,16,384]{2,1,0:T(8,128)(2,1)S(1)}, bf16[8,16,384]{2,1,0:T(8,128)(2,1)S(1)}, u32[]{:S(2)}, u32[]{:S(2)}) collective-permute-start(bf16[8,16,384]{2,1,0:T(8,128)(2,1)S(1)} %fold.1.own_ref), channel_id=1, source_target_pairs={{8,0},{16,8},{24,16},{32,24},{40,32},{48,40},{56,48},{64,56},{72,6... | collective-permute-start | bytes 294920 | tf_op jit(solution)/shard_map/ppermute | solution.py:345
  6.3 7.5 %collective-permute-start = (bf16[8,16,384]{2,1,0:T(8,128)(2,1)S(1)}, bf16[8,16,384]{2,1,0:T(8,128)(2,1)S(1)}, u32[]{:S(2)}, u32[]{:S(2)}) collective-permute-start(bf16[8,16,384]{2,1,0:T(8,128)(2,1)S(1)} %fold.1.own_ref), channel_id=1, source_target_pairs={{0,8},{8,16},{16,24},{24,32},{32,40},{40,48},{48,56},{56,64},{64,7... | collective-permute-start | bytes 294920 | tf_op jit(solution)/shard_map/ppermute | solution.py:345
  11.8 16.1 %copy-start.2 = (s32[16]{0:T(128)S(1)}, s32[16]{0:T(128)}, u32[]{:S(2)}) copy-start(s32[16]{0:T(128)} %param.9) | copy-start | bytes 196
  11.9 16.2 %copy-start.1 = (f32[16,16,192]{2,1,0:T(8,128)S(1)}, f32[16,16,192]{2,1,0:T(8,128)}, u32[]{:S(2)}) copy-start(f32[16,16,192]{2,1,0:T(8,128)} %x_ref.3) | copy-start | bytes 589828
  15.5 17.2 %collective-permute-start.2 = (bf16[8,16,384]{2,1,0:T(8,128)(2,1)S(1)}, bf16[8,16,384]{2,1,0:T(8,128)(2,1)S(1)}, u32[]{:S(2)}, u32[]{:S(2)}) collective-permute-start(bf16[8,16,384]{2,1,0:T(8,128)(2,1)S(1)} %couple.3.near_ref), channel_id=1, source_target_pairs={{0,2},{1,7},{2,0},{3,5},{4,6},{5,3},{6,4},{7,1},{8,10},{9,15},{10,... | collective-permute-start | bytes 294920 | tf_op jit(solution)/shard_map/ppermute | solution.py:354
  32.7 12.2 %collective-permute-start.3 = (bf16[8,16,384]{2,1,0:T(8,128)(2,1)S(1)}, bf16[8,16,384]{2,1,0:T(8,128)(2,1)S(1)}, u32[]{:S(2)}, u32[]{:S(2)}) collective-permute-start(bf16[8,16,384]{2,1,0:T(8,128)(2,1)S(1)} %pair.3.near_ref), channel_id=1, source_target_pairs={{0,6},{1,3},{2,4},{3,1},{4,2},{5,7},{6,0},{7,5},{8,14},{9,11},{10,... | collective-permute-start | bytes 294920 | tf_op jit(solution)/shard_map/ppermute | solution.py:354
  44.9 5.6 %collective-permute-start.5 = (bf16[9,16,384]{2,1,0:T(8,128)(2,1)S(1)}, bf16[9,16,384]{2,1,0:T(8,128)(2,1)S(1)}, u32[]{:S(2)}, u32[]{:S(2)}) collective-permute-start(bf16[9,16,384]{2,1,0:T(8,128)(2,1)S(1)} %get-tuple-element.17.own_ref), channel_id=1, source_target_pairs={{8,0},{16,8},{24,16},{32,24},{40,32},{48,40},{56,48},{64,56},{72,6... | collective-permute-start | bytes 331784 | tf_op jit(solution)/shard_map/ppermute | solution.py:345
  48.5 7.6 %collective-permute-start.4 = (bf16[9,16,384]{2,1,0:T(8,128)(2,1)S(1)}, bf16[9,16,384]{2,1,0:T(8,128)(2,1)S(1)}, u32[]{:S(2)}, u32[]{:S(2)}) collective-permute-start(bf16[9,16,384]{2,1,0:T(8,128)(2,1)S(1)} %get-tuple-element.17.own_ref), channel_id=1, source_target_pairs={{0,8},{8,16},{16,24},{24,32},{32,40},{40,48},{48,56},{56,64},{64,7... | collective-permute-start | bytes 331784 | tf_op jit(solution)/shard_map/ppermute | solution.py:345
  57.8 9.3 %collective-permute-start.6 = (bf16[8,16,384]{2,1,0:T(8,128)(2,1)S(1)}, bf16[8,16,384]{2,1,0:T(8,128)(2,1)S(1)}, u32[]{:S(2)}, u32[]{:S(2)}) collective-permute-start(bf16[8,16,384]{2,1,0:T(8,128)(2,1)S(1)} %couple.4.near_ref), channel_id=1, source_target_pairs={{0,2},{1,7},{2,0},{3,5},{4,6},{5,3},{6,4},{7,1},{8,10},{9,15},{10,... | collective-permute-start | bytes 294920 | tf_op jit(solution)/shard_map/ppermute | solution.py:354
  67.1 12.3 %collective-permute-start.7 = (bf16[8,16,384]{2,1,0:T(8,128)(2,1)S(1)}, bf16[8,16,384]{2,1,0:T(8,128)(2,1)S(1)}, u32[]{:S(2)}, u32[]{:S(2)}) collective-permute-start(bf16[8,16,384]{2,1,0:T(8,128)(2,1)S(1)} %pair.4.near_ref), channel_id=1, source_target_pairs={{0,6},{1,3},{2,4},{3,1},{4,2},{5,7},{6,0},{7,5},{8,14},{9,11},{10,... | collective-permute-start | bytes 294920 | tf_op jit(solution)/shard_map/ppermute | solution.py:354
  79.5 5.4 %collective-permute-start.9 = (bf16[8,16,384]{2,1,0:T(8,128)(2,1)S(1)}, bf16[8,16,384]{2,1,0:T(8,128)(2,1)S(1)}, u32[]{:S(2)}, u32[]{:S(2)}) collective-permute-start(bf16[8,16,384]{2,1,0:T(8,128)(2,1)S(1)} %get-tuple-element.19.own_ref), channel_id=1, source_target_pairs={{8,0},{16,8},{24,16},{32,24},{40,32},{48,40},{56,48},{64,56},{72,6... | collective-permute-start | bytes 294920 | tf_op jit(solution)/shard_map/ppermute | solution.py:345
  81.4 7.8 %collective-permute-start.8 = (bf16[8,16,384]{2,1,0:T(8,128)(2,1)S(1)}, bf16[8,16,384]{2,1,0:T(8,128)(2,1)S(1)}, u32[]{:S(2)}, u32[]{:S(2)}) collective-permute-start(bf16[8,16,384]{2,1,0:T(8,128)(2,1)S(1)} %get-tuple-element.19.own_ref), channel_id=1, source_target_pairs={{0,8},{8,16},{16,24},{24,32},{32,40},{40,48},{48,56},{56,64},{64,7... | collective-permute-start | bytes 294920 | tf_op jit(solution)/shard_map/ppermute | solution.py:345
  90.9 9.4 %collective-permute-start.10 = (bf16[9,16,384]{2,1,0:T(8,128)(2,1)S(1)}, bf16[9,16,384]{2,1,0:T(8,128)(2,1)S(1)}, u32[]{:S(2)}, u32[]{:S(2)}) collective-permute-start(bf16[9,16,384]{2,1,0:T(8,128)(2,1)S(1)} %couple.5.near_ref), channel_id=1, source_target_pairs={{0,2},{1,7},{2,0},{3,5},{4,6},{5,3},{6,4},{7,1},{8,10},{9,15},{10,... | collective-permute-start | bytes 331784 | tf_op jit(solution)/shard_map/ppermute | solution.py:354
  100.4 13.4 %collective-permute-start.11 = (bf16[8,16,384]{2,1,0:T(8,128)(2,1)S(1)}, bf16[8,16,384]{2,1,0:T(8,128)(2,1)S(1)}, u32[]{:S(2)}, u32[]{:S(2)}) collective-permute-start(bf16[8,16,384]{2,1,0:T(8,128)(2,1)S(1)} %pair.5.near_ref), channel_id=1, source_target_pairs={{0,6},{1,3},{2,4},{3,1},{4,2},{5,7},{6,0},{7,5},{8,14},{9,11},{10,... | collective-permute-start | bytes 294920 | tf_op jit(solution)/shard_map/ppermute | solution.py:354
  131.7 15.7 %collective-permute-start.12 = (bf16[8,2,16,384]{3,2,1,0:T(8,128)(2,1)S(1)}, bf16[8,2,16,384]{3,2,1,0:T(8,128)(2,1)S(1)}, u32[]{:S(2)}, u32[]{:S(2)}) collective-permute-start(bf16[8,2,16,384]{3,2,1,0:T(8,128)(2,1)S(1)} %fit.1.near_ref), channel_id=1, source_target_pairs={{0,2},{1,7},{2,0},{3,5},{4,6},{5,3},{6,4},{7,1},{8,10},{9,15},{10,... | collective-permute-start | bytes 589832 | tf_op jit(solution)/shard_map/ppermute | solution.py:354
  148.4 19.4 %collective-permute-start.13 = (bf16[8,4,16,384]{3,2,1,0:T(8,128)(2,1)S(1)}, bf16[8,4,16,384]{3,2,1,0:T(8,128)(2,1)S(1)}, u32[]{:S(2)}, u32[]{:S(2)}) collective-permute-start(bf16[8,4,16,384]{3,2,1,0:T(8,128)(2,1)S(1)} %slots.1.near_ref), channel_id=1, source_target_pairs={{0,6},{1,3},{2,4},{3,1},{4,2},{5,7},{6,0},{7,5},{8,14},{9,11},{10,... | collective-permute-start | bytes 1179656 | tf_op jit(solution)/shard_map/ppermute | solution.py:354
  169.2 11.8 %collective-permute-start.16 = (bf16[8,4,16,384]{3,2,1,0:T(8,128)(2,1)S(1)}, bf16[8,4,16,384]{3,2,1,0:T(8,128)(2,1)S(1)}, u32[]{:S(2)}, u32[]{:S(2)}) collective-permute-start(bf16[8,4,16,384]{3,2,1,0:T(8,128)(2,1)S(1)} %get-tuple-element.21.own_ref), channel_id=1, source_target_pairs={{0,1},{1,0},{2,3},{3,2},{4,5},{5,4},{6,7},{7,6},{8,9},{9,8},{10,11... | collective-permute-start | bytes 1179656 | tf_op jit(solution)/shard_map/ppermute | solution.py:528
  175.5 12.6 %collective-permute-start.15 = (bf16[8,4,16,384]{3,2,1,0:T(8,128)(2,1)S(1)}, bf16[8,4,16,384]{3,2,1,0:T(8,128)(2,1)S(1)}, u32[]{:S(2)}, u32[]{:S(2)}) collective-permute-start(bf16[8,4,16,384]{3,2,1,0:T(8,128)(2,1)S(1)} %get-tuple-element.21.own_ref), channel_id=1, source_target_pairs={{8,0},{16,8},{24,16},{32,24},{40,32},{48,40},{56,48},{64,56},{72,6... | collective-permute-start | bytes 1179656 | tf_op jit(solution)/shard_map/ppermute | solution.py:345
  177.5 14.7 %collective-permute-start.14 = (bf16[8,4,16,384]{3,2,1,0:T(8,128)(2,1)S(1)}, bf16[8,4,16,384]{3,2,1,0:T(8,128)(2,1)S(1)}, u32[]{:S(2)}, u32[]{:S(2)}) collective-permute-start(bf16[8,4,16,384]{3,2,1,0:T(8,128)(2,1)S(1)} %get-tuple-element.21.own_ref), channel_id=1, source_target_pairs={{0,8},{8,16},{16,24},{24,32},{32,40},{40,48},{48,56},{56,64},{64,7... | collective-permute-start | bytes 1179656 | tf_op jit(solution)/shard_map/ppermute | solution.py:345
  197.4 10.7 %collective-permute-start.17 = (bf16[2,96,256]{2,1,0:T(8,128)(2,1)S(1)}, bf16[2,96,256]{2,1,0:T(8,128)(2,1)S(1)}, u32[]{:S(2)}, u32[]{:S(2)}) collective-permute-start(bf16[2,96,256]{2,1,0:T(8,128)(2,1)S(1)} %get-tuple-element.23), channel_id=1, source_target_pairs={{0,2},{1,7},{2,0},{3,5},{4,6},{5,3},{6,4},{7,1},{8,10},{9,15},{10,... | collective-permute-start | bytes 294920 | tf_op jit(solution)/shard_map/ppermute | solution.py:354
  208.1 8.8 %collective-permute-start.18 = (bf16[96,256]{1,0:T(8,128)(2,1)S(1)}, bf16[96,256]{1,0:T(8,128)(2,1)S(1)}, u32[]{:S(2)}, u32[]{:S(2)}) collective-permute-start(bf16[96,256]{1,0:T(8,128)(2,1)S(1)} %fusion.6), channel_id=1, source_target_pairs={{0,6},{1,3},{2,4},{3,1},{4,2},{5,7},{6,0},{7,5},{8,14},{9,11},{10,... | collective-permute-start | bytes 147464 | tf_op jit(solution)/shard_map/ppermute | solution.py:354
  216.9 7.3 %collective-permute-start.19 = (f32[96,128]{1,0:T(8,128)S(1)}, f32[96,128]{1,0:T(8,128)S(1)}, u32[]{:S(2)}, u32[]{:S(2)}) collective-permute-start(f32[96,128]{1,0:T(8,128)S(1)} %slice.50), channel_id=1, source_target_pairs={{0,1},{1,0},{2,3},{3,2},{4,5},{5,4},{6,7},{7,6},{8,9},{9,8},{10,11... | collective-permute-start | bytes 147464 | tf_op jit(solution)/shard_map/ppermute | solution.py:558

commit v5 on v4

--- a/solution.py
+++ b/solution.py
@@ -237,20 +237,21 @@
             out_ref[m, p] = total.astype(BF16)
 
 
-def finish_kernel(where_ref, rest_ref, near_ref, far_ref, scale_ref, out_ref, here_ref):
-    half = rest_ref.shape[0]
-    slot = where_ref[1]
-    for m in range(half):
+def finish_kernel(rest_ref, near_ref, far_ref, scale_ref, out_ref):
+    for m in range(rest_ref.shape[0]):
         scale = scale_ref[m : m + 1, :]
-        here = jnp.zeros(rest_ref.shape[1:], F32)
         for p in range(SLOTS):
             total = near_ref[m, p].astype(F32) + far_ref[m, p].astype(F32)
             value = -scale * total
             if p == 0:
                 value = rest_ref[m] + value
             out_ref[m, p] = value.astype(BF16)
-            here = jnp.where(slot == p, value, here)
-        take_into(here_ref.at[m, 0], here_ref.at[half + m, 0], here.astype(BF16))
+
+
+def here_kernel(where_ref, prolong_ref, here_ref):
+    half = prolong_ref.shape[0]
+    for m in range(half):
+        take_into(here_ref.at[m, 0], here_ref.at[half + m, 0], prolong_ref[m, where_ref[1]])
 
 
 def inverse_factor_kernel(m_ref, out_ref):
@@ -275,7 +276,7 @@
     vectors = own_ref.shape[2]
     share = rows // 4
     slot = where_ref[1]
-    span = reach.shape[1]
+    span = reach.shape[0]
     diag_copy = pltpu.make_async_copy(
         diag_source_ref.at[pl.ds(slot * share, share)], diag_ref, diag_sem.at[0]
     )
@@ -293,42 +294,61 @@
 
     span_rows = SLOTS * vectors
 
-    def add(i, row, image):
-        for q in range(SLOTS):
-            at = place_ref[row, q]
-            reach[i, at] = reach[i, at] + image[q * vectors : (q + 1) * vectors]
-
-    for m in range(half):
+    def add(lanes, row, image, fresh):
+        places = [place_ref[row, q] for q in range(SLOTS)]
+        zero = jnp.zeros((span_rows, 2 * LANES - width), F32)
+        image = jnp.concatenate([image, zero], axis=1)
+        blocks = [image[q * vectors : (q + 1) * vectors] for q in range(SLOTS)]
+        if not fresh:
+            held_now = [reach[at, :, lanes] for at in places]
+            blocks = [block + now for block, now in zip(blocks, held_now)]
+        for at, block in zip(places, blocks):
+            reach[at, :, lanes] = block
+
+    def lanes_of(i):
+        if isinstance(i, int):
+            return slice(i * 2 * LANES, (i + 1) * 2 * LANES)
+        return pl.ds(pl.multiple_of(i * 2 * LANES, LANES), 2 * LANES)
+
+    for m in range(half):
+        low_lanes, high_lanes = lanes_of(m), lanes_of(half + m)
         for p in range(SLOTS):
             first = place_ref[rows + m, p] - SLAB_AGGS
             second = place_ref[rows + half + m, p] - SLAB_AGGS
-            for side, ref in enumerate((own_ref, other_ref)):
-                take_into(left.at[m, side, first], left.at[half + m, side, second], ref[m, p])
-    for m in range(half):
-        for i in (m, half + m):
-            first, second = col_ref[i, 0], col_ref[i, 1]
-            images = dot_nt(
-                stacked(
-                    low[first].reshape(span_rows, 2 * LANES),
-                    high[second].reshape(span_rows, 2 * LANES),
-                ),
-                a_ref[i],
+            left[0, first, :, low_lanes] = low[rows + m, p]
+            left[0, second, :, high_lanes] = low[rows + half + m, p]
+            block = other_ref[m, p]
+            zero = jnp.zeros((vectors, 2 * LANES - width), BF16)
+            left[1, first, :, low_lanes] = jnp.concatenate([block[:, :width], zero], axis=1)
+            left[1, second, :, high_lanes] = jnp.concatenate(
+                [block[:, 2 * width - LANES :], block[:, width : 2 * width - LANES], zero], axis=1
             )
-            add(i, first, images[:span_rows])
-            add(i, second, images[span_rows:])
+    for i in range(rows):
+        first, second = col_ref[i, 0], col_ref[i, 1]
+        images = dot_nt(
+            stacked(
+                low[first].reshape(span_rows, 2 * LANES),
+                high[second].reshape(span_rows, 2 * LANES),
+            ),
+            a_ref[i],
+        )
+        add(lanes_of(i), first, images[:span_rows], True)
+        add(lanes_of(i), second, images[span_rows:], False)
 
     diag_copy.wait()
     for r in range(share):
         i = slot * share + r
         own = low[rows + i].reshape(span_rows, 2 * LANES)[:, :width]
-        add(i, rows + i, dot_nt(own, diag_ref[r]))
-
-    for i in range(rows):
+        add(lanes_of(i), rows + i, dot_nt(own, diag_ref[r]), False)
+
+    depth = 4 * 2 * LANES
+    for c in range(rows // 4):
+        lanes = slice(c * depth, (c + 1) * depth)
         product = dot_nt(
-            reach[i].astype(BF16).reshape(span * vectors, width),
-            left[i].reshape(2 * SLAB_AGGS * vectors, width),
+            reach[:, :, lanes].astype(BF16).reshape(span * vectors, depth),
+            left[:, :, :, lanes].reshape(2 * SLAB_AGGS * vectors, depth),
         )
-        if i == 0:
+        if c == 0:
             total[...] = product
         else:
             total[...] = total[...] + product
@@ -518,11 +538,14 @@
     pair = kernel_call(
         slot_kernel, "slots", slots_shape, [near_slot, far_slot, moved, exchange(moved, 0)]
     )
-    prolong, prolong_here = kernel_call(
-        finish_kernel,
-        "finish",
-        [slots_shape, jax.ShapeDtypeStruct((rows, 1, vectors, width), BF16)],
-        [where, rest, pair, exchange(pair, 1), folded_scale],
+    prolong = kernel_call(
+        finish_kernel, "finish", slots_shape, [rest, pair, exchange(pair, 1), folded_scale]
+    )
+    prolong_here = kernel_call(
+        here_kernel,
+        "here",
+        jax.ShapeDtypeStruct((rows, 1, vectors, width), BF16),
+        [where, prolong],
     )
 
     other = lax.ppermute(prolong, "vecs", [(0, 1), (1, 0)])
@@ -542,8 +565,8 @@
         [
             pltpu.VMEM((3 * rows, SLOTS, vectors, 2 * LANES), BF16),
             pltpu.VMEM((3 * rows, SLOTS, vectors, 2 * LANES), BF16),
-            pltpu.VMEM((rows, span, vectors, width), F32),
-            pltpu.VMEM((rows, 2, SLAB_AGGS, vectors, width), BF16),
+            pltpu.VMEM((span, vectors, rows * 2 * LANES), F32),
+            pltpu.VMEM((2, SLAB_AGGS, vectors, rows * 2 * LANES), BF16),
             pltpu.VMEM((span * vectors, wide), F32),
         ]
         + [

time: 227 us -> 221 us (0.974)
  the two profiles are of different devices: /device:TPU:3 before, /device:TPU:31 now
where the time goes in v5:
time: 221 us; the launch traced here: 220 us
  starting transfers between devices  102 us (46%)
  waiting for transfers between devices  74.1 us (34%)
  Pallas kernels  26.8 us (12%)
  blocking collectives  8.54 us (4%)
  other arithmetic  2.66 us (1%)
  matrix products  2.34 us (1%)
    ppermute x10, starting transfers between devices, exchange(): return lax.ppermute(x, ('aggs', 'vecs'), pairs)  61.9 us
    ppermute x10, waiting for transfers between devices, exchange(): return lax.ppermute(x, ('aggs', 'vecs'), pairs)  51.5 us
    pallas_call x20, Pallas kernels, kernel_call(): pl.pallas_call(body, out_shape=shapes, in_specs=specs, out_specs=[VMEM_SP...  24.7 us
    ppermute x8, starting transfers between devices, shift(): lax.ppermute(x, 'rows', [(i, i + by) for i in range(size) if 0 <= i + by...  24.4 us
    ppermute x8, waiting for transfers between devices, shift(): lax.ppermute(x, 'rows', [(i, i + by) for i in range(size) if 0 <= i + by...  22.6 us
    ppermute x1, starting transfers between devices, on_device(): theirs = lax.ppermute(theirs, 'vecs', [(0, 1), (1, 0)])  10.6 us
    all_gather x1, blocking collectives, on_device(): every = lax.all_gather(current, 'vecs', axis=1, tiled=True)  8.54 us
    ppermute x1, starting transfers between devices, on_device(): other = lax.ppermute(prolong, 'vecs', [(0, 1), (1, 0)])  5.49 us
  transfers between devices with their start and end apart: 20, of which 14 were waited for; matrix products, arithmetic and copies ran while one was open for 1% of the time, Pallas kernels for 6%

profile of v5, /device:TPU:31, one launch (start us, length us, event | category | flops | bytes accessed | tf_op | source)
XLA Modules:
  0.0 220.1 jit_solution(393896637727073950)
XLA Ops:
  0.6 0.9 copy-done
  1.7 3.1 %collective-permute-start = (bf16[8,16,384]{2,1,0:T(8,128)(2,1)S(1)}, bf16[8,16,384]{2,1,0:T(8,128)(2,1)S(1)}, u32[]{:S(2)}, u32[]{:S(2)}) collective-permute-start(bf16[8,16,384]{2,1,0:T(8,128)(2,1)S(1)} %fold.1.own_ref), channel_id=1, source_target_pairs={{0,8},{8,16},{16,24},{24,32},{32,40},{40,48},{48,56},{56,64},{64,7... | collective-permute-start | bytes 294920 | tf_op jit(solution)/shard_map/ppermute | solution.py:365
  4.8 2.2 collective-permute-start.1
  7.0 0.7 broadcast_subtract_fusion.1
  7.7 0.7 pad_add_fusion.1
  8.5 2.1 stage.1.a_ref
  10.6 3.7 %collective-permute-done.1.after_ref = bf16[8,16,384]{2,1,0:T(8,128)(2,1)S(1)} collective-permute-done((bf16[8,16,384]{2,1,0:T(8,128)(2,1)S(1)}, bf16[8,16,384]{2,1,0:T(8,128)(2,1)S(1)}, u32[]{:S(2)}, u32[]{:S(2)}) %collective-permute-start.1) | collective-permute-done | bytes 98336 | tf_op jit(solution)/shard_map/ppermute | solution.py:365
  14.4 1.7 couple.3.near_ref
  16.1 11.6 %collective-permute-start.2 = (bf16[8,16,384]{2,1,0:T(8,128)(2,1)S(1)}, bf16[8,16,384]{2,1,0:T(8,128)(2,1)S(1)}, u32[]{:S(2)}, u32[]{:S(2)}) collective-permute-start(bf16[8,16,384]{2,1,0:T(8,128)(2,1)S(1)} %couple.3.near_ref), channel_id=1, source_target_pairs={{0,2},{1,7},{2,0},{3,5},{4,6},{5,3},{6,4},{7,1},{8,10},{9,15},{10,... | collective-permute-start | bytes 294920 | tf_op jit(solution)/shard_map/ppermute | solution.py:374
  27.8 2.2 first_center.1
  30.0 0.4 collective-permute-done.2.far_ref
  30.3 7.4 %collective-permute-start.3 = (bf16[8,16,384]{2,1,0:T(8,128)(2,1)S(1)}, bf16[8,16,384]{2,1,0:T(8,128)(2,1)S(1)}, u32[]{:S(2)}, u32[]{:S(2)}) collective-permute-start(bf16[8,16,384]{2,1,0:T(8,128)(2,1)S(1)} %pair.3.near_ref), channel_id=1, source_target_pairs={{0,6},{1,3},{2,4},{3,1},{4,2},{5,7},{6,0},{7,5},{8,14},{9,11},{10,... | collective-permute-start | bytes 294920 | tf_op jit(solution)/shard_map/ppermute | solution.py:374
  37.7 0.2 select_reduce_fusion
  37.9 3.0 %collective-permute-done.3.far_ref = bf16[8,16,384]{2,1,0:T(8,128)(2,1)S(1)} collective-permute-done((bf16[8,16,384]{2,1,0:T(8,128)(2,1)S(1)}, bf16[8,16,384]{2,1,0:T(8,128)(2,1)S(1)}, u32[]{:S(2)}, u32[]{:S(2)}) %collective-permute-start.3) | collective-permute-done | bytes 98336 | tf_op jit(solution)/shard_map/ppermute | solution.py:374
  40.9 6.6 %collective-permute-start.4 = (bf16[9,16,384]{2,1,0:T(8,128)(2,1)S(1)}, bf16[9,16,384]{2,1,0:T(8,128)(2,1)S(1)}, u32[]{:S(2)}, u32[]{:S(2)}) collective-permute-start(bf16[9,16,384]{2,1,0:T(8,128)(2,1)S(1)} %get-tuple-element.15.own_ref), channel_id=1, source_target_pairs={{0,8},{8,16},{16,24},{24,32},{32,40},{40,48},{48,56},{56,64},{64,7... | collective-permute-start | bytes 331784 | tf_op jit(solution)/shard_map/ppermute | solution.py:365
  47.5 1.9 collective-permute-start.5
  49.5 7.7 %collective-permute-done.5.after_ref = bf16[9,16,384]{2,1,0:T(8,128)(2,1)S(1)} collective-permute-done((bf16[9,16,384]{2,1,0:T(8,128)(2,1)S(1)}, bf16[9,16,384]{2,1,0:T(8,128)(2,1)S(1)}, u32[]{:S(2)}, u32[]{:S(2)}) %collective-permute-start.5) | collective-permute-done | bytes 110624 | tf_op jit(solution)/shard_map/ppermute | solution.py:365
  57.2 1.7 couple.4.near_ref
  58.9 4.8 %collective-permute-start.6 = (bf16[8,16,384]{2,1,0:T(8,128)(2,1)S(1)}, bf16[8,16,384]{2,1,0:T(8,128)(2,1)S(1)}, u32[]{:S(2)}, u32[]{:S(2)}) collective-permute-start(bf16[8,16,384]{2,1,0:T(8,128)(2,1)S(1)} %couple.4.near_ref), channel_id=1, source_target_pairs={{0,2},{1,7},{2,0},{3,5},{4,6},{5,3},{6,4},{7,1},{8,10},{9,15},{10,... | collective-permute-start | bytes 294920 | tf_op jit(solution)/shard_map/ppermute | solution.py:374
  63.7 5.5 %collective-permute-done.6.far_ref = bf16[8,16,384]{2,1,0:T(8,128)(2,1)S(1)} collective-permute-done((bf16[8,16,384]{2,1,0:T(8,128)(2,1)S(1)}, bf16[8,16,384]{2,1,0:T(8,128)(2,1)S(1)}, u32[]{:S(2)}, u32[]{:S(2)}) %collective-permute-start.6) | collective-permute-done | bytes 98336 | tf_op jit(solution)/shard_map/ppermute | solution.py:374
  69.3 3.7 %collective-permute-start.7 = (bf16[8,16,384]{2,1,0:T(8,128)(2,1)S(1)}, bf16[8,16,384]{2,1,0:T(8,128)(2,1)S(1)}, u32[]{:S(2)}, u32[]{:S(2)}) collective-permute-start(bf16[8,16,384]{2,1,0:T(8,128)(2,1)S(1)} %pair.4.near_ref), channel_id=1, source_target_pairs={{0,6},{1,3},{2,4},{3,1},{4,2},{5,7},{6,0},{7,5},{8,14},{9,11},{10,... | collective-permute-start | bytes 294920 | tf_op jit(solution)/shard_map/ppermute | solution.py:374
  73.1 0.1 copy.42
  73.2 2.3 %center.3.rest_ref = f32[8,16,384]{2,1,0:T(8,128)S(1)} custom-call(bf16[16,192,192]{2,1,0:T(8,128)(2,1)} %diag_source_ref.1, f32[8,16,384]{2,1,0:T(8,128)S(1)} %get-tuple-element.13.x_ref, f32[16,192]{1,0:T(8,128)S(1)} %get-tuple-element.14.scale_ref), custom_call_target="tpu_custom_call" | custom-call | tf_op jit(solution)/shard_map/center/pallas_call | solution.py:388
  75.4 3.5 %collective-permute-done.7.far_ref = bf16[8,16,384]{2,1,0:T(8,128)(2,1)S(1)} collective-permute-done((bf16[8,16,384]{2,1,0:T(8,128)(2,1)S(1)}, bf16[8,16,384]{2,1,0:T(8,128)(2,1)S(1)}, u32[]{:S(2)}, u32[]{:S(2)}) %collective-permute-start.7) | collective-permute-done | bytes 98336 | tf_op jit(solution)/shard_map/ppermute | solution.py:374
  79.0 1.9 collective-permute-start.8
  80.9 3.4 %collective-permute-start.9 = (bf16[8,16,384]{2,1,0:T(8,128)(2,1)S(1)}, bf16[8,16,384]{2,1,0:T(8,128)(2,1)S(1)}, u32[]{:S(2)}, u32[]{:S(2)}) collective-permute-start(bf16[8,16,384]{2,1,0:T(8,128)(2,1)S(1)} %get-tuple-element.17.own_ref), channel_id=1, source_target_pairs={{8,0},{16,8},{24,16},{32,24},{40,32},{48,40},{56,48},{64,56},{72,6... | collective-permute-start | bytes 294920 | tf_op jit(solution)/shard_map/ppermute | solution.py:365
  84.3 6.1 %collective-permute-done.9.after_ref = bf16[8,16,384]{2,1,0:T(8,128)(2,1)S(1)} collective-permute-done((bf16[8,16,384]{2,1,0:T(8,128)(2,1)S(1)}, bf16[8,16,384]{2,1,0:T(8,128)(2,1)S(1)}, u32[]{:S(2)}, u32[]{:S(2)}) %collective-permute-start.9) | collective-permute-done | bytes 98336 | tf_op jit(solution)/shard_map/ppermute | solution.py:365
  90.5 1.7 couple.5.near_ref
  92.2 5.1 %collective-permute-start.10 = (bf16[9,16,384]{2,1,0:T(8,128)(2,1)S(1)}, bf16[9,16,384]{2,1,0:T(8,128)(2,1)S(1)}, u32[]{:S(2)}, u32[]{:S(2)}) collective-permute-start(bf16[9,16,384]{2,1,0:T(8,128)(2,1)S(1)} %couple.5.near_ref), channel_id=1, source_target_pairs={{0,2},{1,7},{2,0},{3,5},{4,6},{5,3},{6,4},{7,1},{8,10},{9,15},{10,... | collective-permute-start | bytes 331784 | tf_op jit(solution)/shard_map/ppermute | solution.py:374
  97.4 2.3 %center.4.rest_ref = f32[8,16,384]{2,1,0:T(8,128)S(1)} custom-call(bf16[16,192,192]{2,1,0:T(8,128)(2,1)} %diag_source_ref.1, f32[8,16,384]{2,1,0:T(8,128)S(1)} %get-tuple-element.16.x_ref, f32[16,192]{1,0:T(8,128)S(1)} %get-tuple-element.14.scale_ref), custom_call_target="tpu_custom_call" | custom-call | tf_op jit(solution)/shard_map/center/pallas_call | solution.py:388
  99.7 1.9 collective-permute-done.10.far_ref
  101.6 4.0 %collective-permute-start.11 = (bf16[8,16,384]{2,1,0:T(8,128)(2,1)S(1)}, bf16[8,16,384]{2,1,0:T(8,128)(2,1)S(1)}, u32[]{:S(2)}, u32[]{:S(2)}) collective-permute-start(bf16[8,16,384]{2,1,0:T(8,128)(2,1)S(1)} %pair.5.near_ref), channel_id=1, source_target_pairs={{0,6},{1,3},{2,4},{3,1},{4,2},{5,7},{6,0},{7,5},{8,14},{9,11},{10,... | collective-permute-start | bytes 294920 | tf_op jit(solution)/shard_map/ppermute | solution.py:374
  105.6 8.7 %collective-permute-done.11.far_ref = bf16[8,16,384]{2,1,0:T(8,128)(2,1)S(1)} collective-permute-done((bf16[8,16,384]{2,1,0:T(8,128)(2,1)S(1)}, bf16[8,16,384]{2,1,0:T(8,128)(2,1)S(1)}, u32[]{:S(2)}, u32[]{:S(2)}) %collective-permute-start.11) | collective-permute-done | bytes 98336 | tf_op jit(solution)/shard_map/ppermute | solution.py:374
  114.3 0.1 last_update.1
  114.4 8.5 %all_gather.3 = f32[16,32,192]{2,1,0:T(8,128)S(1)} all-gather(f32[16,16,192]{2,1,0:T(8,128)S(1)} %last_update.1), channel_id=1, replica_groups=mesh['rows'=64,'aggs'=4,'vecs'=2] {'vecs'}, dimensions={1}, use_global_device_ids=true | all-gather | bytes 589824 | tf_op jit(solution)/shard_map/all_gather | solution.py:509
  123.0 0.6 fusion.16
  123.6 0.7 convolution_multiply_fusion.m_ref
  124.3 0.8 inverse_factor.1
  125.0 0.6 fusion.1
  125.7 0.4 fusion.15
  126.1 1.8 fit.1.near_ref
  127.9 7.6 %collective-permute-start.12 = (bf16[8,2,16,384]{3,2,1,0:T(8,128)(2,1)S(1)}, bf16[8,2,16,384]{3,2,1,0:T(8,128)(2,1)S(1)}, u32[]{:S(2)}, u32[]{:S(2)}) collective-permute-start(bf16[8,2,16,384]{3,2,1,0:T(8,128)(2,1)S(1)} %fit.1.near_ref), channel_id=1, source_target_pairs={{0,2},{1,7},{2,0},{3,5},{4,6},{5,3},{6,4},{7,1},{8,10},{9,15},{10,... | collective-permute-start | bytes 589832 | tf_op jit(solution)/shard_map/ppermute | solution.py:374
  135.5 6.6 %collective-permute-done.12.far_ref = bf16[8,2,16,384]{3,2,1,0:T(8,128)(2,1)S(1)} collective-permute-done((bf16[8,2,16,384]{3,2,1,0:T(8,128)(2,1)S(1)}, bf16[8,2,16,384]{3,2,1,0:T(8,128)(2,1)S(1)}, u32[]{:S(2)}, u32[]{:S(2)}) %collective-permute-start.12) | collective-permute-done | bytes 196640 | tf_op jit(solution)/shard_map/ppermute | solution.py:374
  142.1 1.1 slots.1.near_ref
  143.2 10.2 %collective-permute-start.13 = (bf16[8,4,16,384]{3,2,1,0:T(8,128)(2,1)S(1)}, bf16[8,4,16,384]{3,2,1,0:T(8,128)(2,1)S(1)}, u32[]{:S(2)}, u32[]{:S(2)}) collective-permute-start(bf16[8,4,16,384]{3,2,1,0:T(8,128)(2,1)S(1)} %slots.1.near_ref), channel_id=1, source_target_pairs={{0,6},{1,3},{2,4},{3,1},{4,2},{5,7},{6,0},{7,5},{8,14},{9,11},{10,... | collective-permute-start | bytes 1179656 | tf_op jit(solution)/shard_map/ppermute | solution.py:374
  153.5 2.3 %center.5.rest_ref = f32[8,16,384]{2,1,0:T(8,128)S(1)} custom-call(bf16[16,192,192]{2,1,0:T(8,128)(2,1)} %diag_source_ref.1, f32[16,16,192]{2,1,0:T(8,128)S(1)} %get-tuple-element.29.x_ref, f32[16,192]{1,0:T(8,128)S(1)} %get-tuple-element.14.scale_ref), custom_call_target="tpu_custom_call" | custom-call | tf_op jit(solution)/shard_map/center/pallas_call | solution.py:388
  155.7 11.5 %collective-permute-done.13.far_ref = bf16[8,4,16,384]{3,2,1,0:T(8,128)(2,1)S(1)} collective-permute-done((bf16[8,4,16,384]{3,2,1,0:T(8,128)(2,1)S(1)}, bf16[8,4,16,384]{3,2,1,0:T(8,128)(2,1)S(1)}, u32[]{:S(2)}, u32[]{:S(2)}) %collective-permute-start.13) | collective-permute-done | bytes 393248 | tf_op jit(solution)/shard_map/ppermute | solution.py:374
  167.2 0.1 finish.1.prolong_ref.own_ref
  167.4 1.9 collective-permute-start.14
  169.3 3.4 %collective-permute-start.15 = (bf16[8,4,16,384]{3,2,1,0:T(8,128)(2,1)S(1)}, bf16[8,4,16,384]{3,2,1,0:T(8,128)(2,1)S(1)}, u32[]{:S(2)}, u32[]{:S(2)}) collective-permute-start(bf16[8,4,16,384]{3,2,1,0:T(8,128)(2,1)S(1)} %finish.1.prolong_ref.own_ref), channel_id=1, source_target_pairs={{8,0},{16,8},{24,16},{32,24},{40,32},{48,40},{56,48},{64,56},{72,6... | collective-permute-start | bytes 1179656 | tf_op jit(solution)/shard_map/ppermute | solution.py:365
  172.7 5.5 %collective-permute-start.16 = (bf16[8,4,16,384]{3,2,1,0:T(8,128)(2,1)S(1)}, bf16[8,4,16,384]{3,2,1,0:T(8,128)(2,1)S(1)}, u32[]{:S(2)}, u32[]{:S(2)}) collective-permute-start(bf16[8,4,16,384]{3,2,1,0:T(8,128)(2,1)S(1)} %finish.1.prolong_ref.own_ref), channel_id=1, source_target_pairs={{0,1},{1,0},{2,3},{3,2},{4,5},{5,4},{6,7},{7,6},{8,9},{9,8},{10,11... | collective-permute-start | bytes 1179656 | tf_op jit(solution)/shard_map/ppermute | solution.py:551
  178.2 5.0 %collective-permute-done.15.after_ref = bf16[8,4,16,384]{3,2,1,0:T(8,128)(2,1)S(1)} collective-permute-done((bf16[8,4,16,384]{3,2,1,0:T(8,128)(2,1)S(1)}, bf16[8,4,16,384]{3,2,1,0:T(8,128)(2,1)S(1)}, u32[]{:S(2)}, u32[]{:S(2)}) %collective-permute-start.15) | collective-permute-done | bytes 393248 | tf_op jit(solution)/shard_map/ppermute | solution.py:365
  183.2 5.3 %coarse.1 = (f32[2,96,256]{2,1,0:T(8,128)S(1)}, bf16[2,96,256]{2,1,0:T(8,128)(2,1)S(1)}) custom-call(s32[6]{0:T(128)S(1)} %stack.24.where_ref, s32[16,2]{1,0:T(8,128)S(1)} %broadcast_add_fusion.2.col_ref, s32[48,4]{1,0:T(8,128)S(1)} %pad_add_fusion.place_ref, bf16[16,192,384]{2,1,0:T(8,128)(2,1)S(1)} %stage.1.a_ref, bf16[16,192,192]{2,1,0:T(8,128)(2,1)} %diag_source_ref.1, ...), custom_call_target="tpu_custom_call" | custom-call | tf_op jit(solution)/shard_map/coarse/pallas_call | solution.py:388
  188.5 1.9 collective-permute-start.17
  190.4 7.4 %collective-permute-done.17 = bf16[2,96,256]{2,1,0:T(8,128)(2,1)S(1)} collective-permute-done((bf16[2,96,256]{2,1,0:T(8,128)(2,1)S(1)}, bf16[2,96,256]{2,1,0:T(8,128)(2,1)S(1)}, u32[]{:S(2)}, u32[]{:S(2)}) %collective-permute-start.17) | collective-permute-done | bytes 98336 | tf_op jit(solution)/shard_map/ppermute | solution.py:374
  197.8 5.6 %collective-permute-start.18 = (bf16[96,256]{1,0:T(8,128)(2,1)S(1)}, bf16[96,256]{1,0:T(8,128)(2,1)S(1)}, u32[]{:S(2)}, u32[]{:S(2)}) collective-permute-start(bf16[96,256]{1,0:T(8,128)(2,1)S(1)} %fusion.6), channel_id=1, source_target_pairs={{0,6},{1,3},{2,4},{3,1},{4,2},{5,7},{6,0},{7,5},{8,14},{9,11},{10,... | collective-permute-start | bytes 147464 | tf_op jit(solution)/shard_map/ppermute | solution.py:374
  203.4 3.1 %collective-permute-done.18 = bf16[96,256]{1,0:T(8,128)(2,1)S(1)} collective-permute-done((bf16[96,256]{1,0:T(8,128)(2,1)S(1)}, bf16[96,256]{1,0:T(8,128)(2,1)S(1)}, u32[]{:S(2)}, u32[]{:S(2)}) %collective-permute-start.18) | collective-permute-done | bytes 49184 | tf_op jit(solution)/shard_map/ppermute | solution.py:374
  206.5 10.6 %collective-permute-start.19 = (f32[96,128]{1,0:T(8,128)S(1)}, f32[96,128]{1,0:T(8,128)S(1)}, u32[]{:S(2)}, u32[]{:S(2)}) collective-permute-start(f32[96,128]{1,0:T(8,128)S(1)} %slice.50), channel_id=1, source_target_pairs={{0,1},{1,0},{2,3},{3,2},{4,5},{5,4},{6,7},{7,6},{8,9},{9,8},{10,11... | collective-permute-start | bytes 147464 | tf_op jit(solution)/shard_map/ppermute | solution.py:581
  217.1 1.3 here.1
  218.4 0.2 concatenate.20
  218.6 0.2 copy.49
  218.8 0.2 concatenate.21
  219.0 0.2 copy.50
  219.2 0.9 maximum_bitcast_fusion
  (44 shorter events, 1.0 us)
Async XLA Ops:
  0.6 1.0 copy-start
  1.7 9.0 %collective-permute-start = (bf16[8,16,384]{2,1,0:T(8,128)(2,1)S(1)}, bf16[8,16,384]{2,1,0:T(8,128)(2,1)S(1)}, u32[]{:S(2)}, u32[]{:S(2)}) collective-permute-start(bf16[8,16,384]{2,1,0:T(8,128)(2,1)S(1)} %fold.1.own_ref), channel_id=1, source_target_pairs={{0,8},{8,16},{16,24},{24,32},{32,40},{40,48},{48,56},{56,64},{64,7... | collective-permute-start | bytes 294920 | tf_op jit(solution)/shard_map/ppermute | solution.py:365
  4.8 9.6 %collective-permute-start.1 = (bf16[8,16,384]{2,1,0:T(8,128)(2,1)S(1)}, bf16[8,16,384]{2,1,0:T(8,128)(2,1)S(1)}, u32[]{:S(2)}, u32[]{:S(2)}) collective-permute-start(bf16[8,16,384]{2,1,0:T(8,128)(2,1)S(1)} %fold.1.own_ref), channel_id=1, source_target_pairs={{8,0},{16,8},{24,16},{32,24},{40,32},{48,40},{56,48},{64,56},{72,6... | collective-permute-start | bytes 294920 | tf_op jit(solution)/shard_map/ppermute | solution.py:365
  10.6 17.1 %copy-start.2 = (s32[16]{0:T(128)S(1)}, s32[16]{0:T(128)}, u32[]{:S(2)}) copy-start(s32[16]{0:T(128)} %param.9) | copy-start | bytes 196
  10.6 17.2 %copy-start.1 = (f32[16,16,192]{2,1,0:T(8,128)S(1)}, f32[16,16,192]{2,1,0:T(8,128)}, u32[]{:S(2)}) copy-start(f32[16,16,192]{2,1,0:T(8,128)} %x_ref.3) | copy-start | bytes 589828
  16.1 14.2 %collective-permute-start.2 = (bf16[8,16,384]{2,1,0:T(8,128)(2,1)S(1)}, bf16[8,16,384]{2,1,0:T(8,128)(2,1)S(1)}, u32[]{:S(2)}, u32[]{:S(2)}) collective-permute-start(bf16[8,16,384]{2,1,0:T(8,128)(2,1)S(1)} %couple.3.near_ref), channel_id=1, source_target_pairs={{0,2},{1,7},{2,0},{3,5},{4,6},{5,3},{6,4},{7,1},{8,10},{9,15},{10,... | collective-permute-start | bytes 294920 | tf_op jit(solution)/shard_map/ppermute | solution.py:374
  30.3 10.5 %collective-permute-start.3 = (bf16[8,16,384]{2,1,0:T(8,128)(2,1)S(1)}, bf16[8,16,384]{2,1,0:T(8,128)(2,1)S(1)}, u32[]{:S(2)}, u32[]{:S(2)}) collective-permute-start(bf16[8,16,384]{2,1,0:T(8,128)(2,1)S(1)} %pair.3.near_ref), channel_id=1, source_target_pairs={{0,6},{1,3},{2,4},{3,1},{4,2},{5,7},{6,0},{7,5},{8,14},{9,11},{10,... | collective-permute-start | bytes 294920 | tf_op jit(solution)/shard_map/ppermute | solution.py:374
  40.9 8.6 %collective-permute-start.4 = (bf16[9,16,384]{2,1,0:T(8,128)(2,1)S(1)}, bf16[9,16,384]{2,1,0:T(8,128)(2,1)S(1)}, u32[]{:S(2)}, u32[]{:S(2)}) collective-permute-start(bf16[9,16,384]{2,1,0:T(8,128)(2,1)S(1)} %get-tuple-element.15.own_ref), channel_id=1, source_target_pairs={{0,8},{8,16},{16,24},{24,32},{32,40},{40,48},{48,56},{56,64},{64,7... | collective-permute-start | bytes 331784 | tf_op jit(solution)/shard_map/ppermute | solution.py:365
  47.5 9.7 %collective-permute-start.5 = (bf16[9,16,384]{2,1,0:T(8,128)(2,1)S(1)}, bf16[9,16,384]{2,1,0:T(8,128)(2,1)S(1)}, u32[]{:S(2)}, u32[]{:S(2)}) collective-permute-start(bf16[9,16,384]{2,1,0:T(8,128)(2,1)S(1)} %get-tuple-element.15.own_ref), channel_id=1, source_target_pairs={{8,0},{16,8},{24,16},{32,24},{40,32},{48,40},{56,48},{64,56},{72,6... | collective-permute-start | bytes 331784 | tf_op jit(solution)/shard_map/ppermute | solution.py:365
  58.9 10.3 %collective-permute-start.6 = (bf16[8,16,384]{2,1,0:T(8,128)(2,1)S(1)}, bf16[8,16,384]{2,1,0:T(8,128)(2,1)S(1)}, u32[]{:S(2)}, u32[]{:S(2)}) collective-permute-start(bf16[8,16,384]{2,1,0:T(8,128)(2,1)S(1)} %couple.4.near_ref), channel_id=1, source_target_pairs={{0,2},{1,7},{2,0},{3,5},{4,6},{5,3},{6,4},{7,1},{8,10},{9,15},{10,... | collective-permute-start | bytes 294920 | tf_op jit(solution)/shard_map/ppermute | solution.py:374
  69.3 9.6 %collective-permute-start.7 = (bf16[8,16,384]{2,1,0:T(8,128)(2,1)S(1)}, bf16[8,16,384]{2,1,0:T(8,128)(2,1)S(1)}, u32[]{:S(2)}, u32[]{:S(2)}) collective-permute-start(bf16[8,16,384]{2,1,0:T(8,128)(2,1)S(1)} %pair.4.near_ref), channel_id=1, source_target_pairs={{0,6},{1,3},{2,4},{3,1},{4,2},{5,7},{6,0},{7,5},{8,14},{9,11},{10,... | collective-permute-start | bytes 294920 | tf_op jit(solution)/shard_map/ppermute | solution.py:374
  79.0 5.4 %collective-permute-start.8 = (bf16[8,16,384]{2,1,0:T(8,128)(2,1)S(1)}, bf16[8,16,384]{2,1,0:T(8,128)(2,1)S(1)}, u32[]{:S(2)}, u32[]{:S(2)}) collective-permute-start(bf16[8,16,384]{2,1,0:T(8,128)(2,1)S(1)} %get-tuple-element.17.own_ref), channel_id=1, source_target_pairs={{0,8},{8,16},{16,24},{24,32},{32,40},{40,48},{48,56},{56,64},{64,7... | collective-permute-start | bytes 294920 | tf_op jit(solution)/shard_map/ppermute | solution.py:365
  80.9 9.6 %collective-permute-start.9 = (bf16[8,16,384]{2,1,0:T(8,128)(2,1)S(1)}, bf16[8,16,384]{2,1,0:T(8,128)(2,1)S(1)}, u32[]{:S(2)}, u32[]{:S(2)}) collective-permute-start(bf16[8,16,384]{2,1,0:T(8,128)(2,1)S(1)} %get-tuple-element.17.own_ref), channel_id=1, source_target_pairs={{8,0},{16,8},{24,16},{32,24},{40,32},{48,40},{56,48},{64,56},{72,6... | collective-permute-start | bytes 294920 | tf_op jit(solution)/shard_map/ppermute | solution.py:365
  92.2 9.4 %collective-permute-start.10 = (bf16[9,16,384]{2,1,0:T(8,128)(2,1)S(1)}, bf16[9,16,384]{2,1,0:T(8,128)(2,1)S(1)}, u32[]{:S(2)}, u32[]{:S(2)}) collective-permute-start(bf16[9,16,384]{2,1,0:T(8,128)(2,1)S(1)} %couple.5.near_ref), channel_id=1, source_target_pairs={{0,2},{1,7},{2,0},{3,5},{4,6},{5,3},{6,4},{7,1},{8,10},{9,15},{10,... | collective-permute-start | bytes 331784 | tf_op jit(solution)/shard_map/ppermute | solution.py:374
  101.6 12.7 %collective-permute-start.11 = (bf16[8,16,384]{2,1,0:T(8,128)(2,1)S(1)}, bf16[8,16,384]{2,1,0:T(8,128)(2,1)S(1)}, u32[]{:S(2)}, u32[]{:S(2)}) collective-permute-start(bf16[8,16,384]{2,1,0:T(8,128)(2,1)S(1)} %pair.5.near_ref), channel_id=1, source_target_pairs={{0,6},{1,3},{2,4},{3,1},{4,2},{5,7},{6,0},{7,5},{8,14},{9,11},{10,... | collective-permute-start | bytes 294920 | tf_op jit(solution)/shard_map/ppermute | solution.py:374
  127.9 14.2 %collective-permute-start.12 = (bf16[8,2,16,384]{3,2,1,0:T(8,128)(2,1)S(1)}, bf16[8,2,16,384]{3,2,1,0:T(8,128)(2,1)S(1)}, u32[]{:S(2)}, u32[]{:S(2)}) collective-permute-start(bf16[8,2,16,384]{3,2,1,0:T(8,128)(2,1)S(1)} %fit.1.near_ref), channel_id=1, source_target_pairs={{0,2},{1,7},{2,0},{3,5},{4,6},{5,3},{6,4},{7,1},{8,10},{9,15},{10,... | collective-permute-start | bytes 589832 | tf_op jit(solution)/shard_map/ppermute | solution.py:374
  143.2 24.0 %collective-permute-start.13 = (bf16[8,4,16,384]{3,2,1,0:T(8,128)(2,1)S(1)}, bf16[8,4,16,384]{3,2,1,0:T(8,128)(2,1)S(1)}, u32[]{:S(2)}, u32[]{:S(2)}) collective-permute-start(bf16[8,4,16,384]{3,2,1,0:T(8,128)(2,1)S(1)} %slots.1.near_ref), channel_id=1, source_target_pairs={{0,6},{1,3},{2,4},{3,1},{4,2},{5,7},{6,0},{7,5},{8,14},{9,11},{10,... | collective-permute-start | bytes 1179656 | tf_op jit(solution)/shard_map/ppermute | solution.py:374
  167.4 10.8 %collective-permute-start.14 = (bf16[8,4,16,384]{3,2,1,0:T(8,128)(2,1)S(1)}, bf16[8,4,16,384]{3,2,1,0:T(8,128)(2,1)S(1)}, u32[]{:S(2)}, u32[]{:S(2)}) collective-permute-start(bf16[8,4,16,384]{3,2,1,0:T(8,128)(2,1)S(1)} %finish.1.prolong_ref.own_ref), channel_id=1, source_target_pairs={{0,8},{8,16},{16,24},{24,32},{32,40},{40,48},{48,56},{56,64},{64,7... | collective-permute-start | bytes 1179656 | tf_op jit(solution)/shard_map/ppermute | solution.py:365
  169.3 13.9 %collective-permute-start.15 = (bf16[8,4,16,384]{3,2,1,0:T(8,128)(2,1)S(1)}, bf16[8,4,16,384]{3,2,1,0:T(8,128)(2,1)S(1)}, u32[]{:S(2)}, u32[]{:S(2)}) collective-permute-start(bf16[8,4,16,384]{3,2,1,0:T(8,128)(2,1)S(1)} %finish.1.prolong_ref.own_ref), channel_id=1, source_target_pairs={{8,0},{16,8},{24,16},{32,24},{40,32},{48,40},{56,48},{64,56},{72,6... | collective-permute-start | bytes 1179656 | tf_op jit(solution)/shard_map/ppermute | solution.py:365
  172.7 10.5 %collective-permute-start.16 = (bf16[8,4,16,384]{3,2,1,0:T(8,128)(2,1)S(1)}, bf16[8,4,16,384]{3,2,1,0:T(8,128)(2,1)S(1)}, u32[]{:S(2)}, u32[]{:S(2)}) collective-permute-start(bf16[8,4,16,384]{3,2,1,0:T(8,128)(2,1)S(1)} %finish.1.prolong_ref.own_ref), channel_id=1, source_target_pairs={{0,1},{1,0},{2,3},{3,2},{4,5},{5,4},{6,7},{7,6},{8,9},{9,8},{10,11... | collective-permute-start | bytes 1179656 | tf_op jit(solution)/shard_map/ppermute | solution.py:551
  188.5 9.3 %collective-permute-start.17 = (bf16[2,96,256]{2,1,0:T(8,128)(2,1)S(1)}, bf16[2,96,256]{2,1,0:T(8,128)(2,1)S(1)}, u32[]{:S(2)}, u32[]{:S(2)}) collective-permute-start(bf16[2,96,256]{2,1,0:T(8,128)(2,1)S(1)} %get-tuple-element.19), channel_id=1, source_target_pairs={{0,2},{1,7},{2,0},{3,5},{4,6},{5,3},{6,4},{7,1},{8,10},{9,15},{10,... | collective-permute-start | bytes 294920 | tf_op jit(solution)/shard_map/ppermute | solution.py:374
  197.8 8.7 %collective-permute-start.18 = (bf16[96,256]{1,0:T(8,128)(2,1)S(1)}, bf16[96,256]{1,0:T(8,128)(2,1)S(1)}, u32[]{:S(2)}, u32[]{:S(2)}) collective-permute-start(bf16[96,256]{1,0:T(8,128)(2,1)S(1)} %fusion.6), channel_id=1, source_target_pairs={{0,6},{1,3},{2,4},{3,1},{4,2},{5,7},{6,0},{7,5},{8,14},{9,11},{10,... | collective-permute-start | bytes 147464 | tf_op jit(solution)/shard_map/ppermute | solution.py:374
  206.5 11.9 %collective-permute-start.19 = (f32[96,128]{1,0:T(8,128)S(1)}, f32[96,128]{1,0:T(8,128)S(1)}, u32[]{:S(2)}, u32[]{:S(2)}) collective-permute-start(f32[96,128]{1,0:T(8,128)S(1)} %slice.50), channel_id=1, source_target_pairs={{0,1},{1,0},{2,3},{3,2},{4,5},{5,4},{6,7},{7,6},{8,9},{9,8},{10,11... | collective-permute-start | bytes 147464 | tf_op jit(solution)/shard_map/ppermute | solution.py:581

commit v6 on v5

--- a/solution.py
+++ b/solution.py
@@ -300,10 +300,10 @@
         image = jnp.concatenate([image, zero], axis=1)
         blocks = [image[q * vectors : (q + 1) * vectors] for q in range(SLOTS)]
         if not fresh:
-            held_now = [reach[at, :, lanes] for at in places]
+            held_now = [reach[at, :, lanes].astype(F32) for at in places]
             blocks = [block + now for block, now in zip(blocks, held_now)]
         for at, block in zip(places, blocks):
-            reach[at, :, lanes] = block
+            reach[at, :, lanes] = block.astype(BF16)
 
     def lanes_of(i):
         if isinstance(i, int):
@@ -345,7 +345,7 @@
     for c in range(rows // 4):
         lanes = slice(c * depth, (c + 1) * depth)
         product = dot_nt(
-            reach[:, :, lanes].astype(BF16).reshape(span * vectors, depth),
+            reach[:, :, lanes].reshape(span * vectors, depth),
             left[:, :, :, lanes].reshape(2 * SLAB_AGGS * vectors, depth),
         )
         if c == 0:
@@ -565,7 +565,7 @@
         [
             pltpu.VMEM((3 * rows, SLOTS, vectors, 2 * LANES), BF16),
             pltpu.VMEM((3 * rows, SLOTS, vectors, 2 * LANES), BF16),
-            pltpu.VMEM((span, vectors, rows * 2 * LANES), F32),
+            pltpu.VMEM((span, vectors, rows * 2 * LANES), BF16),
             pltpu.VMEM((2, SLAB_AGGS, vectors, rows * 2 * LANES), BF16),
             pltpu.VMEM((span * vectors, wide), F32),
         ]

time: 221 us -> 220 us (level)
  the two profiles are of different devices: /device:TPU:31 before, /device:TPU:95 now
where the time goes in v6:
time: 220 us; the launch traced here: 219 us
  starting transfers between devices  99.5 us (45%)
  waiting for transfers between devices  70.3 us (32%)
  Pallas kernels  26.8 us (12%)
  blocking collectives  14.4 us (7%)
  other arithmetic  2.66 us (1%)
  matrix products  2.34 us (1%)
    ppermute x10, starting transfers between devices, exchange(): return lax.ppermute(x, ('aggs', 'vecs'), pairs)  58.7 us
    ppermute x10, waiting for transfers between devices, exchange(): return lax.ppermute(x, ('aggs', 'vecs'), pairs)  51.1 us
    pallas_call x20, Pallas kernels, kernel_call(): pl.pallas_call(body, out_shape=shapes, in_specs=specs, out_specs=[VMEM_SP...  24.7 us
    ppermute x8, starting transfers between devices, shift(): lax.ppermute(x, 'rows', [(i, i + by) for i in range(size) if 0 <= i + by...  21.6 us
    ppermute x8, waiting for transfers between devices, shift(): lax.ppermute(x, 'rows', [(i, i + by) for i in range(size) if 0 <= i + by...  19.2 us
    all_gather x1, blocking collectives, on_device(): every = lax.all_gather(current, 'vecs', axis=1, tiled=True)  14.4 us
    ppermute x1, starting transfers between devices, on_device(): theirs = lax.ppermute(theirs, 'vecs', [(0, 1), (1, 0)])  11.5 us
    ppermute x1, starting transfers between devices, on_device(): other = lax.ppermute(prolong, 'vecs', [(0, 1), (1, 0)])  7.75 us
  transfers between devices with their start and end apart: 20, of which 14 were waited for; matrix products, arithmetic and copies ran while one was open for 1% of the time, Pallas kernels for 6%

profile of v6, /device:TPU:95, one launch (start us, length us, event | category | flops | bytes accessed | tf_op | source)
XLA Modules:
  0.0 219.3 jit_solution(4514114592262212320)
XLA Ops:
  0.6 0.9 copy-done
  1.7 3.1 %collective-permute-start = (bf16[8,16,384]{2,1,0:T(8,128)(2,1)S(1)}, bf16[8,16,384]{2,1,0:T(8,128)(2,1)S(1)}, u32[]{:S(2)}, u32[]{:S(2)}) collective-permute-start(bf16[8,16,384]{2,1,0:T(8,128)(2,1)S(1)} %fold.1.own_ref), channel_id=1, source_target_pairs={{0,8},{8,16},{16,24},{24,32},{32,40},{40,48},{48,56},{56,64},{64,7... | collective-permute-start | bytes 294920 | tf_op jit(solution)/shard_map/ppermute | solution.py:365
  4.8 2.2 collective-permute-start.1
  7.0 0.7 broadcast_subtract_fusion.1
  7.7 0.7 pad_add_fusion.1
  8.5 2.1 stage.1.a_ref
  10.6 3.7 %collective-permute-done.1.after_ref = bf16[8,16,384]{2,1,0:T(8,128)(2,1)S(1)} collective-permute-done((bf16[8,16,384]{2,1,0:T(8,128)(2,1)S(1)}, bf16[8,16,384]{2,1,0:T(8,128)(2,1)S(1)}, u32[]{:S(2)}, u32[]{:S(2)}) %collective-permute-start.1) | collective-permute-done | bytes 98336 | tf_op jit(solution)/shard_map/ppermute | solution.py:365
  14.4 1.7 couple.3.near_ref
  16.1 9.8 %collective-permute-start.2 = (bf16[8,16,384]{2,1,0:T(8,128)(2,1)S(1)}, bf16[8,16,384]{2,1,0:T(8,128)(2,1)S(1)}, u32[]{:S(2)}, u32[]{:S(2)}) collective-permute-start(bf16[8,16,384]{2,1,0:T(8,128)(2,1)S(1)} %couple.3.near_ref), channel_id=1, source_target_pairs={{0,2},{1,7},{2,0},{3,5},{4,6},{5,3},{6,4},{7,1},{8,10},{9,15},{10,... | collective-permute-start | bytes 294920 | tf_op jit(solution)/shard_map/ppermute | solution.py:374
  26.0 2.2 first_center.1
  28.2 1.8 collective-permute-done.2.far_ref
  30.0 5.1 %collective-permute-start.3 = (bf16[8,16,384]{2,1,0:T(8,128)(2,1)S(1)}, bf16[8,16,384]{2,1,0:T(8,128)(2,1)S(1)}, u32[]{:S(2)}, u32[]{:S(2)}) collective-permute-start(bf16[8,16,384]{2,1,0:T(8,128)(2,1)S(1)} %pair.3.near_ref), channel_id=1, source_target_pairs={{0,6},{1,3},{2,4},{3,1},{4,2},{5,7},{6,0},{7,5},{8,14},{9,11},{10,... | collective-permute-start | bytes 294920 | tf_op jit(solution)/shard_map/ppermute | solution.py:374
  35.1 0.2 select_reduce_fusion
  35.3 4.0 %collective-permute-done.3.far_ref = bf16[8,16,384]{2,1,0:T(8,128)(2,1)S(1)} collective-permute-done((bf16[8,16,384]{2,1,0:T(8,128)(2,1)S(1)}, bf16[8,16,384]{2,1,0:T(8,128)(2,1)S(1)}, u32[]{:S(2)}, u32[]{:S(2)}) %collective-permute-start.3) | collective-permute-done | bytes 98336 | tf_op jit(solution)/shard_map/ppermute | solution.py:374
  39.3 3.8 %collective-permute-start.4 = (bf16[9,16,384]{2,1,0:T(8,128)(2,1)S(1)}, bf16[9,16,384]{2,1,0:T(8,128)(2,1)S(1)}, u32[]{:S(2)}, u32[]{:S(2)}) collective-permute-start(bf16[9,16,384]{2,1,0:T(8,128)(2,1)S(1)} %get-tuple-element.15.own_ref), channel_id=1, source_target_pairs={{0,8},{8,16},{16,24},{24,32},{32,40},{40,48},{48,56},{56,64},{64,7... | collective-permute-start | bytes 331784 | tf_op jit(solution)/shard_map/ppermute | solution.py:365
  43.2 1.9 collective-permute-start.5
  45.2 7.7 %collective-permute-done.5.after_ref = bf16[9,16,384]{2,1,0:T(8,128)(2,1)S(1)} collective-permute-done((bf16[9,16,384]{2,1,0:T(8,128)(2,1)S(1)}, bf16[9,16,384]{2,1,0:T(8,128)(2,1)S(1)}, u32[]{:S(2)}, u32[]{:S(2)}) %collective-permute-start.5) | collective-permute-done | bytes 110624 | tf_op jit(solution)/shard_map/ppermute | solution.py:365
  52.9 1.7 couple.4.near_ref
  54.6 5.4 %collective-permute-start.6 = (bf16[8,16,384]{2,1,0:T(8,128)(2,1)S(1)}, bf16[8,16,384]{2,1,0:T(8,128)(2,1)S(1)}, u32[]{:S(2)}, u32[]{:S(2)}) collective-permute-start(bf16[8,16,384]{2,1,0:T(8,128)(2,1)S(1)} %couple.4.near_ref), channel_id=1, source_target_pairs={{0,2},{1,7},{2,0},{3,5},{4,6},{5,3},{6,4},{7,1},{8,10},{9,15},{10,... | collective-permute-start | bytes 294920 | tf_op jit(solution)/shard_map/ppermute | solution.py:374
  60.0 6.0 %collective-permute-done.6.far_ref = bf16[8,16,384]{2,1,0:T(8,128)(2,1)S(1)} collective-permute-done((bf16[8,16,384]{2,1,0:T(8,128)(2,1)S(1)}, bf16[8,16,384]{2,1,0:T(8,128)(2,1)S(1)}, u32[]{:S(2)}, u32[]{:S(2)}) %collective-permute-start.6) | collective-permute-done | bytes 98336 | tf_op jit(solution)/shard_map/ppermute | solution.py:374
  66.0 5.4 %collective-permute-start.7 = (bf16[8,16,384]{2,1,0:T(8,128)(2,1)S(1)}, bf16[8,16,384]{2,1,0:T(8,128)(2,1)S(1)}, u32[]{:S(2)}, u32[]{:S(2)}) collective-permute-start(bf16[8,16,384]{2,1,0:T(8,128)(2,1)S(1)} %pair.4.near_ref), channel_id=1, source_target_pairs={{0,6},{1,3},{2,4},{3,1},{4,2},{5,7},{6,0},{7,5},{8,14},{9,11},{10,... | collective-permute-start | bytes 294920 | tf_op jit(solution)/shard_map/ppermute | solution.py:374
  71.5 0.1 copy.42
  71.6 2.3 %center.3.rest_ref = f32[8,16,384]{2,1,0:T(8,128)S(1)} custom-call(bf16[16,192,192]{2,1,0:T(8,128)(2,1)} %diag_source_ref.1, f32[8,16,384]{2,1,0:T(8,128)S(1)} %get-tuple-element.13.x_ref, f32[16,192]{1,0:T(8,128)S(1)} %get-tuple-element.14.scale_ref), custom_call_target="tpu_custom_call" | custom-call | tf_op jit(solution)/shard_map/center/pallas_call | solution.py:388
  73.8 1.5 collective-permute-done.7.far_ref
  75.4 1.9 collective-permute-start.8
  77.3 3.4 %collective-permute-start.9 = (bf16[8,16,384]{2,1,0:T(8,128)(2,1)S(1)}, bf16[8,16,384]{2,1,0:T(8,128)(2,1)S(1)}, u32[]{:S(2)}, u32[]{:S(2)}) collective-permute-start(bf16[8,16,384]{2,1,0:T(8,128)(2,1)S(1)} %get-tuple-element.17.own_ref), channel_id=1, source_target_pairs={{8,0},{16,8},{24,16},{32,24},{40,32},{48,40},{56,48},{64,56},{72,6... | collective-permute-start | bytes 294920 | tf_op jit(solution)/shard_map/ppermute | solution.py:365
  80.7 6.1 %collective-permute-done.9.after_ref = bf16[8,16,384]{2,1,0:T(8,128)(2,1)S(1)} collective-permute-done((bf16[8,16,384]{2,1,0:T(8,128)(2,1)S(1)}, bf16[8,16,384]{2,1,0:T(8,128)(2,1)S(1)}, u32[]{:S(2)}, u32[]{:S(2)}) %collective-permute-start.9) | collective-permute-done | bytes 98336 | tf_op jit(solution)/shard_map/ppermute | solution.py:365
  86.9 1.7 couple.5.near_ref
  88.6 7.9 %collective-permute-start.10 = (bf16[9,16,384]{2,1,0:T(8,128)(2,1)S(1)}, bf16[9,16,384]{2,1,0:T(8,128)(2,1)S(1)}, u32[]{:S(2)}, u32[]{:S(2)}) collective-permute-start(bf16[9,16,384]{2,1,0:T(8,128)(2,1)S(1)} %couple.5.near_ref), channel_id=1, source_target_pairs={{0,2},{1,7},{2,0},{3,5},{4,6},{5,3},{6,4},{7,1},{8,10},{9,15},{10,... | collective-permute-start | bytes 331784 | tf_op jit(solution)/shard_map/ppermute | solution.py:374
  96.6 2.3 %center.4.rest_ref = f32[8,16,384]{2,1,0:T(8,128)S(1)} custom-call(bf16[16,192,192]{2,1,0:T(8,128)(2,1)} %diag_source_ref.1, f32[8,16,384]{2,1,0:T(8,128)S(1)} %get-tuple-element.16.x_ref, f32[16,192]{1,0:T(8,128)S(1)} %get-tuple-element.14.scale_ref), custom_call_target="tpu_custom_call" | custom-call | tf_op jit(solution)/shard_map/center/pallas_call | solution.py:388
  98.8 0.4 collective-permute-done.10.far_ref
  99.3 6.0 %collective-permute-start.11 = (bf16[8,16,384]{2,1,0:T(8,128)(2,1)S(1)}, bf16[8,16,384]{2,1,0:T(8,128)(2,1)S(1)}, u32[]{:S(2)}, u32[]{:S(2)}) collective-permute-start(bf16[8,16,384]{2,1,0:T(8,128)(2,1)S(1)} %pair.5.near_ref), channel_id=1, source_target_pairs={{0,6},{1,3},{2,4},{3,1},{4,2},{5,7},{6,0},{7,5},{8,14},{9,11},{10,... | collective-permute-start | bytes 294920 | tf_op jit(solution)/shard_map/ppermute | solution.py:374
  105.3 5.7 %collective-permute-done.11.far_ref = bf16[8,16,384]{2,1,0:T(8,128)(2,1)S(1)} collective-permute-done((bf16[8,16,384]{2,1,0:T(8,128)(2,1)S(1)}, bf16[8,16,384]{2,1,0:T(8,128)(2,1)S(1)}, u32[]{:S(2)}, u32[]{:S(2)}) %collective-permute-start.11) | collective-permute-done | bytes 98336 | tf_op jit(solution)/shard_map/ppermute | solution.py:374
  110.9 0.1 last_update.1
  111.0 14.4 %all_gather.3 = f32[16,32,192]{2,1,0:T(8,128)S(1)} all-gather(f32[16,16,192]{2,1,0:T(8,128)S(1)} %last_update.1), channel_id=1, replica_groups=mesh['rows'=64,'aggs'=4,'vecs'=2] {'vecs'}, dimensions={1}, use_global_device_ids=true | all-gather | bytes 589824 | tf_op jit(solution)/shard_map/all_gather | solution.py:509
  125.5 0.6 fusion.16
  126.1 0.7 convolution_multiply_fusion.m_ref
  126.8 0.8 inverse_factor.1
  127.5 0.6 fusion.1
  128.2 0.4 fusion.15
  128.6 1.8 fit.1.near_ref
  130.4 6.0 %collective-permute-start.12 = (bf16[8,2,16,384]{3,2,1,0:T(8,128)(2,1)S(1)}, bf16[8,2,16,384]{3,2,1,0:T(8,128)(2,1)S(1)}, u32[]{:S(2)}, u32[]{:S(2)}) collective-permute-start(bf16[8,2,16,384]{3,2,1,0:T(8,128)(2,1)S(1)} %fit.1.near_ref), channel_id=1, source_target_pairs={{0,2},{1,7},{2,0},{3,5},{4,6},{5,3},{6,4},{7,1},{8,10},{9,15},{10,... | collective-permute-start | bytes 589832 | tf_op jit(solution)/shard_map/ppermute | solution.py:374
  136.4 8.7 %collective-permute-done.12.far_ref = bf16[8,2,16,384]{3,2,1,0:T(8,128)(2,1)S(1)} collective-permute-done((bf16[8,2,16,384]{3,2,1,0:T(8,128)(2,1)S(1)}, bf16[8,2,16,384]{3,2,1,0:T(8,128)(2,1)S(1)}, u32[]{:S(2)}, u32[]{:S(2)}) %collective-permute-start.12) | collective-permute-done | bytes 196640 | tf_op jit(solution)/shard_map/ppermute | solution.py:374
  145.1 1.1 slots.1.near_ref
  146.2 8.0 %collective-permute-start.13 = (bf16[8,4,16,384]{3,2,1,0:T(8,128)(2,1)S(1)}, bf16[8,4,16,384]{3,2,1,0:T(8,128)(2,1)S(1)}, u32[]{:S(2)}, u32[]{:S(2)}) collective-permute-start(bf16[8,4,16,384]{3,2,1,0:T(8,128)(2,1)S(1)} %slots.1.near_ref), channel_id=1, source_target_pairs={{0,6},{1,3},{2,4},{3,1},{4,2},{5,7},{6,0},{7,5},{8,14},{9,11},{10,... | collective-permute-start | bytes 1179656 | tf_op jit(solution)/shard_map/ppermute | solution.py:374
  154.2 2.3 %center.5.rest_ref = f32[8,16,384]{2,1,0:T(8,128)S(1)} custom-call(bf16[16,192,192]{2,1,0:T(8,128)(2,1)} %diag_source_ref.1, f32[16,16,192]{2,1,0:T(8,128)S(1)} %get-tuple-element.29.x_ref, f32[16,192]{1,0:T(8,128)S(1)} %get-tuple-element.14.scale_ref), custom_call_target="tpu_custom_call" | custom-call | tf_op jit(solution)/shard_map/center/pallas_call | solution.py:388
  156.5 10.3 %collective-permute-done.13.far_ref = bf16[8,4,16,384]{3,2,1,0:T(8,128)(2,1)S(1)} collective-permute-done((bf16[8,4,16,384]{3,2,1,0:T(8,128)(2,1)S(1)}, bf16[8,4,16,384]{3,2,1,0:T(8,128)(2,1)S(1)}, u32[]{:S(2)}, u32[]{:S(2)}) %collective-permute-start.13) | collective-permute-done | bytes 393248 | tf_op jit(solution)/shard_map/ppermute | solution.py:374
  166.8 0.1 finish.1.prolong_ref.own_ref
  166.9 1.9 collective-permute-start.14
  168.8 3.4 %collective-permute-start.15 = (bf16[8,4,16,384]{3,2,1,0:T(8,128)(2,1)S(1)}, bf16[8,4,16,384]{3,2,1,0:T(8,128)(2,1)S(1)}, u32[]{:S(2)}, u32[]{:S(2)}) collective-permute-start(bf16[8,4,16,384]{3,2,1,0:T(8,128)(2,1)S(1)} %finish.1.prolong_ref.own_ref), channel_id=1, source_target_pairs={{8,0},{16,8},{24,16},{32,24},{40,32},{48,40},{56,48},{64,56},{72,6... | collective-permute-start | bytes 1179656 | tf_op jit(solution)/shard_map/ppermute | solution.py:365
  172.2 7.7 %collective-permute-start.16 = (bf16[8,4,16,384]{3,2,1,0:T(8,128)(2,1)S(1)}, bf16[8,4,16,384]{3,2,1,0:T(8,128)(2,1)S(1)}, u32[]{:S(2)}, u32[]{:S(2)}) collective-permute-start(bf16[8,4,16,384]{3,2,1,0:T(8,128)(2,1)S(1)} %finish.1.prolong_ref.own_ref), channel_id=1, source_target_pairs={{0,1},{1,0},{2,3},{3,2},{4,5},{5,4},{6,7},{7,6},{8,9},{9,8},{10,11... | collective-permute-start | bytes 1179656 | tf_op jit(solution)/shard_map/ppermute | solution.py:551
  180.0 1.6 collective-permute-done.15.after_ref
  181.6 5.2 %coarse.1 = (f32[2,96,256]{2,1,0:T(8,128)S(1)}, bf16[2,96,256]{2,1,0:T(8,128)(2,1)S(1)}) custom-call(s32[6]{0:T(128)S(1)} %stack.24.where_ref, s32[16,2]{1,0:T(8,128)S(1)} %broadcast_add_fusion.2.col_ref, s32[48,4]{1,0:T(8,128)S(1)} %pad_add_fusion.place_ref, bf16[16,192,384]{2,1,0:T(8,128)(2,1)S(1)} %stage.1.a_ref, bf16[16,192,192]{2,1,0:T(8,128)(2,1)} %diag_source_ref.1, ...), custom_call_target="tpu_custom_call" | custom-call | tf_op jit(solution)/shard_map/coarse/pallas_call | solution.py:388
  186.8 1.9 collective-permute-start.17
  188.8 7.3 %collective-permute-done.17 = bf16[2,96,256]{2,1,0:T(8,128)(2,1)S(1)} collective-permute-done((bf16[2,96,256]{2,1,0:T(8,128)(2,1)S(1)}, bf16[2,96,256]{2,1,0:T(8,128)(2,1)S(1)}, u32[]{:S(2)}, u32[]{:S(2)}) %collective-permute-start.17) | collective-permute-done | bytes 98336 | tf_op jit(solution)/shard_map/ppermute | solution.py:374
  196.1 3.2 %collective-permute-start.18 = (bf16[96,256]{1,0:T(8,128)(2,1)S(1)}, bf16[96,256]{1,0:T(8,128)(2,1)S(1)}, u32[]{:S(2)}, u32[]{:S(2)}) collective-permute-start(bf16[96,256]{1,0:T(8,128)(2,1)S(1)} %fusion.6), channel_id=1, source_target_pairs={{0,6},{1,3},{2,4},{3,1},{4,2},{5,7},{6,0},{7,5},{8,14},{9,11},{10,... | collective-permute-start | bytes 147464 | tf_op jit(solution)/shard_map/ppermute | solution.py:374
  199.4 5.5 %collective-permute-done.18 = bf16[96,256]{1,0:T(8,128)(2,1)S(1)} collective-permute-done((bf16[96,256]{1,0:T(8,128)(2,1)S(1)}, bf16[96,256]{1,0:T(8,128)(2,1)S(1)}, u32[]{:S(2)}, u32[]{:S(2)}) %collective-permute-start.18) | collective-permute-done | bytes 49184 | tf_op jit(solution)/shard_map/ppermute | solution.py:374
  204.9 11.5 %collective-permute-start.19 = (f32[96,128]{1,0:T(8,128)S(1)}, f32[96,128]{1,0:T(8,128)S(1)}, u32[]{:S(2)}, u32[]{:S(2)}) collective-permute-start(f32[96,128]{1,0:T(8,128)S(1)} %slice.50), channel_id=1, source_target_pairs={{0,1},{1,0},{2,3},{3,2},{4,5},{5,4},{6,7},{7,6},{8,9},{9,8},{10,11... | collective-permute-start | bytes 147464 | tf_op jit(solution)/shard_map/ppermute | solution.py:581
  216.4 1.3 here.1
  217.7 0.2 concatenate.20
  217.9 0.2 copy.49
  218.1 0.2 concatenate.21
  218.2 0.2 copy.50
  218.4 0.9 maximum_bitcast_fusion
  (44 shorter events, 1.0 us)
Async XLA Ops:
  0.6 1.0 copy-start
  1.7 9.0 %collective-permute-start = (bf16[8,16,384]{2,1,0:T(8,128)(2,1)S(1)}, bf16[8,16,384]{2,1,0:T(8,128)(2,1)S(1)}, u32[]{:S(2)}, u32[]{:S(2)}) collective-permute-start(bf16[8,16,384]{2,1,0:T(8,128)(2,1)S(1)} %fold.1.own_ref), channel_id=1, source_target_pairs={{0,8},{8,16},{16,24},{24,32},{32,40},{40,48},{48,56},{56,64},{64,7... | collective-permute-start | bytes 294920 | tf_op jit(solution)/shard_map/ppermute | solution.py:365
  4.8 9.6 %collective-permute-start.1 = (bf16[8,16,384]{2,1,0:T(8,128)(2,1)S(1)}, bf16[8,16,384]{2,1,0:T(8,128)(2,1)S(1)}, u32[]{:S(2)}, u32[]{:S(2)}) collective-permute-start(bf16[8,16,384]{2,1,0:T(8,128)(2,1)S(1)} %fold.1.own_ref), channel_id=1, source_target_pairs={{8,0},{16,8},{24,16},{32,24},{40,32},{48,40},{56,48},{64,56},{72,6... | collective-permute-start | bytes 294920 | tf_op jit(solution)/shard_map/ppermute | solution.py:365
  10.6 15.3 %copy-start.2 = (s32[16]{0:T(128)S(1)}, s32[16]{0:T(128)}, u32[]{:S(2)}) copy-start(s32[16]{0:T(128)} %param.9) | copy-start | bytes 196
  10.6 15.4 %copy-start.1 = (f32[16,16,192]{2,1,0:T(8,128)S(1)}, f32[16,16,192]{2,1,0:T(8,128)}, u32[]{:S(2)}) copy-start(f32[16,16,192]{2,1,0:T(8,128)} %x_ref.3) | copy-start | bytes 589828
  16.1 13.9 %collective-permute-start.2 = (bf16[8,16,384]{2,1,0:T(8,128)(2,1)S(1)}, bf16[8,16,384]{2,1,0:T(8,128)(2,1)S(1)}, u32[]{:S(2)}, u32[]{:S(2)}) collective-permute-start(bf16[8,16,384]{2,1,0:T(8,128)(2,1)S(1)} %couple.3.near_ref), channel_id=1, source_target_pairs={{0,2},{1,7},{2,0},{3,5},{4,6},{5,3},{6,4},{7,1},{8,10},{9,15},{10,... | collective-permute-start | bytes 294920 | tf_op jit(solution)/shard_map/ppermute | solution.py:374
  30.0 9.3 %collective-permute-start.3 = (bf16[8,16,384]{2,1,0:T(8,128)(2,1)S(1)}, bf16[8,16,384]{2,1,0:T(8,128)(2,1)S(1)}, u32[]{:S(2)}, u32[]{:S(2)}) collective-permute-start(bf16[8,16,384]{2,1,0:T(8,128)(2,1)S(1)} %pair.3.near_ref), channel_id=1, source_target_pairs={{0,6},{1,3},{2,4},{3,1},{4,2},{5,7},{6,0},{7,5},{8,14},{9,11},{10,... | collective-permute-start | bytes 294920 | tf_op jit(solution)/shard_map/ppermute | solution.py:374
  39.3 5.9 %collective-permute-start.4 = (bf16[9,16,384]{2,1,0:T(8,128)(2,1)S(1)}, bf16[9,16,384]{2,1,0:T(8,128)(2,1)S(1)}, u32[]{:S(2)}, u32[]{:S(2)}) collective-permute-start(bf16[9,16,384]{2,1,0:T(8,128)(2,1)S(1)} %get-tuple-element.15.own_ref), channel_id=1, source_target_pairs={{0,8},{8,16},{16,24},{24,32},{32,40},{40,48},{48,56},{56,64},{64,7... | collective-permute-start | bytes 331784 | tf_op jit(solution)/shard_map/ppermute | solution.py:365
  43.2 9.7 %collective-permute-start.5 = (bf16[9,16,384]{2,1,0:T(8,128)(2,1)S(1)}, bf16[9,16,384]{2,1,0:T(8,128)(2,1)S(1)}, u32[]{:S(2)}, u32[]{:S(2)}) collective-permute-start(bf16[9,16,384]{2,1,0:T(8,128)(2,1)S(1)} %get-tuple-element.15.own_ref), channel_id=1, source_target_pairs={{8,0},{16,8},{24,16},{32,24},{40,32},{48,40},{56,48},{64,56},{72,6... | collective-permute-start | bytes 331784 | tf_op jit(solution)/shard_map/ppermute | solution.py:365
  54.6 11.4 %collective-permute-start.6 = (bf16[8,16,384]{2,1,0:T(8,128)(2,1)S(1)}, bf16[8,16,384]{2,1,0:T(8,128)(2,1)S(1)}, u32[]{:S(2)}, u32[]{:S(2)}) collective-permute-start(bf16[8,16,384]{2,1,0:T(8,128)(2,1)S(1)} %couple.4.near_ref), channel_id=1, source_target_pairs={{0,2},{1,7},{2,0},{3,5},{4,6},{5,3},{6,4},{7,1},{8,10},{9,15},{10,... | collective-permute-start | bytes 294920 | tf_op jit(solution)/shard_map/ppermute | solution.py:374
  66.0 9.3 %collective-permute-start.7 = (bf16[8,16,384]{2,1,0:T(8,128)(2,1)S(1)}, bf16[8,16,384]{2,1,0:T(8,128)(2,1)S(1)}, u32[]{:S(2)}, u32[]{:S(2)}) collective-permute-start(bf16[8,16,384]{2,1,0:T(8,128)(2,1)S(1)} %pair.4.near_ref), channel_id=1, source_target_pairs={{0,6},{1,3},{2,4},{3,1},{4,2},{5,7},{6,0},{7,5},{8,14},{9,11},{10,... | collective-permute-start | bytes 294920 | tf_op jit(solution)/shard_map/ppermute | solution.py:374
  75.4 5.4 %collective-permute-start.8 = (bf16[8,16,384]{2,1,0:T(8,128)(2,1)S(1)}, bf16[8,16,384]{2,1,0:T(8,128)(2,1)S(1)}, u32[]{:S(2)}, u32[]{:S(2)}) collective-permute-start(bf16[8,16,384]{2,1,0:T(8,128)(2,1)S(1)} %get-tuple-element.17.own_ref), channel_id=1, source_target_pairs={{0,8},{8,16},{16,24},{24,32},{32,40},{40,48},{48,56},{56,64},{64,7... | collective-permute-start | bytes 294920 | tf_op jit(solution)/shard_map/ppermute | solution.py:365
  77.3 9.6 %collective-permute-start.9 = (bf16[8,16,384]{2,1,0:T(8,128)(2,1)S(1)}, bf16[8,16,384]{2,1,0:T(8,128)(2,1)S(1)}, u32[]{:S(2)}, u32[]{:S(2)}) collective-permute-start(bf16[8,16,384]{2,1,0:T(8,128)(2,1)S(1)} %get-tuple-element.17.own_ref), channel_id=1, source_target_pairs={{8,0},{16,8},{24,16},{32,24},{40,32},{48,40},{56,48},{64,56},{72,6... | collective-permute-start | bytes 294920 | tf_op jit(solution)/shard_map/ppermute | solution.py:365
  88.6 10.7 %collective-permute-start.10 = (bf16[9,16,384]{2,1,0:T(8,128)(2,1)S(1)}, bf16[9,16,384]{2,1,0:T(8,128)(2,1)S(1)}, u32[]{:S(2)}, u32[]{:S(2)}) collective-permute-start(bf16[9,16,384]{2,1,0:T(8,128)(2,1)S(1)} %couple.5.near_ref), channel_id=1, source_target_pairs={{0,2},{1,7},{2,0},{3,5},{4,6},{5,3},{6,4},{7,1},{8,10},{9,15},{10,... | collective-permute-start | bytes 331784 | tf_op jit(solution)/shard_map/ppermute | solution.py:374
  99.3 11.7 %collective-permute-start.11 = (bf16[8,16,384]{2,1,0:T(8,128)(2,1)S(1)}, bf16[8,16,384]{2,1,0:T(8,128)(2,1)S(1)}, u32[]{:S(2)}, u32[]{:S(2)}) collective-permute-start(bf16[8,16,384]{2,1,0:T(8,128)(2,1)S(1)} %pair.5.near_ref), channel_id=1, source_target_pairs={{0,6},{1,3},{2,4},{3,1},{4,2},{5,7},{6,0},{7,5},{8,14},{9,11},{10,... | collective-permute-start | bytes 294920 | tf_op jit(solution)/shard_map/ppermute | solution.py:374
  130.4 14.7 %collective-permute-start.12 = (bf16[8,2,16,384]{3,2,1,0:T(8,128)(2,1)S(1)}, bf16[8,2,16,384]{3,2,1,0:T(8,128)(2,1)S(1)}, u32[]{:S(2)}, u32[]{:S(2)}) collective-permute-start(bf16[8,2,16,384]{3,2,1,0:T(8,128)(2,1)S(1)} %fit.1.near_ref), channel_id=1, source_target_pairs={{0,2},{1,7},{2,0},{3,5},{4,6},{5,3},{6,4},{7,1},{8,10},{9,15},{10,... | collective-permute-start | bytes 589832 | tf_op jit(solution)/shard_map/ppermute | solution.py:374
  146.2 20.5 %collective-permute-start.13 = (bf16[8,4,16,384]{3,2,1,0:T(8,128)(2,1)S(1)}, bf16[8,4,16,384]{3,2,1,0:T(8,128)(2,1)S(1)}, u32[]{:S(2)}, u32[]{:S(2)}) collective-permute-start(bf16[8,4,16,384]{3,2,1,0:T(8,128)(2,1)S(1)} %slots.1.near_ref), channel_id=1, source_target_pairs={{0,6},{1,3},{2,4},{3,1},{4,2},{5,7},{6,0},{7,5},{8,14},{9,11},{10,... | collective-permute-start | bytes 1179656 | tf_op jit(solution)/shard_map/ppermute | solution.py:374
  166.9 13.1 %collective-permute-start.14 = (bf16[8,4,16,384]{3,2,1,0:T(8,128)(2,1)S(1)}, bf16[8,4,16,384]{3,2,1,0:T(8,128)(2,1)S(1)}, u32[]{:S(2)}, u32[]{:S(2)}) collective-permute-start(bf16[8,4,16,384]{3,2,1,0:T(8,128)(2,1)S(1)} %finish.1.prolong_ref.own_ref), channel_id=1, source_target_pairs={{0,8},{8,16},{16,24},{24,32},{32,40},{40,48},{48,56},{56,64},{64,7... | collective-permute-start | bytes 1179656 | tf_op jit(solution)/shard_map/ppermute | solution.py:365
  168.8 12.7 %collective-permute-start.15 = (bf16[8,4,16,384]{3,2,1,0:T(8,128)(2,1)S(1)}, bf16[8,4,16,384]{3,2,1,0:T(8,128)(2,1)S(1)}, u32[]{:S(2)}, u32[]{:S(2)}) collective-permute-start(bf16[8,4,16,384]{3,2,1,0:T(8,128)(2,1)S(1)} %finish.1.prolong_ref.own_ref), channel_id=1, source_target_pairs={{8,0},{16,8},{24,16},{32,24},{40,32},{48,40},{56,48},{64,56},{72,6... | collective-permute-start | bytes 1179656 | tf_op jit(solution)/shard_map/ppermute | solution.py:365
  172.2 9.4 %collective-permute-start.16 = (bf16[8,4,16,384]{3,2,1,0:T(8,128)(2,1)S(1)}, bf16[8,4,16,384]{3,2,1,0:T(8,128)(2,1)S(1)}, u32[]{:S(2)}, u32[]{:S(2)}) collective-permute-start(bf16[8,4,16,384]{3,2,1,0:T(8,128)(2,1)S(1)} %finish.1.prolong_ref.own_ref), channel_id=1, source_target_pairs={{0,1},{1,0},{2,3},{3,2},{4,5},{5,4},{6,7},{7,6},{8,9},{9,8},{10,11... | collective-permute-start | bytes 1179656 | tf_op jit(solution)/shard_map/ppermute | solution.py:551
  186.8 9.3 %collective-permute-start.17 = (bf16[2,96,256]{2,1,0:T(8,128)(2,1)S(1)}, bf16[2,96,256]{2,1,0:T(8,128)(2,1)S(1)}, u32[]{:S(2)}, u32[]{:S(2)}) collective-permute-start(bf16[2,96,256]{2,1,0:T(8,128)(2,1)S(1)} %get-tuple-element.19), channel_id=1, source_target_pairs={{0,2},{1,7},{2,0},{3,5},{4,6},{5,3},{6,4},{7,1},{8,10},{9,15},{10,... | collective-permute-start | bytes 294920 | tf_op jit(solution)/shard_map/ppermute | solution.py:374
  196.1 8.7 %collective-permute-start.18 = (bf16[96,256]{1,0:T(8,128)(2,1)S(1)}, bf16[96,256]{1,0:T(8,128)(2,1)S(1)}, u32[]{:S(2)}, u32[]{:S(2)}) collective-permute-start(bf16[96,256]{1,0:T(8,128)(2,1)S(1)} %fusion.6), channel_id=1, source_target_pairs={{0,6},{1,3},{2,4},{3,1},{4,2},{5,7},{6,0},{7,5},{8,14},{9,11},{10,... | collective-permute-start | bytes 147464 | tf_op jit(solution)/shard_map/ppermute | solution.py:374
  204.9 12.8 %collective-permute-start.19 = (f32[96,128]{1,0:T(8,128)S(1)}, f32[96,128]{1,0:T(8,128)S(1)}, u32[]{:S(2)}, u32[]{:S(2)}) collective-permute-start(f32[96,128]{1,0:T(8,128)S(1)} %slice.50), channel_id=1, source_target_pairs={{0,1},{1,0},{2,3},{3,2},{4,5},{5,4},{6,7},{7,6},{8,9},{9,8},{10,11... | collective-permute-start | bytes 147464 | tf_op jit(solution)/shard_map/ppermute | solution.py:581
